TPU v7x, 32 devices: a whole 2x2x4 slice. The times are simulated.
32 devices in a mesh: section: 2 (over core), tensor: 4 (over y, x), seq: 4 (over z).
Axes of the slice: x: 2, y: 2, z: 4, core: 2. Of those that a mesh axis runs over, the one named last changes fastest.
Arguments:
- byte_ids: int32 [2, 2048], P(None, 'seq'), may hold values from 0 to 255
- byte_lengths: int32 [2], replicated, may hold values from 1024 to 2048, as said below
- embedding: bfloat16 [256, 768], replicated, may hold values from -6 to 6
- conv_weight: bfloat16 [5, 768], replicated, may hold values from -2.5 to 2.5
- conv_bias: bfloat16 [768], replicated, may hold values from -2.5 to 2.5
- score_weight: bfloat16 [768], replicated, may hold values from -0.4375 to 0.4375
- norm_first: bfloat16 [768], replicated, may hold values from 0.5 to 1.5
- query_weight: bfloat16 [768, 768], P(None, 'tensor'), may hold values from -0.109375 to 0.109375
- key_weight: bfloat16 [768, 768], P(None, 'tensor'), may hold values from -0.109375 to 0.109375
- value_weight: bfloat16 [768, 768], P(None, 'tensor'), may hold values from -0.21875 to 0.21875
- out_weight: bfloat16 [768, 768], P('tensor'), may hold values from -0.875 to 0.875
- rel_bias: bfloat16 [32, 12], P(None, 'tensor'), may hold values from -4 to 4
- norm_second: bfloat16 [768], replicated, may hold values from 0.5 to 1.5
- gate_weight: bfloat16 [768, 2048], P(None, 'tensor'), may hold values from -0.21875 to 0.21875
- up_weight: bfloat16 [768, 2048], P(None, 'tensor'), may hold values from -0.21875 to 0.21875
- down_weight: bfloat16 [2048, 768], P('tensor'), may hold values from -0.1875 to 0.1875
- out_grad: bfloat16 [2, 1024, 768], P(None, 'seq'), may hold values from -6 to 6
Outputs:
- encoded: bfloat16 [2, 1024, 768], P('section', 'seq')
- grad_embedding: float32 [256, 768], replicated
- grad_conv_weight: float32 [5, 768], replicated
- grad_conv_bias: float32 [768], replicated
- grad_score_weight: float32 [768], replicated
- grad_norm_first: float32 [768], replicated
- grad_query_weight: float32 [768, 768], P(None, 'tensor')
- grad_key_weight: float32 [768, 768], P(None, 'tensor')
- grad_value_weight: float32 [768, 768], P(None, 'tensor')
- grad_out_weight: float32 [768, 768], P('tensor')
- grad_rel_bias: float32 [32, 12], P(None, 'tensor')
- grad_norm_second: float32 [768], replicated
- grad_gate_weight: float32 [768, 2048], P(None, 'tensor')
- grad_up_weight: float32 [768, 2048], P(None, 'tensor')
- grad_down_weight: float32 [2048, 768], P('tensor')
Inputs may be any that keep to these rules, and one draw needn't show every extreme that they name: `byte_lengths`: one micro-batch's sequence, drawn from the seed, has all 2048 bytes in use; the others use at least half.
All inputs are finite; a program needn't handle non-finite values.
Results may differ from a plain program's by a relative error of at most 0.022.
Values may be sent and summed in bfloat16 or wider, within the bound.
No kernel may reach another device: no remote copies, remote signals or barrier semaphores. Data moves between devices by JAX's collectives and lax.ppermute only.
A program may use at most 192 MiB of HBM per device.

v0:
```python
import jax
import jax.numpy as jnp
from jax import lax
from jax.sharding import PartitionSpec as P

epsilon = 1e-06
masked_score = -1e30
highest = lax.Precision.HIGHEST
far_thresholds = (12, 16, 23, 32, 46, 64, 91)


def padded(shard, sides, width):
    for axis, dim in sides:
        size, length = (lax.axis_size(axis), shard.shape[dim])
        up = [(i, (i + 1) % size) for i in range(size - 1)]
        down = [(j, i) for i, j in up]
        last = lax.slice_in_dim(shard, length - width, length, axis=dim)
        first = lax.slice_in_dim(shard, 0, width, axis=dim)
        before = lax.ppermute(last, axis, up)
        after = lax.ppermute(first, axis, down)
        shard = jnp.concatenate([before, shard, after], axis=dim)
    return shard


def passed_along(value, axis, steps):
    count = lax.axis_size(axis)
    first, last = (max(0, -steps), min(count, count - steps))
    return lax.ppermute(value, axis, [(source, source + steps) for source in range(first, last)])


def bucket_of(relative):
    distance = jnp.abs(relative)
    far_bucket = 8 + sum(
        ((distance >= threshold).astype(jnp.int32) for threshold in far_thresholds)
    )
    return jnp.where(distance < 8, distance, far_bucket) + 16 * (relative > 0).astype(jnp.int32)


def position_bias(bias_table, query_first, query_count, key_first, key_count, seq_tokens):
    offsets = jnp.arange(2 * seq_tokens - 1, dtype=jnp.int32) - (seq_tokens - 1)
    bucket_ids = jnp.arange(bias_table.shape[0], dtype=jnp.int32)
    onehot = (bucket_of(offsets)[:, None] == bucket_ids[None, :]).astype(jnp.float32)
    by_distance = jnp.dot(onehot, bias_table, precision=highest).T
    starts = key_first - query_first - jnp.arange(query_count, dtype=jnp.int32) + seq_tokens - 1

    def one_row(begin):
        return lax.dynamic_slice_in_dim(by_distance, begin, key_count, 1)

    return jax.vmap(one_row, out_axes=1)(starts)


def on_section(active, work, *operands):

    def skipped(*values):
        return jax.tree.map(jnp.zeros_like, work(*values))

    return lax.cond(active, work, skipped, *operands)


def gbst_local(weights, ids_ext, length, base, total_bytes):
    embedding, conv_weight, conv_bias, score_weight = weights
    count = ids_ext.shape[0] - 10
    positions = base - 5 + jnp.arange(count + 10, dtype=jnp.int32)
    present = ((positions >= 0) & (positions < length)).astype(jnp.float32)
    byte_values = jnp.arange(embedding.shape[0], dtype=jnp.int32)
    onehot = (ids_ext[:, None] == byte_values[None, :]).astype(jnp.float32) * present[:, None]
    embedded = jnp.dot(onehot, embedding, precision=highest)
    conv = conv_bias + sum(
        (conv_weight[tap] * embedded[tap : tap + count + 6] for tap in range(conv_weight.shape[0]))
    )
    conv_positions = positions[2 : count + 8]
    inside = ((conv_positions >= 0) & (conv_positions < total_bytes)).astype(jnp.float32)
    conv = conv * inside[:, None]
    own_positions = base + jnp.arange(count, dtype=jnp.int32)
    pooled = []
    for size in range(1, 5):
        phase = own_positions % size
        pool_total = jnp.zeros((count, conv.shape[1]), jnp.float32)
        for offset in range(size):
            window = sum((conv[3 - offset + tap : 3 - offset + tap + count] for tap in range(size)))
            pool_total = pool_total + jnp.where((phase == offset)[:, None], window, 0.0)
        pooled.append(pool_total / size)
    stacked = jnp.stack(pooled)
    scores = jnp.einsum("bnd,d->bn", stacked, score_weight, precision=highest)
    size_weights = jax.nn.softmax(scores, axis=0)
    mixed = jnp.sum(size_weights[:, :, None] * stacked, axis=0)
    return mixed.reshape(count // 2, 2, -1).mean(axis=1)


def shards(
    byte_ids,
    byte_lengths,
    embedding,
    conv_weight,
    conv_bias,
    score_weight,
    norm_first,
    query_weight,
    key_weight,
    value_weight,
    out_weight,
    rel_bias,
    norm_second,
    gate_weight,
    up_weight,
    down_weight,
    out_grad,
):
    micro_count, group = byte_ids.shape
    seq_index = lax.axis_index("seq")
    seq_devices = lax.axis_size("seq")
    total_bytes = group * seq_devices
    local_tokens = group // 2
    seq_tokens = local_tokens * seq_devices
    token_first = seq_index * local_tokens
    first_section = lax.axis_index("section") == 0
    second_section = jnp.logical_not(first_section)
    heads_local = rel_bias.shape[1]
    head_dim = query_weight.shape[1] // heads_local
    gain_first = norm_first.astype(jnp.float32)
    gain_second = norm_second.astype(jnp.float32)
    bias_table = rel_bias.astype(jnp.float32)
    gbst_weights = tuple(
        (item.astype(jnp.float32) for item in (embedding, conv_weight, conv_bias, score_weight))
    )
    ids_ext = padded(byte_ids, (("seq", 1),), 5)
    piece_first = 0

    def gbst_run(weights, micro):
        piece_ids = ids_ext[micro]
        return gbst_local(
            weights, piece_ids, byte_lengths[micro], seq_index * group + piece_first, total_bytes
        )

    def gbst_backward(micro, grad_tokens):
        grad_piece = grad_tokens.astype(jnp.float32)

        def work(weights, grad_rows):
            pullback = jax.vjp(lambda values: gbst_run(values, micro), weights)[1]
            return pullback(grad_rows)[0]

        return on_section(first_section, work, gbst_weights, grad_piece)

    def all_bias(table_values):
        return position_bias(table_values, token_first, local_tokens, 0, seq_tokens, seq_tokens)

    def t5_micro(hidden_rows, length, grad_rows):
        key_live = 2 * jnp.arange(seq_tokens, dtype=jnp.int32) < length

        def front(hidden_bf):
            hidden = hidden_bf.astype(jnp.float32)
            scale = lax.rsqrt(jnp.mean(hidden * hidden, axis=-1, keepdims=True) + epsilon)
            normed = (hidden * scale * gain_first).astype(jnp.bfloat16)
            projected = [
                jnp.dot(normed, weight_item, preferred_element_type=jnp.float32).astype(
                    jnp.bfloat16
                )
                for weight_item in (query_weight, key_weight, value_weight)
            ]
            return (hidden, scale, normed, projected[0], projected[1], projected[2])

        hidden, scale_first, normed_first, queries, keys, values = on_section(
            second_section, front, hidden_rows
        )
        all_keys, all_values = (
            lax.all_gather(keys, "seq", axis=0, tiled=True),
            lax.all_gather(values, "seq", axis=0, tiled=True),
        )
        query_heads = queries.reshape(local_tokens, heads_local, head_dim)
        key_heads = all_keys.reshape(seq_tokens, heads_local, head_dim)
        value_heads = all_values.reshape(seq_tokens, heads_local, head_dim)

        def attend(query_heads, key_heads, value_heads):
            scores = jnp.einsum(
                "qhd,khd->hqk", query_heads, key_heads, preferred_element_type=jnp.float32
            ) + all_bias(bias_table)
            scores = jnp.where(key_live[None, None, :], scores, masked_score)
            log_total = jax.nn.logsumexp(scores, axis=-1)
            probs = jnp.exp(scores - log_total[:, :, None])
            mixed = jnp.einsum(
                "hqk,khd->qhd",
                probs.astype(jnp.bfloat16),
                value_heads,
                preferred_element_type=jnp.float32,
            )
            attended = mixed.reshape(local_tokens, -1).astype(jnp.bfloat16)
            return (
                log_total,
                probs,
                attended,
                jnp.dot(attended, out_weight, preferred_element_type=jnp.float32),
            )

        log_total, probs, attended, branch_part = on_section(
            second_section, attend, query_heads, key_heads, value_heads
        )
        branch = lax.psum(branch_part, "tensor")

        def feed(hidden, branch):
            middle = hidden + branch
            scale = lax.rsqrt(jnp.mean(middle * middle, axis=-1, keepdims=True) + epsilon)
            normed = (middle * scale * gain_second).astype(jnp.bfloat16)
            gate = jnp.dot(normed, gate_weight, preferred_element_type=jnp.float32)
            upward = jnp.dot(normed, up_weight, preferred_element_type=jnp.float32)
            inner = (jax.nn.gelu(gate, approximate=True) * upward).astype(jnp.bfloat16)
            return (
                middle,
                scale,
                normed,
                gate,
                upward,
                inner,
                jnp.dot(inner, down_weight, preferred_element_type=jnp.float32),
            )

        middle, scale_second, normed_second, gate, upward, inner, feed_part = on_section(
            second_section, feed, hidden, branch
        )
        output = middle + lax.psum(feed_part.astype(jnp.bfloat16), "tensor").astype(jnp.float32)

        def feed_back(grad_rows):
            grad_down = jnp.einsum(
                "tf,td->fd", inner, grad_rows, preferred_element_type=jnp.float32
            )
            grad_inner = jnp.dot(grad_rows, down_weight.T, preferred_element_type=jnp.float32)
            activated, gelu_back = jax.vjp(lambda value: jax.nn.gelu(value, approximate=True), gate)
            grad_gate = gelu_back(grad_inner * upward)[0].astype(jnp.bfloat16)
            grad_upward = (grad_inner * activated).astype(jnp.bfloat16)
            grad_gate_weight = jnp.einsum(
                "td,tf->df", normed_second, grad_gate, preferred_element_type=jnp.float32
            )
            grad_up_weight = jnp.einsum(
                "td,tf->df", normed_second, grad_upward, preferred_element_type=jnp.float32
            )
            grad_normed = jnp.dot(
                grad_gate, gate_weight.T, preferred_element_type=jnp.float32
            ) + jnp.dot(grad_upward, up_weight.T, preferred_element_type=jnp.float32)
            return (grad_down, grad_gate_weight, grad_up_weight, grad_normed)

        grad_down, grad_gate_weight, grad_up_weight, normed_part = on_section(
            second_section, feed_back, grad_rows
        )
        grad_normed_second = lax.psum(normed_part, "tensor")

        def attend_back(grad_normed):
            grad_gain_second = jnp.sum(grad_normed * middle * scale_second, axis=0)
            through = grad_normed * gain_second
            cubed = scale_second * scale_second * scale_second
            grad_middle = (
                grad_rows.astype(jnp.float32)
                + scale_second * through
                - middle * cubed * jnp.mean(through * middle, axis=-1, keepdims=True)
            )
            grad_branch = grad_middle.astype(jnp.bfloat16)
            grad_out_weight = jnp.einsum(
                "th,td->hd", attended, grad_branch, preferred_element_type=jnp.float32
            )
            grad_attended = jnp.dot(
                grad_branch, out_weight.T, preferred_element_type=jnp.float32
            ).astype(jnp.bfloat16)
            grad_heads = grad_attended.reshape(local_tokens, heads_local, head_dim)
            grad_probs = jnp.einsum(
                "qhd,khd->hqk", grad_heads, value_heads, preferred_element_type=jnp.float32
            )
            row_total = jnp.sum(probs * grad_probs, axis=-1)
            grad_scores = (probs * (grad_probs - row_total[:, :, None])).astype(jnp.bfloat16)
            grad_queries = jnp.einsum(
                "hqk,khd->qhd", grad_scores, key_heads, preferred_element_type=jnp.float32
            )
            grad_queries = grad_queries.reshape(local_tokens, -1).astype(jnp.bfloat16)
            grad_table = jax.vjp(all_bias, bias_table)[1](grad_scores.astype(jnp.float32))[0]
            return (
                grad_gain_second,
                grad_middle,
                grad_out_weight,
                grad_attended,
                row_total,
                grad_scores,
                grad_queries,
                grad_table,
            )

        (
            grad_gain_second,
            grad_middle,
            grad_out_weight,
            grad_attended,
            row_total,
            grad_scores,
            grad_queries,
            grad_table,
        ) = on_section(second_section, attend_back, grad_normed_second)
        grad_heads = grad_attended.reshape(local_tokens, heads_local, head_dim)
        width_local = keys.shape[1]

        def term_work(grad_scores, probs):
            prob_rows = probs.astype(jnp.bfloat16)
            grad_keys = jnp.einsum(
                "hqk,qhd->khd", grad_scores, query_heads, preferred_element_type=jnp.float32
            )
            grad_values = jnp.einsum(
                "hqk,qhd->khd", prob_rows, grad_heads, preferred_element_type=jnp.float32
            )
            return jnp.concatenate(
                [
                    grad_keys.reshape(local_tokens * lax.axis_size("seq"), -1),
                    grad_values.reshape(local_tokens * lax.axis_size("seq"), -1),
                ],
                axis=1,
            )

        summed = lax.psum_scatter(
            on_section(second_section, term_work, grad_scores, probs).astype(jnp.bfloat16),
            "seq",
            scatter_dimension=0,
            tiled=True,
        ).astype(jnp.float32)
        grad_keys = summed[:, :width_local]
        grad_values = summed[:, width_local:]
        grad_keys = grad_keys.astype(jnp.bfloat16)
        grad_values = grad_values.astype(jnp.bfloat16)

        def front_back(grad_queries, grad_keys, grad_values):
            weight_grads = [
                jnp.einsum("td,th->dh", normed_first, grad_item, preferred_element_type=jnp.float32)
                for grad_item in (grad_queries, grad_keys, grad_values)
            ]
            normed_grad = (
                jnp.dot(grad_queries, query_weight.T, preferred_element_type=jnp.float32)
                + jnp.dot(grad_keys, key_weight.T, preferred_element_type=jnp.float32)
                + jnp.dot(grad_values, value_weight.T, preferred_element_type=jnp.float32)
            )
            return (weight_grads[0], weight_grads[1], weight_grads[2], normed_grad)

        grad_query_weight, grad_key_weight, grad_value_weight, first_part = on_section(
            second_section, front_back, grad_queries, grad_keys, grad_values
        )
        grad_normed_first = lax.psum(first_part.astype(jnp.bfloat16), "tensor").astype(jnp.float32)
        grad_gain_first = jnp.sum(grad_normed_first * hidden * scale_first, axis=0)
        through_first = grad_normed_first * gain_first
        cubed_first = scale_first * scale_first * scale_first
        grad_hidden = (
            grad_middle
            + scale_first * through_first
            - hidden * cubed_first * jnp.mean(through_first * hidden, axis=-1, keepdims=True)
        )
        layer_grads = (
            grad_gain_first,
            grad_query_weight,
            grad_key_weight,
            grad_value_weight,
            grad_out_weight,
            grad_table,
            grad_gain_second,
            grad_gate_weight,
            grad_up_weight,
            grad_down,
        )
        return (grad_hidden.astype(jnp.bfloat16), output.astype(jnp.bfloat16), layer_grads)

    pending = None
    arriving = None
    own_encoded = None
    gbst_sums = None
    layer_sums = None
    for tick in range(micro_count + 1):
        if tick < micro_count:
            gbst_micro = tick
            tokens_part = on_section(
                first_section, lambda weights: gbst_run(weights, gbst_micro), gbst_weights
            ).astype(jnp.bfloat16)
            outgoing = tokens_part
        if tick >= 1:
            micro = tick - 1
            grad_tokens, encoded_rows, layer_grads = t5_micro(
                pending, byte_lengths[micro], out_grad[micro]
            )
            layer_sums = (
                layer_grads
                if layer_sums is None
                else jax.tree.map(jnp.add, layer_sums, layer_grads)
            )
            back_tokens, back_encoded = passed_along((grad_tokens, encoded_rows), "section", -1)
            if micro == 0:
                arriving = back_encoded
            own_encoded = encoded_rows
            block_grads = gbst_backward(micro, back_tokens)
            gbst_sums = (
                block_grads if gbst_sums is None else jax.tree.map(jnp.add, gbst_sums, block_grads)
            )
        if tick < micro_count:
            pending = passed_along(outgoing, "section", 1)
    totals = (
        lax.psum(gbst_sums[0].astype(jnp.bfloat16), ("section", "seq")).astype(jnp.float32),
        lax.psum(gbst_sums[1].astype(jnp.bfloat16), ("section", "seq")).astype(jnp.float32),
        lax.psum(gbst_sums[2].astype(jnp.bfloat16), ("section", "seq")).astype(jnp.float32),
        lax.psum(gbst_sums[3].astype(jnp.bfloat16), ("section", "seq")).astype(jnp.float32),
        lax.psum(layer_sums[0].astype(jnp.bfloat16), ("section", "seq")).astype(jnp.float32),
        lax.psum(layer_sums[1].astype(jnp.bfloat16), ("section", "seq")).astype(jnp.float32),
        lax.psum(layer_sums[2].astype(jnp.bfloat16), ("section", "seq")).astype(jnp.float32),
        lax.psum(layer_sums[3].astype(jnp.bfloat16), ("section", "seq")).astype(jnp.float32),
        lax.psum(layer_sums[4].astype(jnp.bfloat16), ("section", "seq")).astype(jnp.float32),
        lax.psum(layer_sums[5].astype(jnp.bfloat16), ("section", "seq")).astype(jnp.float32),
        lax.psum(layer_sums[6].astype(jnp.bfloat16), ("section", "seq")).astype(jnp.float32),
        lax.psum(layer_sums[7].astype(jnp.bfloat16), ("section", "seq")).astype(jnp.float32),
        lax.psum(layer_sums[8].astype(jnp.bfloat16), ("section", "seq")).astype(jnp.float32),
        lax.psum(layer_sums[9].astype(jnp.bfloat16), ("section", "seq")).astype(jnp.float32),
    )
    encoded = jnp.where(first_section, arriving, own_encoded)[None]
    return (
        encoded,
        totals[0],
        totals[1],
        totals[2],
        totals[3],
        totals[4],
        totals[5],
        totals[6],
        totals[7],
        totals[8],
        totals[9],
        totals[10],
        totals[11],
        totals[12],
        totals[13],
    )


def solution(mesh):
    return jax.shard_map(
        shards,
        mesh=mesh,
        in_specs=(
            P(None, "seq"),
            P(),
            P(),
            P(),
            P(),
            P(),
            P(),
            P(None, "tensor"),
            P(None, "tensor"),
            P(None, "tensor"),
            P("tensor", None),
            P(None, "tensor"),
            P(),
            P(None, "tensor"),
            P(None, "tensor"),
            P("tensor", None),
            P(None, "seq", None),
        ),
        out_specs=(
            P("section", "seq", None),
            P(),
            P(),
            P(),
            P(),
            P(),
            P(None, "tensor"),
            P(None, "tensor"),
            P(None, "tensor"),
            P("tensor", None),
            P(None, "tensor"),
            P(),
            P(None, "tensor"),
            P(None, "tensor"),
            P("tensor", None),
        ),
        check_vma=False,
    )
```

profile of v0, /device:TPU:0, one launch (start us, length us, event | category | flops | bytes accessed | tf_op | source)
XLA Modules:
  0.0 5623.2 jit_solution(7740806853174346435)
XLA Ops:
  8.0 4.9 collective-permute-start
  19.2 21.3 conditional.22
  28.1 5.4 fusion.141
  43.3 22.6 conditional.18
  51.1 5.4 fusion.110
  69.7 15.1 all_gather.14
  84.8 15.4 all_gather.15
  103.2 14.7 all_gather.12
  117.8 14.5 all_gather.13
  142.7 1547.6 %all-reduce.96.cloned.1.call-done = (f32[256,768]{1,0:T(8,128)}, f32[256,768]{1,0:T(8,128)}) async-done(((f32[256,768]{1,0:T(8,128)}, f32[256,768]{1,0:T(8,128)}), (f32[256,768]{1,0:T(8,128)}, f32[256,768]{1,0:T(8,128)})) %all-reduce.96.cloned.1.call-update) | async-done | bytes 1572880 | tf_op jit(solution)/shard_map/psum | solution.py:197
  1701.0 4.9 conditional.31
  1706.0 96.3 %all-reduce.94.cloned.1.call-done = (f32[256,768]{1,0:T(8,128)}, f32[256,768]{1,0:T(8,128)}) async-done(((f32[256,768]{1,0:T(8,128)}, f32[256,768]{1,0:T(8,128)}), (f32[256,768]{1,0:T(8,128)}, f32[256,768]{1,0:T(8,128)})) %all-reduce.94.cloned.1.call-update) | async-done | bytes 1572880 | tf_op jit(solution)/shard_map/psum | solution.py:243
  1810.7 5.1 conditional.32
  1822.6 1688.6 %reduce-scatter.3.cloned.1.call-done = bf16[256,384]{1,0:T(8,128)(2,1)} async-done(((bf16[1024,384]{1,0:T(8,128)(2,1)}), bf16[256,384]{1,0:T(8,128)(2,1)}) %reduce-scatter.3.cloned.1.call-update) | async-done | bytes 196624 | tf_op jit(solution)/shard_map/reduce_scatter | solution.py:312
  3514.5 1824.5 %reduce-scatter.5.cloned.1.call-done = bf16[256,384]{1,0:T(8,128)(2,1)} async-done(((bf16[1024,384]{1,0:T(8,128)(2,1)}), bf16[256,384]{1,0:T(8,128)(2,1)}) %reduce-scatter.5.cloned.1.call-update) | async-done | bytes 196624 | tf_op jit(solution)/shard_map/reduce_scatter | solution.py:312
  5353.6 54.6 all-reduce.100.cloned.1.call-done
  5421.7 40.5 conditional.30
  5435.3 5.4 fusion.199
  5449.8 7.7 multiply_reduce_fusion.17
  5462.2 45.7 conditional.35
  5475.5 5.4 fusion.252
  5491.5 12.6 multiply_reduce_fusion.24
  5512.7 31.7 all-reduce.86
  5548.9 56.5 %all-reduce.98.cloned.1.call-done = (bf16[256,768]{1,0:T(8,128)(2,1)}, bf16[768,192]{0,1:T(8,128)(2,1)}, bf16[768,192]{0,1:T(8,128)(2,1)}, bf16[768,192]{0,1:T(8...) async-done(((bf16[256,768]{1,0:T(8,128)(2,1)}, bf16[768,192]{0,1:T(8,128)(2,1)}, ...) | async-done | bytes 3932176 | tf_op jit(solution)/shard_map/psum | solution.py:394
  (374 shorter events, 232.0 us)
Async XLA Ops:
  7.2 1683.2 %all-reduce.96.cloned.1.call-start = ((), (), s32[]{:S(2)}) async-start(), calls=%async_computation.5 | async-start | bytes 3145728 | tf_op jit(solution)/shard_map/psum | solution.py:197
  8.0 9.4 collective-permute-start
  12.9 5.5 collective-permute-start.1
  40.4 26.9 collective-permute-start.4
  65.9 34.2 collective-permute-start.2
  67.3 65.1 %copy-start.71 = (s32[1024]{0:T(1024)}, s32[1024]{0:T(1024)S(1)}, u32[]{:S(2)}) copy-start(s32[1024]{0:T(1024)S(1)} %iota_multiply_fusion.2) | copy-start | bytes 12292
  69.7 30.5 copy-start.88
  69.7 66.2 %copy-start.56 = (bf16[256,3,64]{0,2,1:T(8,128)(2,1)}, bf16[256,3,64]{0,2,1:T(8,128)(2,1)S(1)}, u32[]{:S(2)}) copy-start(bf16[256,3,64]{0,2,1:T(8,128)(2,1)S(1)} %get-tuple-element.501) | copy-start | bytes 294916
  84.8 51.2 copy-start.29
  100.2 35.8 copy-start.25
  100.2 32.2 copy-start.22
  103.2 29.2 copy-start.90
  140.5 1549.9 %copy-start.6 = (bf16[768,512]{1,0:T(8,128)(2,1)S(1)}, bf16[768,512]{1,0:T(8,128)(2,1)}, u32[]{:S(2)}) copy-start(bf16[768,512]{1,0:T(8,128)(2,1)} %param.66) | copy-start | bytes 2359300
  140.5 1549.9 %copy-start.37 = (bf16[512,768]{1,0:T(8,128)(2,1)S(1)}, bf16[512,768]{1,0:T(8,128)(2,1)}, u32[]{:S(2)}) copy-start(bf16[512,768]{1,0:T(8,128)(2,1)} %param.68) | copy-start | bytes 2359300
  140.5 1661.8 %all-reduce.94.cloned.1.call-start = ((), (), s32[]{:S(2)}) async-start(), calls=%async_computation.4 | async-start | bytes 3145728 | tf_op jit(solution)/shard_map/psum | solution.py:243
  1705.9 1805.2 %reduce-scatter.3.cloned.1.call-start = ((), (), s32[]{:S(2)}) async-start(), calls=%async_computation.2 | async-start | bytes 983040 | tf_op jit(solution)/shard_map/reduce_scatter | solution.py:312
  1810.4 3528.6 %reduce-scatter.5.cloned.1.call-start = ((), (), s32[]{:S(2)}) async-start(), calls=%async_computation.3 | async-start | bytes 983040 | tf_op jit(solution)/shard_map/reduce_scatter | solution.py:312
  1819.7 1691.5 %copy-start.15 = (bf16[768,192]{0,1:T(8,128)(2,1)S(1)}, bf16[768,192]{0,1:T(8,128)(2,1)}, u32[]{:S(2)}) copy-start(bf16[768,192]{0,1:T(8,128)(2,1)} %param.61) | copy-start | bytes 884740
  1819.7 3588.5 %all-reduce.100.cloned.1.call-start = ((), (), s32[]{:S(2)}) async-start(), calls=%async_computation.7 | async-start | bytes 3145728 | tf_op jit(solution)/shard_map/psum | solution.py:219
  5342.4 263.0 %all-reduce.98.cloned.1.call-start = ((), (), s32[]{:S(2)}) async-start(), calls=%async_computation.6 | async-start | bytes 7864320 | tf_op jit(solution)/shard_map/psum | solution.py:394
  5413.6 7.1 collective-permute-start.5
  5414.9 6.8 collective-permute-start.6
  5509.9 38.1 copy-start.62
  5511.4 36.7 collective-permute-start.3
  (39 other events, 249.1 us)
Sparse Core Ops, SparseCore 0:
  140.6 1549.6 all-reduce.95
  1706.1 96.2 all-reduce.93
  1810.6 1700.5 reduce-scatter.2
  3513.3 1825.6 reduce-scatter.4
  5342.7 65.4 all-reduce.99
  5510.0 95.3 all-reduce.97
where the time goes:
time: 5700 us; the launch traced here: 5620 us
  waiting for transfers between devices  5270 us (92%)
  other arithmetic  116 us (2%)
  blocking collectives  91.4 us (2%)
  local copies, waits for them, and re-layouts  74.7 us (1%)
    reduce_scatter x2, waiting for transfers between devices, t5_micro(): lax.psum_scatter(on_section(second_section, term_work, grad_scores, probs...  3510 us
    psum x1, waiting for transfers between devices, t5_micro(): branch = lax.psum(branch_part, 'tensor')  1550 us
  transfers between devices with their start and end apart: 13, of which 7 were waited for; matrix products, arithmetic and copies ran while one was open for 1% of the time, Pallas kernels for 0%

commit v1 on v0

v1 whole, which is shorter than its diff:
```python
import functools

import jax
import jax.numpy as jnp
import numpy as np
from jax import lax
from jax.experimental import pallas as pl
from jax.experimental.pallas import tpu as pltpu
from jax.sharding import PartitionSpec as P

epsilon = 1e-06
masked_score = -1e30
far_thresholds = (12, 16, 23, 32, 46, 64, 91)
period = 12
pairs = period // 2
taps = 5
columns = period + taps - 1
chunk_rows = 176
vmem_limit = 56 * 2**20
f32 = jnp.float32
bf16 = jnp.bfloat16
whole = pl.BlockSpec(memory_space=pltpu.VMEM)
scalars = pl.BlockSpec(memory_space=pltpu.SMEM)


def pool_tables():
    pool = np.zeros((3, 128, 128), np.float32)
    spread = np.zeros((4, 128, 128), np.float32)
    total = np.zeros((128, 128), np.float32)
    for size in range(1, 5):
        for g in range(period):
            for r in range(period):
                if r // size == g // size:
                    if size > 1:
                        pool[size - 2, 4 + r, 4 + g] = 1.0 / size
                    spread[size - 1, 4 + g, period * (g // 2) + r] = 0.5 / size
    for j in range(pairs):
        total[period * j : period * (j + 1), j] = 1.0
    return (pool, spread, total)


def reached(j):
    found = set()
    for g in (2 * j, 2 * j + 1):
        for size in range(1, 5):
            first = size * (g // size)
            found.update(range(first, first + size))
    return sorted(found)


def exact(a, b, dims=((1,), (0,))):
    return lax.dot_general(
        a, b, (dims, ((), ())), precision=lax.Precision.HIGHEST, preferred_element_type=f32
    )


def mm(a, b, dims=((1,), (0,))):
    return lax.dot_general(a, b, (dims, ((), ())), preferred_element_type=f32)


rows_rows = ((0,), (0,))
cols_cols = ((1,), (1,))


def call(kernel, out, *args, specs=None, scratch=(), grid=None, out_specs=None, limit=vmem_limit):
    extra = {} if grid is None else {"grid": grid}
    return pl.pallas_call(
        kernel,
        out_shape=out,
        in_specs=[whole] * len(args) if specs is None else specs,
        out_specs=jax.tree.map(lambda _: whole, out) if out_specs is None else out_specs,
        scratch_shapes=list(scratch),
        compiler_params=pltpu.CompilerParams(vmem_limit_bytes=limit),
        **extra,
    )(*args)


def like(shape, kind):
    return jax.ShapeDtypeStruct(shape, kind)


def iota(shape, dim):
    return lax.broadcasted_iota(jnp.int32, shape, dim)


def bucket_of(relative):
    distance = jnp.abs(relative)
    far_bucket = 8 + sum(
        ((distance >= threshold).astype(jnp.int32) for threshold in far_thresholds)
    )
    return jnp.where(distance < 8, distance, far_bucket) + 16 * (relative > 0).astype(jnp.int32)


def bucket_hot(buckets, width, query_first, queries):
    offsets = iota((buckets, width), 1) - (queries - 1) - query_first
    return (bucket_of(offsets) == iota((buckets, width), 0)).astype(f32)


def one_hot(ids, vocab):
    return jnp.where(ids == iota((ids.shape[0], vocab), 1), 1.0, 0.0).astype(bf16)


def head_mask(width, head_dim, head):
    return iota((1, width), 1) // head_dim == head


def prepare_kernel(embedding, conv_weight, score_weight, conv_bias, table, score_table, bias_score):
    vocab = embedding.shape[0]
    emb = embedding[...].astype(f32)
    conv = conv_weight[...].astype(f32)
    score = score_weight[...].astype(f32)
    for tap in range(taps):
        table[tap * vocab : (tap + 1) * vocab, :] = (emb * conv[tap : tap + 1]).astype(bf16)
    scored = jnp.concatenate(
        [conv[tap : tap + 1] * score for tap in reversed(range(taps))]
        + [jnp.zeros((128 - taps, conv.shape[1]), f32)],
        axis=0,
    )
    by_byte = exact(emb, scored, cols_cols)
    high = by_byte.astype(bf16).astype(f32)
    middle = (by_byte - high).astype(bf16).astype(f32)
    low = by_byte - high - middle
    score_table[...] = (high + pltpu.roll(middle, 32, 1) + pltpu.roll(low, 64, 1)).astype(bf16)
    bias_score[...] = jnp.broadcast_to(
        jnp.sum(conv_bias[...].astype(f32) * score, axis=1, keepdims=True), bias_score.shape
    )


def position_inside(rows, first, total_bytes):
    lane = iota((rows, 128), 1)
    place = period * (first + iota((rows, 128), 0)) + lane - 4
    return (lane >= 4) & (lane < 4 + period) & (place < total_bytes)


def coefficient_inside(rows, first, total_bytes):
    lane = iota((rows, 128), 1)
    place = period * (first + iota((rows, 128), 0)) + lax.rem(lane, period)
    return (lane < period * pairs) & (place < total_bytes)


def gbst_kernel(
    total_bytes,
    ids,
    table,
    score_table,
    pool,
    spread,
    total,
    conv_bias,
    bias_score,
    tokens,
    mixing,
    coefficients,
    size_weights,
    hot,
    natural,
):
    rows = ids.shape[0]
    vocab = score_table.shape[0]
    width = table.shape[1]
    first = pl.program_id(0) * rows
    scores = jnp.zeros((rows, 128), f32)
    for r in range(columns):
        found = one_hot(ids[:, r : r + 1], vocab)
        hot[:, r * vocab : (r + 1) * vocab] = found
        part = mm(found, score_table[...])
        scores = scores + (pltpu.roll(part, r, 1) if r else part)
    scores = scores + pltpu.roll(scores, 96, 1) + pltpu.roll(scores, 64, 1)
    scores = jnp.where(
        position_inside(rows, first, total_bytes), scores + bias_score[0:1, :], 0.0
    )
    by_size = [scores] + [exact(scores, pool[size]) for size in range(3)]
    largest = functools.reduce(jnp.maximum, by_size)
    weights = [jnp.exp(item - largest) for item in by_size]
    scale = 1.0 / sum(weights)
    spread_sum = jnp.zeros((rows, 128), f32)
    for size in range(4):
        weight = weights[size] * scale
        size_weights[size] = weight
        spread_sum = spread_sum + exact(weight, spread[size])
    spread_sum = jnp.where(coefficient_inside(rows, first, total_bytes), spread_sum, 0.0)
    coefficients[...] = spread_sum
    row_total = exact(spread_sum, total[...])
    narrow = spread_sum.astype(bf16)
    bias = conv_bias[...].astype(f32)
    for j in range(pairs):
        for tap in range(taps):
            acc = None
            for r in reached(j):
                at = (r + tap) * vocab
                term = hot[:, at : at + vocab] * narrow[:, period * j + r : period * j + r + 1]
                acc = term if acc is None else acc + term
            mixing[j, :, tap * vocab : (tap + 1) * vocab] = acc
        rows_j = mm(mixing[j], table[...]) + row_total[:, j : j + 1] * bias
        for at in range(width // 128):
            natural[at, pl.ds(j, rows, stride=pairs), :] = rows_j[:, at * 128 : (at + 1) * 128]
    for at in range(width // 128):
        tokens[:, at * 128 : (at + 1) * 128] = natural[at].astype(bf16)


def attend_kernel(
    heads,
    info,
    tokens,
    gain,
    query_weight,
    key_weight,
    value_weight,
    rel_bias,
    normed,
    queries,
    keys,
    values,
    probs,
    attended,
):
    seq_tokens = normed.shape[0]
    count, width = queries.shape
    head_dim = width // heads
    query_first = pl.multiple_of(info[2] * count, count)
    live_tokens = info[3]
    hidden = tokens[0:seq_tokens, :].astype(f32)
    scale = lax.rsqrt(jnp.mean(hidden * hidden, axis=-1, keepdims=True) + epsilon)
    normed[...] = (hidden * scale * gain[...].astype(f32)).astype(bf16)
    keys[...] = mm(normed[...], key_weight[...]).astype(bf16)
    values[...] = mm(normed[...], value_weight[...]).astype(bf16)
    queries[...] = mm(normed[pl.ds(query_first, count), :], query_weight[...]).astype(bf16)
    span = seq_tokens + count
    hot = bucket_hot(rel_bias.shape[0], span, query_first, count)
    by_offset = mm(rel_bias[...].astype(f32), hot, rows_rows)
    live = 2 * iota((1, seq_tokens), 1) < live_tokens
    mixed = jnp.zeros((count, width), f32)
    for head in range(heads):
        mask = head_mask(width, head_dim, head)
        row = jnp.broadcast_to(by_offset[head : head + 1, :], (count, span))
        bias = pltpu.roll(row, span - (count - 1), 1, stride=1, stride_axis=0)[:, :seq_tokens]
        own = jnp.where(mask, queries[...], jnp.zeros((), bf16))
        scores = mm(own, keys[...], cols_cols) + bias
        scores = jnp.where(live, scores, masked_score)
        raised = jnp.exp(scores - jnp.max(scores, axis=-1, keepdims=True))
        part = (raised * (1.0 / jnp.sum(raised, axis=-1, keepdims=True))).astype(bf16)
        probs[head] = part
        mixed = jnp.where(mask, mm(part, values[...]), mixed)
    attended[...] = mixed.astype(bf16)


def gelu(value):
    inner = np.float32(np.sqrt(2 / np.pi)) * (value + 0.044715 * (value * value * value))
    return 0.5 * value * (1.0 + jnp.tanh(inner))


def gelu_both(value):
    root = np.float32(np.sqrt(2 / np.pi))
    square = value * value
    tanh = jnp.tanh(root * value * (1.0 + 0.044715 * square))
    half = 0.5 * (1.0 + tanh)
    slope = half + 0.5 * value * (1.0 - tanh * tanh) * root * (1.0 + 3 * 0.044715 * square)
    return (value * half, slope)


def feed_kernel(ways, info, *refs):
    attended = refs[:ways]
    out_weight = refs[ways : 2 * ways]
    tokens, gain, gate_weight, up_weight, down_weight, out_grad = refs[2 * ways : 2 * ways + 6]
    middle, normed, inner, grad_gate, grad_up = refs[2 * ways + 6 : 2 * ways + 11]
    pieces = refs[2 * ways + 11 : 3 * ways + 11]
    whole_part = refs[3 * ways + 11]
    count = middle.shape[0]
    first = pl.multiple_of(info[2] * count, count)
    branch = sum(mm(a[...], w[...]) for a, w in zip(attended, out_weight))
    total = tokens[pl.ds(first, count), :].astype(f32) + branch
    middle[...] = total
    scale = lax.rsqrt(jnp.mean(total * total, axis=-1, keepdims=True) + epsilon)
    normed[...] = (total * scale * gain[...].astype(f32)).astype(bf16)
    gate = mm(normed[...], gate_weight[...])
    upward = mm(normed[...], up_weight[...])
    grad_inner = mm(out_grad[...], down_weight[...], cols_cols)
    active, slope = gelu_both(gate)
    inner[...] = (active * upward).astype(bf16)
    grad_gate[...] = (grad_inner * upward * slope).astype(bf16)
    grad_up[...] = (grad_inner * active).astype(bf16)
    whole_part[...] = mm(grad_gate[...], gate_weight[...], cols_cols) + mm(
        grad_up[...], up_weight[...], cols_cols
    )
    piece = count // ways
    for k in range(ways):
        at = pl.multiple_of((info[1] ^ k) * piece, piece)
        pieces[k][...] = whole_part[pl.ds(at, piece), :].astype(bf16)


def feed_grad_kernel(
    inner, normed, grad_gate, grad_up, out_grad, down_weight, encoded, down, gate, up
):
    encoded[...] = mm(inner[...], down_weight[...]).astype(bf16)
    down[...] = mm(inner[...], out_grad[...], rows_rows).astype(bf16)
    gate[...] = mm(normed[...], grad_gate[...], rows_rows).astype(bf16)
    up[...] = mm(normed[...], grad_up[...], rows_rows).astype(bf16)


def middle_kernel(ways, info, *refs):
    pieces = refs[:ways]
    middle, out_grad, gain, grad_branch, grad_middle, grad_gain = refs[ways:]
    piece = pieces[0].shape[0]
    at = pl.multiple_of(info[1] * piece, piece)
    grad_normed = sum(item[...].astype(f32) for item in pieces)
    own = middle[pl.ds(at, piece), :]
    scale = lax.rsqrt(jnp.mean(own * own, axis=-1, keepdims=True) + epsilon)
    grad_gain[...] = jnp.sum(grad_normed * own * scale, axis=0, keepdims=True)
    through = grad_normed * gain[...].astype(f32)
    total = (
        out_grad[pl.ds(at, piece), :].astype(f32)
        + scale * through
        - own * (scale * scale * scale) * jnp.mean(through * own, axis=-1, keepdims=True)
    )
    grad_middle[...] = total
    grad_branch[...] = total.astype(bf16)


def attend_back_kernel(heads, ways, info, *refs):
    branches = refs[:ways]
    attended, probs, queries, keys, values, normed, out_weight, rel_bias = refs[ways : ways + 8]
    out_grad, query_grad, key_grad, value_grad, rel_grad = refs[ways + 8 : ways + 13]
    grad_queries, grad_keys, grad_values, branch = refs[ways + 13 :]
    count, width = queries.shape
    seq_tokens = keys.shape[0]
    head_dim = width // heads
    piece = branches[0].shape[0]
    for k in range(ways):
        at = pl.multiple_of((info[1] ^ k) * piece, piece)
        branch[pl.ds(at, piece), :] = branches[k][...]
    query_first = pl.multiple_of(info[2] * count, count)
    grad_attended = mm(branch[...], out_weight[...], cols_cols).astype(bf16)
    out_grad[...] = mm(attended[...], branch[...], rows_rows).astype(bf16)
    span = seq_tokens + count
    flip = (iota((count, count), 0) + iota((count, count), 1) == count - 1).astype(bf16)
    zero = jnp.zeros((), bf16)
    by_offset = []
    query_sum = jnp.zeros((count, width), f32)
    key_sum = jnp.zeros((seq_tokens, width), f32)
    value_sum = jnp.zeros((seq_tokens, width), f32)
    for head in range(heads):
        mask = head_mask(width, head_dim, head)
        own = jnp.where(mask, grad_attended, zero)
        grad_probs = mm(own, values[...], cols_cols)
        part = probs[head].astype(f32)
        inside = jnp.sum(part * grad_probs, axis=-1, keepdims=True)
        grad_scores = (part * (grad_probs - inside)).astype(bf16)
        flipped = jnp.concatenate(
            [mm(flip, grad_scores), jnp.zeros((count, count), f32)], axis=1
        )
        by_offset.append(
            jnp.sum(pltpu.roll(flipped, 0, 1, stride=1, stride_axis=0), axis=0, keepdims=True)
        )
        query_sum = jnp.where(mask, mm(grad_scores, keys[...]), query_sum)
        key_sum = key_sum + mm(
            grad_scores, jnp.where(mask, queries[...], zero), rows_rows
        )
        value_sum = value_sum + mm(probs[head], own, rows_rows)
    by_offset = jnp.concatenate(by_offset + [jnp.zeros((8 - heads, span), f32)], axis=0)
    hot = bucket_hot(rel_bias.shape[0], span, query_first, count)
    rel_grad[...] = exact(hot, by_offset, cols_cols)
    query_sum = query_sum.astype(bf16)
    query_grad[...] = mm(normed[pl.ds(query_first, count), :], query_sum, rows_rows).astype(bf16)
    grad_queries[...] = jnp.zeros(grad_queries.shape, bf16)
    grad_queries[pl.ds(query_first, count), :] = query_sum
    rest = grad_keys.shape[0] - seq_tokens
    for total, place, weight_grad in (
        (key_sum, grad_keys, key_grad),
        (value_sum, grad_values, value_grad),
    ):
        total = total.astype(bf16)
        place[0:seq_tokens, :] = total
        place[seq_tokens:, :] = jnp.zeros((rest, width), bf16)
        weight_grad[...] = mm(normed[...], total, rows_rows).astype(bf16)


def gbst_back_kernel(
    total_bytes,
    seq_tokens,
    info,
    grad_queries,
    grad_keys,
    grad_values,
    tokens,
    query_weight,
    key_weight,
    value_weight,
    gain,
    grad_middle,
    grad_gain_second,
    table,
    mixing,
    coefficients,
    size_weights,
    ids,
    pool,
    spread,
    total,
    embedding,
    conv_weight,
    conv_bias,
    score_weight,
    packed,
    natural,
    hot,
    by_byte,
    by_score,
    small,
    normed_grad,
):
    rows = ids.shape[0]
    token_rows = rows * pairs
    vocab, width = embedding.shape
    step = pl.program_id(0)
    first = step * rows
    score = score_weight[...].astype(f32)
    bias = conv_bias[...].astype(f32)

    @pl.when(step == 0)
    def _():
        by_byte[...] = jnp.zeros(by_byte.shape, f32)
        by_score[...] = jnp.zeros(by_score.shape, f32)
        small[...] = jnp.zeros(small.shape, f32)

    grad_normed = (
        mm(grad_queries[...], query_weight[...], cols_cols)
        + mm(grad_keys[...], key_weight[...], cols_cols)
        + mm(grad_values[...], value_weight[...], cols_cols)
    )
    present = token_rows * step + iota((token_rows, 1), 0) < seq_tokens
    hidden = jnp.where(present, tokens[...].astype(f32), 0.0)
    scale = lax.rsqrt(jnp.mean(hidden * hidden, axis=-1, keepdims=True) + epsilon)
    small[0:1, :] += jnp.sum(grad_normed * hidden * scale, axis=0, keepdims=True)
    through = grad_normed * gain[...].astype(f32)
    normed_grad[...] = scale * through - hidden * (scale * scale * scale) * jnp.mean(
        through * hidden, axis=-1, keepdims=True
    )
    piece = grad_middle.shape[0]
    own_first = (info[2] * lax.axis_size("tensor") + info[1]) * piece - token_rows * step
    block = int(np.gcd(piece, token_rows))
    for part in range(piece // block):
        at = own_first + part * block

        @pl.when((at >= 0) & (at < token_rows))
        def _():
            place = pl.ds(pl.multiple_of(at, block), block)
            normed_grad[place, :] += grad_middle[part * block : (part + 1) * block, :]

    for at in range(width // 128):
        natural[at] = normed_grad[:, at * 128 : (at + 1) * 128]
    for r in range(columns):
        hot[:, r * vocab : (r + 1) * vocab] = one_hot(ids[:, r : r + 1], vocab)
    row_total = exact(coefficients[...], total[...])
    lane = iota((rows, 128), 1)
    grad_coefficients = jnp.zeros((rows, 128), f32)
    bias_grad = jnp.zeros((1, width), f32)
    for j in range(pairs):
        grad_rows = jnp.concatenate(
            [natural[at, pl.ds(j, rows, stride=pairs), :] for at in range(width // 128)], axis=1
        )
        bias_grad = bias_grad + jnp.sum(row_total[:, j : j + 1] * grad_rows, axis=0, keepdims=True)
        on_bias = jnp.sum(grad_rows * bias, axis=1, keepdims=True)
        narrow = grad_rows.astype(bf16)
        by_byte[...] += mm(mixing[j], narrow, rows_rows)
        against = mm(narrow, table[...], cols_cols)
        for r in reached(j):
            picked = hot[:, r * vocab : (r + taps) * vocab].astype(f32) * against
            found = jnp.sum(picked, axis=1, keepdims=True) + on_bias
            grad_coefficients = jnp.where(lane == period * j + r, found, grad_coefficients)
    grad_coefficients = jnp.where(
        coefficient_inside(rows, first, total_bytes), grad_coefficients, 0.0
    )
    grad_sizes = [exact(grad_coefficients, spread[size], cols_cols) for size in range(4)]
    mean_grad = sum(size_weights[size] * grad_sizes[size] for size in range(4))
    grad_scores = jnp.zeros((rows, 128), f32)
    for size in range(4):
        grad_size = size_weights[size] * (grad_sizes[size] - mean_grad)
        grad_scores = grad_scores + (
            grad_size if size == 0 else exact(grad_size, pool[size - 1], cols_cols)
        )
    grad_scores = jnp.where(position_inside(rows, first, total_bytes), grad_scores, 0.0)
    score_sum = jnp.sum(jnp.sum(grad_scores, axis=1, keepdims=True), axis=0, keepdims=True)
    small[1:2, :] += bias_grad + score_sum * score
    small[2:3, :] += score_sum * bias
    for r in range(columns):
        shifted = pltpu.roll(grad_scores, 128 - r, 1) if r else grad_scores
        shifted = jnp.where(lane < taps, shifted, 0.0)
        high = shifted.astype(bf16)
        by_score[...] += mm(hot[:, r * vocab : (r + 1) * vocab], high, rows_rows)

    @pl.when(step == pl.num_programs(0) - 1)
    def _():
        emb = embedding[...].astype(f32)
        conv = conv_weight[...].astype(f32)
        grad_embedding = jnp.zeros((vocab, width), f32)
        grad_score = small[2:3, :]
        bytes_score = mm(by_score[...].astype(bf16), embedding[...], rows_rows)
        conv_rows = []
        for tap in range(taps):
            at = taps - 1 - tap
            here = by_byte[tap * vocab : (tap + 1) * vocab, :] + by_score[:, at : at + 1] * score
            grad_embedding = grad_embedding + conv[tap : tap + 1] * here
            conv_rows.append(jnp.sum(emb * here, axis=0, keepdims=True))
            grad_score = grad_score + conv[tap : tap + 1] * bytes_score[at : at + 1, :]
        rest = packed.shape[0] - vocab
        tail = conv_rows + [small[1:2, :], grad_score, small[0:1, :], grad_gain_second[...]]
        tail = jnp.concatenate(tail + [jnp.zeros((rest - len(tail), width), f32)], axis=0)
        packed[0:vocab, :] = grad_embedding.astype(bf16)
        packed[vocab:, :] = tail.astype(bf16)


def exchange(value, axis, mask):
    size = lax.axis_size(axis)
    return lax.ppermute(value, axis, [(i, i ^ mask) for i in range(size)])


def shards(
    byte_ids,
    byte_lengths,
    embedding,
    conv_weight,
    conv_bias,
    score_weight,
    norm_first,
    query_weight,
    key_weight,
    value_weight,
    out_weight,
    rel_bias,
    norm_second,
    gate_weight,
    up_weight,
    down_weight,
    out_grad,
):
    group = byte_ids.shape[1]
    ways = lax.axis_size("tensor")
    section, tensor, seq = (lax.axis_index(name) for name in ("section", "tensor", "seq"))
    total_bytes = group * lax.axis_size("seq")
    count = group // 2
    seq_tokens = total_bytes // 2
    heads = rel_bias.shape[1]
    width = query_weight.shape[1]
    vocab, model = embedding.shape
    units = gate_weight.shape[1]
    piece = count // ways
    conv_bias, score_weight, norm_first, norm_second = (
        item[None, :] for item in (conv_bias, score_weight, norm_first, norm_second)
    )
    length = byte_lengths[section]
    info = jnp.stack([section, tensor, seq, length]).astype(jnp.int32)
    steps = -(-total_bytes // (period * chunk_rows))
    rows = steps * chunk_rows
    token_rows = rows * pairs
    chunk_tokens = chunk_rows * pairs

    own_ids = lax.dynamic_index_in_dim(byte_ids, section, 0, keepdims=False)
    all_ids = lax.all_gather(own_ids, "seq", axis=0, tiled=True)
    all_ids = jnp.where(jnp.arange(total_bytes) < length, all_ids, -1)
    padded = jnp.pad(all_ids, (2, rows * period - total_bytes + 10), constant_values=-1)
    ids = jnp.concatenate(
        [
            padded[: rows * period].reshape(rows, period),
            padded[period : (rows + 1) * period].reshape(rows, period)[:, : taps - 1],
        ],
        axis=1,
    )
    out_weights = [out_weight] + [exchange(out_weight, "tensor", k) for k in range(1, ways)]
    pool, spread, total = (jnp.asarray(item) for item in pool_tables())
    table, score_table, bias_score = call(
        prepare_kernel,
        [like((taps * vocab, model), bf16), like((vocab, 128), bf16), like((8, 128), f32)],
        embedding,
        conv_weight,
        score_weight,
        conv_bias,
    )

    tokens, mixing, coefficients, size_weights = call(
        functools.partial(gbst_kernel, total_bytes),
        [
            like((token_rows, model), bf16),
            like((pairs, rows, taps * vocab), bf16),
            like((rows, 128), f32),
            like((4, rows, 128), f32),
        ],
        ids,
        table,
        score_table,
        pool,
        spread,
        total,
        conv_bias,
        bias_score,
        specs=[pl.BlockSpec((chunk_rows, columns), lambda i: (i, 0))] + [whole] * 7,
        out_specs=[
            pl.BlockSpec((chunk_tokens, model), lambda i: (i, 0)),
            pl.BlockSpec((pairs, chunk_rows, taps * vocab), lambda i: (0, i, 0)),
            pl.BlockSpec((chunk_rows, 128), lambda i: (i, 0)),
            pl.BlockSpec((4, chunk_rows, 128), lambda i: (0, i, 0)),
        ],
        scratch=[
            pltpu.VMEM((chunk_rows, columns * vocab), bf16),
            pltpu.VMEM((model // 128, chunk_tokens, 128), f32),
        ],
        grid=(steps,),
    )

    normed, queries, keys, values, probs, attended = call(
        functools.partial(attend_kernel, heads),
        [
            like((seq_tokens, model), bf16),
            like((count, width), bf16),
            like((seq_tokens, width), bf16),
            like((seq_tokens, width), bf16),
            like((heads, count, seq_tokens), bf16),
            like((count, width), bf16),
        ],
        info,
        tokens,
        norm_first,
        query_weight,
        key_weight,
        value_weight,
        rel_bias,
        specs=[scalars] + [whole] * 6,
    )
    all_attended = [attended] + [exchange(attended, "tensor", k) for k in range(1, ways)]

    def of_section(*dims):
        return pl.BlockSpec((None, *dims), lambda i, info: (info[0], *(0 for _ in dims)))

    def feed_call(kernel, out, args, specs, scratch=()):
        return pl.pallas_call(
            kernel,
            out_shape=out,
            grid_spec=pltpu.PrefetchScalarGridSpec(
                num_scalar_prefetch=1,
                grid=(1,),
                in_specs=specs,
                out_specs=[whole] * len(out),
                scratch_shapes=list(scratch),
            ),
            compiler_params=pltpu.CompilerParams(vmem_limit_bytes=vmem_limit),
        )(*args)

    middle, normed_second, inner, grad_gate, grad_up, *normed_parts = feed_call(
        functools.partial(feed_kernel, ways),
        [
            like((count, model), f32),
            like((count, model), bf16),
            like((count, units), bf16),
            like((count, units), bf16),
            like((count, units), bf16),
        ]
        + [like((piece, model), bf16)] * ways,
        [info, *all_attended, *out_weights, tokens, norm_second]
        + [gate_weight, up_weight, down_weight, out_grad],
        [whole] * (2 * ways + 5) + [of_section(count, model)],
        [pltpu.VMEM((count, model), f32)],
    )
    normed_parts = normed_parts[:1] + [
        exchange(normed_parts[k], "tensor", k) for k in range(1, ways)
    ]

    def feed_grads(info, *refs):
        feed_grad_kernel(*refs)

    encoded, grad_down, grad_gate_weight, grad_up_weight = feed_call(
        feed_grads,
        [
            like((count, model), bf16),
            like((units, model), bf16),
            like((model, units), bf16),
            like((model, units), bf16),
        ],
        [info, inner, normed_second, grad_gate, grad_up, out_grad, down_weight],
        [whole] * 4 + [of_section(count, model), whole],
    )
    output = (middle + lax.psum(encoded, "tensor").astype(f32)).astype(bf16)[None]

    grad_branch, grad_middle, grad_gain_second = feed_call(
        functools.partial(middle_kernel, ways),
        [like((piece, model), bf16), like((piece, model), f32), like((1, model), f32)],
        [info, *normed_parts, middle, out_grad, norm_second],
        [whole] * (ways + 1) + [of_section(count, model), whole],
    )
    branches = [grad_branch] + [exchange(grad_branch, "tensor", k) for k in range(1, ways)]
    (
        grad_out_weight,
        grad_query_weight,
        grad_key_weight,
        grad_value_weight,
        grad_rel,
        grad_queries,
        grad_keys,
        grad_values,
    ) = call(
        functools.partial(attend_back_kernel, heads, ways),
        [
            like((width, model), bf16),
            like((model, width), bf16),
            like((model, width), bf16),
            like((model, width), bf16),
            like((rel_bias.shape[0], 8), f32),
            like((token_rows, width), bf16),
            like((token_rows, width), bf16),
            like((token_rows, width), bf16),
        ],
        info,
        *branches,
        attended,
        probs,
        queries,
        keys,
        values,
        normed,
        out_weight,
        rel_bias,
        specs=[scalars] + [whole] * (ways + 8),
        scratch=[pltpu.VMEM((count, model), bf16)],
    )

    per_chunk = pl.BlockSpec((chunk_tokens, width), lambda i: (i, 0))
    packed_rows = 16 * ways * -(-(vocab + taps + 4) // (16 * ways))
    packed = call(
        functools.partial(gbst_back_kernel, total_bytes, seq_tokens),
        like((packed_rows, model), bf16),
        info,
        grad_queries,
        grad_keys,
        grad_values,
        tokens,
        query_weight,
        key_weight,
        value_weight,
        norm_first,
        grad_middle,
        grad_gain_second,
        table,
        mixing,
        coefficients,
        size_weights,
        ids,
        pool,
        spread,
        total,
        embedding,
        conv_weight,
        conv_bias,
        score_weight,
        specs=[scalars]
        + [per_chunk] * 3
        + [pl.BlockSpec((chunk_tokens, model), lambda i: (i, 0))]
        + [whole] * 7
        + [
            pl.BlockSpec((pairs, chunk_rows, taps * vocab), lambda i: (0, i, 0)),
            pl.BlockSpec((chunk_rows, 128), lambda i: (i, 0)),
            pl.BlockSpec((4, chunk_rows, 128), lambda i: (0, i, 0)),
            pl.BlockSpec((chunk_rows, columns), lambda i: (i, 0)),
        ]
        + [whole] * 7,
        scratch=[
            pltpu.VMEM((model // 128, chunk_tokens, 128), f32),
            pltpu.VMEM((chunk_rows, columns * vocab), bf16),
            pltpu.VMEM((taps * vocab, model), f32),
            pltpu.VMEM((vocab, 128), f32),
            pltpu.VMEM((8, model), f32),
            pltpu.VMEM((chunk_tokens, model), f32),
        ],
        grid=(steps,),
    )
    packed = lax.psum(packed, ("section", "tensor", "seq")).astype(f32)
    sums = lax.psum(
        (
            grad_query_weight,
            grad_key_weight,
            grad_value_weight,
            grad_out_weight,
            grad_rel[:, :heads].astype(bf16),
            grad_gate_weight,
            grad_up_weight,
            grad_down,
        ),
        ("section", "seq"),
    )
    sums = [item.astype(f32) for item in sums]
    tail = packed[vocab:]
    return (
        output,
        packed[:vocab],
        tail[:taps],
        tail[taps],
        tail[taps + 1],
        tail[taps + 2],
        sums[0],
        sums[1],
        sums[2],
        sums[3],
        sums[4],
        tail[taps + 3],
        sums[5],
        sums[6],
        sums[7],
    )


def solution(mesh):
    return jax.shard_map(
        shards,
        mesh=mesh,
        in_specs=(
            P(None, "seq"),
            P(),
            P(),
            P(),
            P(),
            P(),
            P(),
            P(None, "tensor"),
            P(None, "tensor"),
            P(None, "tensor"),
            P("tensor", None),
            P(None, "tensor"),
            P(),
            P(None, "tensor"),
            P(None, "tensor"),
            P("tensor", None),
            P(None, "seq", None),
        ),
        out_specs=(
            P("section", "seq", None),
            P(),
            P(),
            P(),
            P(),
            P(),
            P(None, "tensor"),
            P(None, "tensor"),
            P(None, "tensor"),
            P("tensor", None),
            P(None, "tensor"),
            P(),
            P(None, "tensor"),
            P(None, "tensor"),
            P("tensor", None),
        ),
        check_vma=False,
    )
```

time: 5700 us -> 373 us (0.07); the launches traced: 5620 us -> 373 us
  waiting for transfers between devices: 5270 us -> 221 us
  other arithmetic: 116 us -> 9.41 us
  blocking collectives: 91.4 us -> 28.1 us
  Pallas kernels: 0 us -> 58.8 us
    reduce_scatter x2 -> x0, waiting for transfers between devices: 3510 us -> none  [t5_micro(): lax.psum_scatter(on_section(second_section, term_work, grad_scores, probs...]
    psum x4 -> x3, waiting for transfers between devices: 1760 us -> 202 us  [the longest x1 110 us: shards(): packed = lax.psum(packed, ('section', 'tensor', 'seq')).astype(f32)]
    pallas_call x0 -> x8, Pallas kernels: none -> 58.8 us  [the longest x5 45 us: call(): pl.pallas_call(kernel, out_shape=out, in_specs=[whole] * len(args) if spe...]
  transfers between devices with their start and end apart: 13 -> 15, of which waited for: 7 -> 10; matrix products, arithmetic and copies ran while one was open for 1% -> 6% of each run, Pallas kernels for 0% -> 13%
where the time goes in v1:
time: 373 us
  waiting for transfers between devices  221 us (59%)
  Pallas kernels  58.8 us (16%)
  blocking collectives  28.1 us (8%)
  local copies, waits for them, and re-layouts  24.6 us (7%)
  starting transfers between devices  16.4 us (4%)
  between operations  13.9 us (4%)
  other arithmetic  9.41 us (3%)
    psum x1, waiting for transfers between devices, shards(): packed = lax.psum(packed, ('section', 'tensor', 'seq')).astype(f32)  110 us
    psum x1, waiting for transfers between devices, shards(): lax.psum((grad_query_weight, grad_key_weight, grad_value_weight, grad_out...  92 us
    pallas_call x5, Pallas kernels, call(): pl.pallas_call(kernel, out_shape=out, in_specs=[whole] * len(args) if spe...  45 us
    ppermute x12, waiting for transfers between devices, exchange(): return lax.ppermute(value, axis, [(i, i ^ mask) for i in range(size)])  18.3 us
    ppermute x12, starting transfers between devices, exchange(): return lax.ppermute(value, axis, [(i, i ^ mask) for i in range(size)])  16.2 us
    psum x1, blocking collectives, shards(): lax.psum((grad_query_weight, grad_key_weight, grad_value_weight, grad_out...  15.6 us
    unnamed x60, local copies, waits for them, and re-layouts  14.7 us
    pallas_call x3, Pallas kernels, feed_call(): pl.pallas_call(kernel, out_shape=out, grid_spec=pltpu.PrefetchScalarGridS...  13.8 us
  transfers between devices with their start and end apart: 15, of which 10 were waited for; matrix products, arithmetic and copies ran while one was open for 6% of the time, Pallas kernels for 13%

profile of v1, /device:TPU:0, one launch (start us, length us, event | category | flops | bytes accessed | tf_op | source)
XLA Modules:
  0.0 372.6 jit_solution(6872610728180073304)
XLA Ops:
  7.3 4.0 %collective-permute-start.5 = (bf16[192,768]{1,0:T(8,128)(2,1)}, bf16[192,768]{1,0:T(8,128)(2,1)S(1)}, u32[]{:S(2)}, u32[]{:S(2)}) collective-permute-start(bf16[192,768]{1,0:T(8,128)(2,1)} %refs_10_.3), channel_id=1, source_target_pairs={{0,12},{4,8},{8,4},{12,0},{1,13},{5,9},{9,5},{13,1},{2,14},{6,10},... | collective-permute-start | bytes 884744 | tf_op jit(solution)/shard_map/ppermute | solution.py:514
  16.9 12.5 %all-gather = s32[1,2048]{1,0:T(1,128)S(1)} all-gather(s32[1,512]{1,0:T(1,128)S(1)} %constant_dynamic-slice_fusion), channel_id=2, replica_groups=mesh['section'=2,'tensor'=4,'seq'=4] {'seq'}, dimensions={1}, use_global_device_ids=true | all-gather | bytes 10240 | tf_op jit(solution)/shard_map/all_gather | solution.py:558
  33.6 1.9 copy.76.key_weight
  37.2 2.8 shard_map.307
  40.0 8.2 %shard_map.308 = (bf16[1056,768]{1,0:T(8,128)(2,1)}, bf16[6,176,1280]{2,1,0:T(8,128)(2,1)}, f32[176,128]{1,0:T(8,128)}, f32[4,176,128]{2,1,0:T(8,128)}) custom-call(s32[176,16]{1,0:T(8,128)} %pad_add_fusion.ids, bf16[1280,768]{1,0:T(8,128)(2,1)} %get-tuple-element.52.table, bf16[256,128]{1,0:T(8,128)(2,1)} %get-tuple-element.53.score_table, ...), custom_call_target="tpu_custom_call" | custom-call | tf_op jit(solution)/shard_map/pallas_call | solution.py:67
  49.5 6.3 %shard_map.309 = (bf16[1024,768]{1,0:T(8,128)(2,1)}, bf16[256,192]{1,0:T(8,128)(2,1)}, bf16[1024,192]{1,0:T(8,128)(2,1)}, bf16[1024,192]{1,0:T(8,128)(2,1)}, bf1...) custom-call(s32[4]{0:T(128)} %pad_add_fusion.1.info, bf16[1056,768]{1,0:T(8,128)(2,1)} %get-tuple-element.55.tokens.refs_8_, ...), custom_call_target="tpu_custom_call" | custom-call | tf_op jit(solution)/shard_map/pallas_call | solution.py:67
  55.8 2.4 collective-permute-start.2
  58.8 3.7 %collective-permute-done.2.refs_3_ = bf16[256,192]{1,0:T(8,128)(2,1)S(1)} collective-permute-done((bf16[256,192]{1,0:T(8,128)(2,1)}, bf16[256,192]{1,0:T(8,128)(2,1)S(1)}, u32[]{:S(2)}, u32[]{:S(2)}) %collective-permute-start.2) | collective-permute-done | bytes 98336 | tf_op jit(solution)/shard_map/ppermute | solution.py:514
  64.6 3.1 collective-permute-done.refs_1_
  69.3 6.4 %shard_map.310 = (f32[256,768]{1,0:T(8,128)}, bf16[256,768]{1,0:T(8,128)(2,1)}, bf16[256,512]{1,0:T(8,128)(2,1)}, bf16[256,512]{1,0:T(8,128)(2,1)}, bf16[256,512...) custom-call(s32[4]{0:T(128)} %pad_add_fusion.1.info, ...), custom_call_target="tpu_custom_call" | custom-call | tf_op jit(solution)/shard_map/pallas_call | solution.py:634
  75.7 4.4 %shard_map.311 = (bf16[256,768]{1,0:T(8,128)(2,1)}, bf16[512,768]{1,0:T(8,128)(2,1)}, bf16[768,512]{1,0:T(8,128)(2,1)}, bf16[768,512]{1,0:T(8,128)(2,1)}) custom-call(s32[4]{0:T(128)} %pad_add_fusion.1.info, bf16[256,512]{1,0:T(8,128)(2,1)} %get-tuple-element.58.refs_0_, bf16[256,768]{1,0:T(8,128)(2,1)} %get-tuple-element.59.refs_1_, ...), custom_call_target="tpu_custom_call" | custom-call | tf_op jit(solution)/shard_map/pallas_call | solution.py:634
  81.7 2.1 collective-permute-start.7
  86.4 4.8 %collective-permute-done.8.refs_3_ = bf16[64,768]{1,0:T(8,128)(2,1)S(1)} collective-permute-done((bf16[64,768]{1,0:T(8,128)(2,1)S(1)}, bf16[64,768]{1,0:T(8,128)(2,1)S(1)}, u32[]{:S(2)}, u32[]{:S(2)}) %collective-permute-start.8) | collective-permute-done | bytes 98336 | tf_op jit(solution)/shard_map/ppermute | solution.py:514
  91.8 3.0 shard_map.312
  94.8 2.0 collective-permute-start.10
  98.3 2.3 collective-permute-done.11.refs_3_
  103.1 8.2 %shard_map.313 = (bf16[192,768]{1,0:T(8,128)(2,1)}, bf16[768,192]{1,0:T(8,128)(2,1)}, bf16[768,192]{1,0:T(8,128)(2,1)}, bf16[768,192]{1,0:T(8,128)(2,1)}, f32[32...) custom-call(s32[4]{0:T(128)} %pad_add_fusion.1.info, ...), custom_call_target="tpu_custom_call" | custom-call | tf_op jit(solution)/shard_map/pallas_call | solution.py:67
  111.3 19.5 %shard_map.314 = bf16[320,768]{1,0:T(8,128)(2,1)} custom-call(s32[4]{0:T(128)} %pad_add_fusion.1.info, bf16[1056,192]{1,0:T(8,128)(2,1)} %get-tuple-element.73.grad_queries, bf16[1056,192]{1,0:T(8,128)(2,1)} %get-tuple-element.74.grad_keys, bf16[1056,192]{1,0:T(8,128)(2,1)} %get-tuple-element.75.grad_values, ...), custom_call_target="tpu_custom_call" | custom-call | tf_op jit(solution)/shard_map/pallas_call | solution.py:67
  131.6 15.6 %psum.76 = bf16[32,3]{1,0:T(8,128)(2,1)S(1)} all-reduce(bf16[32,3]{1,0:T(8,128)(2,1)S(1)} %slice.78), channel_id=1, replica_groups=mesh['section'=2,'tensor'=4,'seq'=4] {'section','seq'}, use_global_device_ids=true, to_apply=%region_6.7 | all-reduce | flops 96 | bytes 384 | tf_op jit(solution)/shard_map/psum | solution.py:774
  149.7 110.4 %all-reduce.8.cloned.1.call-done = bf16[320,768]{1,0:T(8,128)(2,1)} async-done(((bf16[320,768]{1,0:T(8,128)(2,1)}), bf16[320,768]{1,0:T(8,128)(2,1)}) %all-reduce.8.cloned.1.call-update) | async-done | bytes 491536 | tf_op jit(solution)/shard_map/psum | solution.py:773
  261.5 1.9 slice.64
  264.2 92.0 %all-reduce.10.cloned.1.call-done = (bf16[768,192]{1,0:T(8,128)(2,1)}, bf16[768,192]{1,0:T(8,128)(2,1)}, bf16[768,192]{1,0:T(8,128)(2,1)}, bf16[192,768]{1,0:T(8...) async-done(((bf16[768,192]{1,0:T(8,128)(2,1)}, bf16[768,192]{1,0:T(8,128)(2,1)}, bf16[768,192]{1,0:T(8,128)(2,1)}, ...) | async-done | bytes 3538960 | tf_op jit(solution)/shard_map/psum | solution.py:774
  356.1 2.0 copy.83
  358.2 2.0 copy.84
  (101 shorter events, 37.0 us)
Async XLA Ops:
  7.2 5.9 %copy-start = (s32[2,512]{1,0:T(2,128)S(1)}, s32[2,512]{1,0:T(2,128)}, u32[]{:S(2)}) copy-start(s32[2,512]{1,0:T(2,128)} %param.20) | copy-start | bytes 12292
  7.2 28.3 %copy-start.8 = (bf16[768,192]{0,1:T(8,128)(2,1)S(1)}, bf16[768,192]{0,1:T(8,128)(2,1)}, u32[]{:S(2)}) copy-start(bf16[768,192]{0,1:T(8,128)(2,1)} %param.29) | copy-start | bytes 884740
  7.2 140.7 %all-reduce.6.cloned.1.call-start = ((), (), s32[]{:S(2)}) async-start(), calls=%async_computation | async-start | bytes 786432 | tf_op jit(solution)/shard_map/psum | solution.py:680
  7.3 60.4 %collective-permute-start.5 = (bf16[192,768]{1,0:T(8,128)(2,1)}, bf16[192,768]{1,0:T(8,128)(2,1)S(1)}, u32[]{:S(2)}, u32[]{:S(2)}) collective-permute-start(bf16[192,768]{1,0:T(8,128)(2,1)} %refs_10_.3), channel_id=1, source_target_pairs={{0,12},{4,8},{8,4},{12,0},{1,13},{5,9},{9,5},{13,1},{2,14},{6,10},... | collective-permute-start | bytes 884744 | tf_op jit(solution)/shard_map/ppermute | solution.py:514
  11.2 56.5 %collective-permute-start.4 = (bf16[192,768]{1,0:T(8,128)(2,1)}, bf16[192,768]{1,0:T(8,128)(2,1)S(1)}, u32[]{:S(2)}, u32[]{:S(2)}) collective-permute-start(bf16[192,768]{1,0:T(8,128)(2,1)} %refs_10_.3), channel_id=1, source_target_pairs={{0,8},{4,12},{8,0},{12,4},{1,9},{5,13},{9,1},{13,5},{2,10},{6,14},... | collective-permute-start | bytes 884744 | tf_op jit(solution)/shard_map/ppermute | solution.py:514
  11.7 56.0 %collective-permute-start.3 = (bf16[192,768]{1,0:T(8,128)(2,1)}, bf16[192,768]{1,0:T(8,128)(2,1)S(1)}, u32[]{:S(2)}, u32[]{:S(2)}) collective-permute-start(bf16[192,768]{1,0:T(8,128)(2,1)} %refs_10_.3), channel_id=1, source_target_pairs={{0,4},{4,0},{8,12},{12,8},{1,5},{5,1},{9,13},{13,9},{2,6},{6,2},{1... | collective-permute-start | bytes 884744 | tf_op jit(solution)/shard_map/ppermute | solution.py:514
  48.2 15.8 %copy-start.22 = (bf16[768]{0:T(1024)(128)(2,1)S(1)}, bf16[768]{0:T(1024)(128)(2,1)}, u32[]{:S(2)}) copy-start(bf16[768]{0:T(1024)(128)(2,1)} %param.32) | copy-start | bytes 4612
  55.8 6.7 %collective-permute-start.2 = (bf16[256,192]{1,0:T(8,128)(2,1)}, bf16[256,192]{1,0:T(8,128)(2,1)S(1)}, u32[]{:S(2)}, u32[]{:S(2)}) collective-permute-start(bf16[256,192]{1,0:T(8,128)(2,1)} %get-tuple-element.56.refs_0_.refs_4_), channel_id=1, source_target_pairs={{0,12},{4,8},{8,4},{12,0},{1,13},{5,9},{9,5},{13,1},{2,14},{6,10},... | collective-permute-start | bytes 294920 | tf_op jit(solution)/shard_map/ppermute | solution.py:514
  58.3 6.3 %collective-permute-start.1 = (bf16[256,192]{1,0:T(8,128)(2,1)}, bf16[256,192]{1,0:T(8,128)(2,1)S(1)}, u32[]{:S(2)}, u32[]{:S(2)}) collective-permute-start(bf16[256,192]{1,0:T(8,128)(2,1)} %get-tuple-element.56.refs_0_.refs_4_), channel_id=1, source_target_pairs={{0,8},{4,12},{8,0},{12,4},{1,9},{5,13},{9,1},{13,5},{2,10},{6,14},... | collective-permute-start | bytes 294920 | tf_op jit(solution)/shard_map/ppermute | solution.py:514
  62.5 5.2 %copy-start.12 = (bf16[256,192]{1,0:T(8,128)(2,1)}, bf16[256,192]{1,0:T(8,128)(2,1)S(1)}, u32[]{:S(2)}) copy-start(bf16[256,192]{1,0:T(8,128)(2,1)S(1)} %collective-permute-done.2.refs_3_) | copy-start | bytes 294916
  62.5 5.2 %collective-permute-start = (bf16[256,192]{1,0:T(8,128)(2,1)}, bf16[256,192]{1,0:T(8,128)(2,1)S(1)}, u32[]{:S(2)}, u32[]{:S(2)}) collective-permute-start(bf16[256,192]{1,0:T(8,128)(2,1)} %get-tuple-element.56.refs_0_.refs_4_), channel_id=1, source_target_pairs={{0,4},{4,0},{8,12},{12,8},{1,5},{5,1},{9,13},{13,9},{2,6},{6,2},{1... | collective-permute-start | bytes 294920 | tf_op jit(solution)/shard_map/ppermute | solution.py:514
  75.7 6.1 %copy-start.24 = (bf16[64,768]{1,0:T(8,128)(2,1)S(1)}, bf16[64,768]{1,0:T(8,128)(2,1)}, u32[]{:S(2)}) copy-start(bf16[64,768]{1,0:T(8,128)(2,1)} %get-tuple-element.65) | copy-start | bytes 294916
  75.7 8.2 %copy-start.23 = (bf16[64,768]{1,0:T(8,128)(2,1)S(1)}, bf16[64,768]{1,0:T(8,128)(2,1)}, u32[]{:S(2)}) copy-start(bf16[64,768]{1,0:T(8,128)(2,1)} %get-tuple-element.66) | copy-start | bytes 294916
  80.1 180.0 %all-reduce.8.cloned.1.call-start = ((), (), s32[]{:S(2)}) async-start(), calls=%async_computation.1 | async-start | bytes 983040 | tf_op jit(solution)/shard_map/psum | solution.py:773
  80.2 4.7 %collective-permute-start.6 = (bf16[64,768]{1,0:T(8,128)(2,1)S(1)}, bf16[64,768]{1,0:T(8,128)(2,1)S(1)}, u32[]{:S(2)}, u32[]{:S(2)}) collective-permute-start(bf16[64,768]{1,0:T(8,128)(2,1)S(1)} %copy-done.25), channel_id=1, source_target_pairs={{0,4},{4,0},{8,12},{12,8},{1,5},{5,1},{9,13},{13,9},{2,6},{6,2},{1... | collective-permute-start | bytes 294920 | tf_op jit(solution)/shard_map/ppermute | solution.py:514
  81.7 4.7 %collective-permute-start.7 = (bf16[64,768]{1,0:T(8,128)(2,1)S(1)}, bf16[64,768]{1,0:T(8,128)(2,1)S(1)}, u32[]{:S(2)}, u32[]{:S(2)}) collective-permute-start(bf16[64,768]{1,0:T(8,128)(2,1)S(1)} %copy-done.24), channel_id=1, source_target_pairs={{0,8},{4,12},{8,0},{12,4},{1,9},{5,13},{9,1},{13,5},{2,10},{6,14},... | collective-permute-start | bytes 294920 | tf_op jit(solution)/shard_map/ppermute | solution.py:514
  83.8 7.3 %collective-permute-start.8 = (bf16[64,768]{1,0:T(8,128)(2,1)S(1)}, bf16[64,768]{1,0:T(8,128)(2,1)S(1)}, u32[]{:S(2)}, u32[]{:S(2)}) collective-permute-start(bf16[64,768]{1,0:T(8,128)(2,1)S(1)} %copy-done.23), channel_id=1, source_target_pairs={{0,12},{4,8},{8,4},{12,0},{1,13},{5,9},{9,5},{13,1},{2,14},{6,10},... | collective-permute-start | bytes 294920 | tf_op jit(solution)/shard_map/ppermute | solution.py:514
  84.9 6.3 %copy-start.15 = (bf16[64,768]{1,0:T(8,128)(2,1)}, bf16[64,768]{1,0:T(8,128)(2,1)S(1)}, u32[]{:S(2)}) copy-start(bf16[64,768]{1,0:T(8,128)(2,1)S(1)} %collective-permute-done.6.refs_1_) | copy-start | bytes 294916
  94.8 5.8 %collective-permute-start.11 = (bf16[64,768]{1,0:T(8,128)(2,1)}, bf16[64,768]{1,0:T(8,128)(2,1)S(1)}, u32[]{:S(2)}, u32[]{:S(2)}) collective-permute-start(bf16[64,768]{1,0:T(8,128)(2,1)} %get-tuple-element.67.refs_0_), channel_id=1, source_target_pairs={{0,12},{4,8},{8,4},{12,0},{1,13},{5,9},{9,5},{13,1},{2,14},{6,10},... | collective-permute-start | bytes 294920 | tf_op jit(solution)/shard_map/ppermute | solution.py:514
  94.8 5.9 %collective-permute-start.10 = (bf16[64,768]{1,0:T(8,128)(2,1)}, bf16[64,768]{1,0:T(8,128)(2,1)S(1)}, u32[]{:S(2)}, u32[]{:S(2)}) collective-permute-start(bf16[64,768]{1,0:T(8,128)(2,1)} %get-tuple-element.67.refs_0_), channel_id=1, source_target_pairs={{0,8},{4,12},{8,0},{12,4},{1,9},{5,13},{9,1},{13,5},{2,10},{6,14},... | collective-permute-start | bytes 294920 | tf_op jit(solution)/shard_map/ppermute | solution.py:514
  96.8 5.7 %collective-permute-start.9 = (bf16[64,768]{1,0:T(8,128)(2,1)}, bf16[64,768]{1,0:T(8,128)(2,1)S(1)}, u32[]{:S(2)}, u32[]{:S(2)}) collective-permute-start(bf16[64,768]{1,0:T(8,128)(2,1)} %get-tuple-element.67.refs_0_), channel_id=1, source_target_pairs={{0,4},{4,0},{8,12},{12,8},{1,5},{5,1},{9,13},{13,9},{2,6},{6,2},{1... | collective-permute-start | bytes 294920 | tf_op jit(solution)/shard_map/ppermute | solution.py:514
  130.9 225.3 %all-reduce.10.cloned.1.call-start = ((), (), s32[]{:S(2)}) async-start(), calls=%async_computation.2 | async-start | bytes 7667712 | tf_op jit(solution)/shard_map/psum | solution.py:774
  130.9 17.0 %copy-start.2 = (f32[256,768]{1,0:T(8,128)S(1)}, f32[256,768]{1,0:T(8,128)}, u32[]{:S(2)}) copy-start(f32[256,768]{1,0:T(8,128)} %get-tuple-element.57.refs_4_) | copy-start | bytes 2359300
  356.1 5.1 %copy-start.7 = (bf16[192,768]{1,0:T(8,128)(2,1)S(1)}, bf16[192,768]{1,0:T(8,128)(2,1)}, u32[]{:S(2)}) copy-start(bf16[192,768]{1,0:T(8,128)(2,1)} %get-tuple-element.156) | copy-start | bytes 884740
  (17 other events, 35.7 us)
Sparse Core Ops, SparseCore 0:
  80.2 46.3 all-reduce.5
  133.4 126.7 all-reduce.7
  263.7 92.4 all-reduce.9

commit v2 on v1

v2 whole, which is shorter than its diff:
```python
import functools

import jax
import jax.numpy as jnp
import numpy as np
from jax import lax
from jax.experimental import pallas as pl
from jax.experimental.pallas import tpu as pltpu
from jax.sharding import PartitionSpec as P

epsilon = 1e-06
masked_score = -1e30
far_thresholds = (12, 16, 23, 32, 46, 64, 91)
period = 12
pairs = period // 2
taps = 5
columns = period + taps - 1
chunk_rows = 176
feed_chunks = 1
f32 = jnp.float32
bf16 = jnp.bfloat16
whole = pl.BlockSpec(memory_space=pltpu.VMEM)
local = pl.BlockSpec(memory_space=pltpu.VMEM)
distant = pl.BlockSpec(memory_space=pltpu.VMEM)
scalars = pl.BlockSpec(memory_space=pltpu.SMEM)


def pool_tables():
    pool = np.zeros((128, 384), np.float32)
    spread = np.zeros((512, 128), np.float32)
    total = np.zeros((128, 128), np.float32)
    for size in range(1, 5):
        for g in range(period):
            for r in range(period):
                if r // size == g // size:
                    if size > 1:
                        pool[4 + r, 128 * (size - 2) + 4 + g] = 1.0
                    spread[128 * (size - 1) + 4 + g, period * (g // 2) + r] = 1.0
    for j in range(pairs):
        total[period * j : period * (j + 1), j] = 1.0
    return (pool, spread, total)


def split_mm(a, b, dims=((1,), (0,))):
    high = a.astype(bf16)
    low = (a - high.astype(f32)).astype(bf16)
    return mm(high, b[...], dims) + mm(low, b[...], dims)


def lanes(value, count):
    return [value[:, 128 * i : 128 * (i + 1)] for i in range(count)]


def reached(j):
    found = set()
    for g in (2 * j, 2 * j + 1):
        for size in range(1, 5):
            first = size * (g // size)
            found.update(range(first, first + size))
    return sorted(found)


def exact(a, b, dims=((1,), (0,))):
    return lax.dot_general(
        a, b, (dims, ((), ())), precision=lax.Precision.HIGHEST, preferred_element_type=f32
    )


def mm(a, b, dims=((1,), (0,))):
    return lax.dot_general(a, b, (dims, ((), ())), preferred_element_type=f32)


rows_rows = ((0,), (0,))
cols_cols = ((1,), (1,))


def call(kernel, out, *args, specs=None, scratch=(), grid=None, out_specs=None, near=False, limit=16, cost=1):
    extra = {} if grid is None else {"grid": grid}
    specs = [whole] * len(args) if specs is None else specs
    if near:
        spaces = {id(local): pltpu.VMEM, id(distant): pltpu.HBM}
        args = [
            pltpu.with_memory_space_constraint(arg, spaces[id(spec)]) if id(spec) in spaces else arg
            for arg, spec in zip(args, specs)
        ]
    return pl.pallas_call(
        kernel,
        out_shape=out,
        in_specs=specs,
        out_specs=jax.tree.map(lambda _: whole, out) if out_specs is None else out_specs,
        scratch_shapes=list(scratch),
        cost_estimate=pl.CostEstimate(
            flops=int(cost * 1e6), bytes_accessed=int(cost * 3e3), transcendentals=0
        ),
        compiler_params=pltpu.CompilerParams(
            vmem_limit_bytes=(limit if near else 56) * 2**20
        ),
        **extra,
    )(*args)


def like(shape, kind):
    return jax.ShapeDtypeStruct(shape, kind)


def iota(shape, dim):
    return lax.broadcasted_iota(jnp.int32, shape, dim)


def bucket_of(relative):
    distance = jnp.abs(relative)
    far_bucket = 8 + sum(
        ((distance >= threshold).astype(jnp.int32) for threshold in far_thresholds)
    )
    return jnp.where(distance < 8, distance, far_bucket) + 16 * (relative > 0).astype(jnp.int32)


def bucket_hot(buckets, width, query_first, queries):
    offsets = iota((buckets, width), 1) - (queries - 1) - query_first
    return (bucket_of(offsets) == iota((buckets, width), 0)).astype(f32)


def one_hot(ids, vocab):
    return jnp.where(ids == iota((ids.shape[0], vocab), 1), 1.0, 0.0).astype(bf16)


def head_mask(width, head_dim, head):
    return iota((1, width), 1) // head_dim == head


def as_row(vector):
    return vector[...].astype(f32).reshape(1, vector.shape[0])


def fill_table(embedding, conv_weight, table):
    vocab = embedding.shape[0]
    emb = embedding[...].astype(f32)
    for tap in range(taps):
        row = conv_weight[tap : tap + 1, :].astype(f32)
        table[tap * vocab : (tap + 1) * vocab, :] = (emb * row).astype(bf16)


def prepare_kernel(embedding, conv_weight, score_weight, conv_bias, table, score_table, bias_score):
    emb = embedding[...].astype(f32)
    conv = conv_weight[...].astype(f32)
    score = as_row(score_weight)
    fill_table(embedding, conv_weight, table)
    scored = jnp.concatenate(
        [conv[tap : tap + 1] * score for tap in reversed(range(taps))]
        + [jnp.zeros((128 - taps, conv.shape[1]), f32)],
        axis=0,
    )
    by_byte = exact(emb, scored, cols_cols)
    high = by_byte.astype(bf16).astype(f32)
    middle = (by_byte - high).astype(bf16).astype(f32)
    low = by_byte - high - middle
    score_table[...] = (high + pltpu.roll(middle, 32, 1) + pltpu.roll(low, 64, 1)).astype(bf16)
    bias_score[...] = jnp.broadcast_to(
        jnp.sum(as_row(conv_bias) * score, axis=1, keepdims=True), bias_score.shape
    )


def position_inside(rows, first, total_bytes):
    lane = iota((rows, 128), 1)
    place = period * (first + iota((rows, 128), 0)) + lane - 4
    return (lane >= 4) & (lane < 4 + period) & (place < total_bytes)


def coefficient_inside(rows, first, total_bytes):
    lane = iota((rows, 128), 1)
    place = period * (first + iota((rows, 128), 0)) + lax.rem(lane, period)
    return (lane < period * pairs) & (place < total_bytes)


def laid_out(pieces, lengths, line, first, rows):
    section, seq = (lax.axis_index("section"), lax.axis_index("seq"))
    count = pieces[0].shape[1] // 128
    line[...] = jnp.full(line.shape, -1.0, f32)
    for k, item in enumerate(pieces):
        for at in range(count):
            both = item[:, at * 128 : (at + 1) * 128]
            row = jnp.where(section == 1, both[1:2], both[0:1])
            line[pl.ds((seq ^ k) * count + at + 1, 1), :] = row.astype(f32)
    place = 128 * (iota(line.shape, 0) - 1) + iota(line.shape, 1)
    values = jnp.where(place < lengths[section], line[...], -1.0).astype(bf16)
    shape = (rows, line.shape[0])
    flipped = first + rows - 1 - iota(shape, 0)
    here = (period * flipped + 126) // 128
    found = [
        mm((here + step == iota(shape, 1)).astype(bf16), values) for step in range(2)
    ]
    start = lax.rem(2 - period * (first + rows - 1) + 128 * period * (rows + first), 128)
    for _ in range(period // 4):
        found = [pltpu.roll(item, 0, 1, stride=4, stride_axis=0) for item in found]
    found = [pltpu.roll(item, start, 1) for item in found]
    shape = (rows, 128)
    lane = iota(shape, 1)
    begin = lax.rem(period * (first + rows - 1 - iota(shape, 0)) + 126, 128)
    merged_rows = jnp.where(lane + begin < 128, found[0], found[1]).astype(bf16)
    flip = (iota((rows, rows), 0) + iota((rows, rows), 1) == rows - 1).astype(bf16)
    return mm(flip, merged_rows)


def fill_hot(ids, hot, vocab):
    rows = ids.shape[0]
    value = iota((rows, vocab), 1).astype(f32)
    for r in range(columns):
        found = jnp.where(ids[:, r : r + 1] == value, 1.0, 0.0).astype(bf16)
        hot[r] = found


def gbst_kernel(total_bytes, steps, count, lengths, *refs):
    pieces = refs[:count]
    table, score_table, pool, spread, total, conv_bias, bias_score = refs[count : count + 7]
    tokens, kept, mixing, coefficients, size_weights, ids = refs[count + 7 : count + 13]
    hot, natural, line, narrow = refs[count + 13 :]
    rows = ids.shape[0]
    vocab = score_table.shape[0]
    width = table.shape[1]
    first = pl.program_id(0) * rows if steps > 1 else 0
    ids[...] = laid_out(pieces, lengths, line, first, rows)
    fill_hot(ids, hot, vocab)
    parts = mm(hot[...].reshape(columns * rows, vocab), score_table[...])
    scores = parts[:rows]
    for r in range(1, columns):
        scores = scores + pltpu.roll(parts[r * rows : (r + 1) * rows], r, 1)
    scores = scores + pltpu.roll(scores, 96, 1) + pltpu.roll(scores, 64, 1)
    scores = jnp.where(
        position_inside(rows, first, total_bytes), scores + bias_score[0:1, :], 0.0
    )
    pooled = lanes(split_mm(scores, pool), 3)
    by_size = [scores] + [item * (1.0 / (size + 2)) for size, item in enumerate(pooled)]
    largest = functools.reduce(jnp.maximum, by_size)
    weights = [jnp.exp(item - largest) for item in by_size]
    scale = 1.0 / sum(weights)
    weights = [weight * scale for weight in weights]
    for size in range(4):
        size_weights[size] = weights[size]
    weights = [weight * (0.5 / (size + 1)) for size, weight in enumerate(weights)]
    spread_sum = split_mm(jnp.concatenate(weights, axis=1), spread)
    spread_sum = jnp.where(coefficient_inside(rows, first, total_bytes), spread_sum, 0.0)
    coefficients[...] = spread_sum
    narrow[...] = spread_sum.astype(bf16)
    row_total = split_mm(spread_sum, total)

    def mix(step, carry):
        own = pl.ds(pl.multiple_of(step * 16, 16), 16)
        weight = narrow[own, :]
        for j in range(pairs):
            acc = [None] * taps
            for r in reached(j):
                at = period * j + r
                column = jnp.broadcast_to(weight[:, at : at + 1], (16, vocab))
                for tap in range(taps):
                    term = hot[r + tap, own, :] * column
                    acc[tap] = term if acc[tap] is None else acc[tap] + term
            for tap in range(taps):
                mixing[j, own, tap * vocab : (tap + 1) * vocab] = acc[tap]
        return carry

    lax.fori_loop(0, rows // 16, mix, 0, unroll=True)
    bias = as_row(conv_bias)
    by_phase = mm(mixing[...].reshape(pairs * rows, taps * vocab), table[...])
    for j in range(pairs):
        rows_j = by_phase[j * rows : (j + 1) * rows] + row_total[:, j : j + 1] * bias
        for at in range(width // 128):
            natural[at, pl.ds(j, rows, stride=pairs), :] = rows_j[:, at * 128 : (at + 1) * 128]
    for at in range(width // 128):
        tokens[:, at * 128 : (at + 1) * 128] = natural[at].astype(bf16)
    kept[...] = tokens[...]


def attend_kernel(
    heads,
    lengths,
    tokens,
    gain,
    query_weight,
    key_weight,
    value_weight,
    rel_bias,
    normed,
    queries,
    keys,
    values,
    probs,
    attended,
    own_tokens,
):
    seq_tokens = normed.shape[0]
    count, width = queries.shape
    head_dim = width // heads
    query_first = pl.multiple_of(lax.axis_index("seq") * count, count)
    live_tokens = lengths[lax.axis_index("section")]
    own_tokens[...] = tokens[pl.ds(query_first, count), :]
    hidden = tokens[0:seq_tokens, :].astype(f32)
    scale = lax.rsqrt(jnp.mean(hidden * hidden, axis=-1, keepdims=True) + epsilon)
    normed[...] = (hidden * scale * as_row(gain)).astype(bf16)
    keys[...] = mm(normed[...], key_weight[...], cols_cols).astype(bf16)
    values[...] = mm(normed[...], value_weight[...], cols_cols).astype(bf16)
    queries[...] = mm(
        normed[pl.ds(query_first, count), :], query_weight[...], cols_cols
    ).astype(bf16)
    span = seq_tokens + count
    hot = bucket_hot(rel_bias.shape[1], span, query_first, count)
    by_offset = mm(rel_bias[...].astype(f32), hot)
    live = 2 * iota((1, seq_tokens), 1) < live_tokens
    mixed = jnp.zeros((count, width), f32)
    for head in range(heads):
        mask = head_mask(width, head_dim, head)
        row = jnp.broadcast_to(by_offset[head : head + 1, :], (count, span))
        bias = pltpu.roll(row, span - (count - 1), 1, stride=1, stride_axis=0)[:, :seq_tokens]
        own = jnp.where(mask, queries[...], jnp.zeros((), bf16))
        scores = mm(own, keys[...], cols_cols) + bias
        scores = jnp.where(live, scores, masked_score)
        raised = jnp.exp(scores - jnp.max(scores, axis=-1, keepdims=True))
        part = (raised * (1.0 / jnp.sum(raised, axis=-1, keepdims=True))).astype(bf16)
        probs[head] = part
        mixed = jnp.where(mask, mm(part, values[...]), mixed)
    attended[...] = mixed.astype(bf16)


def gelu(value):
    inner = np.float32(np.sqrt(2 / np.pi)) * (value + 0.044715 * (value * value * value))
    return 0.5 * value * (1.0 + jnp.tanh(inner))


def gelu_both(value):
    root = np.float32(np.sqrt(2 / np.pi))
    square = value * value
    tanh = jnp.tanh(root * value * (1.0 + 0.044715 * square))
    half = 0.5 * (1.0 + tanh)
    slope = half + 0.5 * value * (1.0 - tanh * tanh) * root * (1.0 + 3 * 0.044715 * square)
    return (value * half, slope)


def feed_kernel(ways, *refs):
    attended = refs[:ways]
    out_weight = refs[ways : 2 * ways]
    tokens, gain, gate_weight, up_weight, down_weight, out_grad = refs[2 * ways : 2 * ways + 6]
    middle, normed, inner, grad_gate, grad_up = refs[2 * ways + 6 : 2 * ways + 11]
    pieces = refs[2 * ways + 11 : 3 * ways + 11]
    whole_part = refs[3 * ways + 11]
    count = middle.shape[0]
    branch = sum(mm(a[...], w[...]) for a, w in zip(attended, out_weight))
    total = tokens[...].astype(f32) + branch
    middle[...] = total
    scale = lax.rsqrt(jnp.mean(total * total, axis=-1, keepdims=True) + epsilon)
    normed[...] = (total * scale * as_row(gain)).astype(bf16)
    gate = mm(normed[...], gate_weight[...])
    upward = mm(normed[...], up_weight[...])
    grad_inner = mm(out_grad[lax.axis_index("section")], down_weight[...], cols_cols)
    active, slope = gelu_both(gate)
    inner[...] = (active * upward).astype(bf16)
    grad_gate[...] = (grad_inner * upward * slope).astype(bf16)
    grad_up[...] = (grad_inner * active).astype(bf16)
    whole_part[...] = mm(grad_gate[...], gate_weight[...], cols_cols) + mm(
        grad_up[...], up_weight[...], cols_cols
    )
    deal(whole_part, pieces)


def deal(source, pieces):
    piece = pieces[0].shape[0]
    for k, out in enumerate(pieces):
        at = pl.multiple_of((lax.axis_index("tensor") ^ k) * piece, piece)
        out[...] = source[pl.ds(at, piece), :].astype(bf16)


def collect(pieces, target):
    piece = pieces[0].shape[0]
    for k, item in enumerate(pieces):
        at = pl.multiple_of((lax.axis_index("tensor") ^ k) * piece, piece)
        target[pl.ds(at, piece), :] = item[...].astype(target.dtype)


def feed_grad_kernel(ways, chunks, inner, normed, grad_gate, grad_up, out_grad, down_weight, *refs):
    sums, pieces = (refs[: 2 * chunks], refs[2 * chunks : 2 * chunks + ways])
    whole_part, stack = refs[2 * chunks + ways :]
    first = 0
    for left, right in (
        (normed, grad_gate[...]),
        (normed, grad_up[...]),
        (inner, out_grad[lax.axis_index("section")]),
    ):
        product = mm(left[...], right, rows_rows)
        rows, columns = product.shape
        for at in range(0, columns, 256):
            stack[first : first + rows, :] = product[:, at : at + 256].astype(bf16)
            first += rows
    section = lax.axis_index("section")
    half = first // (2 * chunks)
    for chunk in range(chunks):
        for side, out in enumerate(sums[2 * chunk : 2 * chunk + 2]):
            at = (2 * chunk + (section ^ side)) * half
            out[...] = stack[pl.ds(pl.multiple_of(at, half), half), :]
    whole_part[...] = mm(inner[...], down_weight[...])
    deal(whole_part, pieces)


def middle_kernel(ways, *refs):
    pieces = refs[:ways]
    middle, out_grad, gain, grad_branch, grad_middle, grad_gain = refs[ways:]
    piece = pieces[0].shape[0]
    at = pl.multiple_of(lax.axis_index("tensor") * piece, piece)
    grad_normed = sum(item[...].astype(f32) for item in pieces)
    own = middle[pl.ds(at, piece), :]
    scale = lax.rsqrt(jnp.mean(own * own, axis=-1, keepdims=True) + epsilon)
    grad_gain[...] = jnp.sum(grad_normed * own * scale, axis=0, keepdims=True)
    through = grad_normed * as_row(gain)
    total = (
        out_grad[lax.axis_index("section"), pl.ds(at, piece), :].astype(f32)
        + scale * through
        - own * (scale * scale * scale) * jnp.mean(through * own, axis=-1, keepdims=True)
    )
    grad_middle[...] = total
    grad_branch[...] = total.astype(bf16)


def attend_back_kernel(heads, ways, *refs):
    branches = refs[:ways]
    attended, probs, queries, keys, values, normed, out_weight = refs[ways : ways + 7]
    keep, send, rel_grad, grad_queries, grad_keys, grad_values = refs[ways + 7 : ways + 13]
    branch, stack = refs[ways + 13 :]
    count, width = queries.shape
    seq_tokens = keys.shape[0]
    head_dim = width // heads
    collect(branches, branch)
    query_first = pl.multiple_of(lax.axis_index("seq") * count, count)
    grad_attended = mm(branch[...], out_weight[...], cols_cols).astype(bf16)
    stack[3 * width :, :] = mm(attended[...], branch[...], rows_rows).astype(bf16)
    span = seq_tokens + count
    flip = (iota((count, count), 0) + iota((count, count), 1) == count - 1).astype(bf16)
    zero = jnp.zeros((), bf16)
    by_offset = []
    query_sum = jnp.zeros((count, width), f32)
    key_sum = jnp.zeros((seq_tokens, width), f32)
    value_sum = jnp.zeros((seq_tokens, width), f32)
    for head in range(heads):
        mask = head_mask(width, head_dim, head)
        own = jnp.where(mask, grad_attended, zero)
        grad_probs = mm(own, values[...], cols_cols)
        part = probs[head].astype(f32)
        inside = jnp.sum(part * grad_probs, axis=-1, keepdims=True)
        grad_scores = (part * (grad_probs - inside)).astype(bf16)
        flipped = jnp.concatenate(
            [mm(flip, grad_scores), jnp.zeros((count, count), f32)], axis=1
        )
        by_offset.append(
            jnp.sum(pltpu.roll(flipped, 0, 1, stride=1, stride_axis=0), axis=0, keepdims=True)
        )
        query_sum = jnp.where(mask, mm(grad_scores, keys[...]), query_sum)
        key_sum = key_sum + mm(
            grad_scores, jnp.where(mask, queries[...], zero), rows_rows
        )
        value_sum = value_sum + mm(probs[head], own, rows_rows)
    by_offset = jnp.concatenate(by_offset + [jnp.zeros((8 - heads, span), f32)], axis=0)
    hot = bucket_hot(128, span, query_first, count)
    rel_grad[...] = exact(by_offset, hot, cols_cols)
    query_sum = query_sum.astype(bf16)
    stack[0:width, :] = mm(
        query_sum, normed[pl.ds(query_first, count), :], rows_rows
    ).astype(bf16)
    grad_queries[...] = jnp.zeros(grad_queries.shape, bf16)
    grad_queries[pl.ds(query_first, count), :] = query_sum
    rest = grad_keys.shape[0] - seq_tokens
    for at, (total, place) in enumerate(((key_sum, grad_keys), (value_sum, grad_values))):
        total = total.astype(bf16)
        place[0:seq_tokens, :] = total
        place[seq_tokens:, :] = jnp.zeros((rest, width), bf16)
        stack[(at + 1) * width : (at + 2) * width, :] = mm(
            total, normed[...], rows_rows
        ).astype(bf16)
    half = keep.shape[0]
    section = lax.axis_index("section")
    keep[...] = stack[pl.ds(pl.multiple_of(section * half, half), half), :]
    send[...] = stack[pl.ds(pl.multiple_of((1 - section) * half, half), half), :]


def normed_back_kernel(
    steps,
    seq_tokens,
    ways,
    grad_queries,
    grad_keys,
    grad_values,
    tokens,
    query_weight,
    key_weight,
    value_weight,
    gain,
    grad_middle,
    grad_tokens,
    grad_gain,
    whole_part,
):
    token_rows, width = tokens.shape
    step = pl.program_id(0) if steps > 1 else 0
    whole_part[...] = (
        mm(grad_queries[...], query_weight[...])
        + mm(grad_keys[...], key_weight[...])
        + mm(grad_values[...], value_weight[...])
    )
    scale_row = as_row(gain)
    block = 32

    def one(part, total):
        own = pl.ds(pl.multiple_of(part * block, block), block)
        place = token_rows * step + part * block + iota((block, 1), 0)
        hidden = jnp.where(place < seq_tokens, tokens[own, :].astype(f32), 0.0)
        grad_normed = whole_part[own, :]
        scale = lax.rsqrt(jnp.mean(hidden * hidden, axis=-1, keepdims=True) + epsilon)
        against = grad_normed * hidden
        total = total + jnp.sum((against * scale).reshape(block // 8, 8, width), axis=0)
        inner = jnp.mean(against * scale_row, axis=-1, keepdims=True)
        result = scale * (grad_normed * scale_row) - hidden * (scale * scale * scale * inner)
        for at in range(width // 128):
            grad_tokens[at, own, :] = result[:, at * 128 : (at + 1) * 128]
        return total

    total = jnp.zeros((8, width), f32)
    total = lax.fori_loop(0, token_rows // block, one, total, unroll=11)
    total = jnp.sum(total, axis=0, keepdims=True)
    if steps > 1:
        total = total + jnp.where(step == 0, 0.0, grad_gain[0:1, :])
    grad_gain[0:1, :] = total
    piece = grad_middle.shape[0]
    own_first = (lax.axis_index("seq") * ways + lax.axis_index("tensor")) * piece
    own_first = own_first - token_rows * step
    for part in range(piece // block):
        begin = own_first + part * block

        @pl.when((begin >= 0) & (begin < token_rows))
        def _():
            place = pl.ds(pl.multiple_of(begin, block), block)
            rows = grad_middle[part * block : (part + 1) * block, :]
            for at in range(width // 128):
                grad_tokens[at, place, :] += rows[:, at * 128 : (at + 1) * 128]


def gbst_back_kernel(
    total_bytes,
    steps,
    grad_tokens,
    grad_gain_first,
    grad_gain_second,
    rel_grad,
    mixing,
    coefficients,
    size_weights,
    ids,
    pool,
    spread,
    total,
    embedding,
    conv_weight,
    conv_bias,
    score_weight,
    keep,
    send,
    hot,
    by_byte,
    by_score,
    small,
    packed,
    table,
    phased,
    against,
    found,
):
    rows = ids.shape[0]
    vocab, width = embedding.shape
    step = pl.program_id(0) if steps > 1 else 0
    first = step * rows
    score = as_row(score_weight)
    bias = as_row(conv_bias)

    def at_step(wanted):
        return pl.when(step == wanted) if steps > 1 else lambda run: run()

    @at_step(0)
    def _():
        by_score[...] = jnp.zeros(by_score.shape, f32)
        small[...] = jnp.zeros(small.shape, f32)
        fill_table(embedding, conv_weight, table)

    row_total = split_mm(coefficients[...], total)
    lane = iota((rows, 128), 1)
    on_bias = []
    bias_grad = jnp.zeros((1, width), f32)
    for j in range(pairs):
        grad_rows = jnp.concatenate(
            [grad_tokens[at, pl.ds(j, rows, stride=pairs), :] for at in range(width // 128)],
            axis=1,
        )
        narrow = grad_rows.astype(bf16)
        phased[j * rows : (j + 1) * rows, :] = narrow
        bias_grad = bias_grad + jnp.sum(row_total[:, j : j + 1] * grad_rows, axis=0, keepdims=True)
        on_bias.append(jnp.sum(grad_rows * bias, axis=1, keepdims=True))
    against[...] = mm(phased[...], table[...], cols_cols)
    fill_hot(ids, hot, vocab)
    product = mm(mixing[...].reshape(pairs * rows, taps * vocab), phased[...], rows_rows)
    if steps > 1:
        by_byte[...] = product + jnp.where(step == 0, 0.0, by_byte[...])
    else:
        by_byte[...] = product

    def pick(part, carry):
        own = pl.ds(pl.multiple_of(part * 16, 16), 16)
        spot = iota((16, 128), 1)
        result = jnp.zeros((16, 128), f32)
        for j in range(pairs):
            for r in reached(j):
                begin = pl.ds(pl.multiple_of(j * rows + part * 16, 16), 16)
                picked = sum(
                    hot[r + tap, own, :].astype(f32)
                    * against[begin, tap * vocab : (tap + 1) * vocab]
                    for tap in range(taps)
                )
                result = jnp.where(
                    spot == period * j + r, jnp.sum(picked, axis=1, keepdims=True), result
                )
        found[own, :] = result
        return carry

    lax.fori_loop(0, rows // 16, pick, 0, unroll=True)
    grad_coefficients = found[...]
    for j in range(pairs):
        grad_coefficients = grad_coefficients + jnp.where(lane // period == j, on_bias[j], 0.0)
    grad_coefficients = jnp.where(
        coefficient_inside(rows, first, total_bytes), grad_coefficients, 0.0
    )
    grad_sizes = lanes(split_mm(grad_coefficients, spread, cols_cols), 4)
    grad_sizes = [item * (0.5 / (size + 1)) for size, item in enumerate(grad_sizes)]
    mean_grad = sum(size_weights[size] * grad_sizes[size] for size in range(4))
    by_size = [size_weights[size] * (grad_sizes[size] - mean_grad) for size in range(4)]
    pooled = [item * (1.0 / (size + 2)) for size, item in enumerate(by_size[1:])]
    grad_scores = by_size[0] + split_mm(jnp.concatenate(pooled, axis=1), pool, cols_cols)
    grad_scores = jnp.where(position_inside(rows, first, total_bytes), grad_scores, 0.0)
    score_sum = jnp.sum(jnp.sum(grad_scores, axis=1, keepdims=True), axis=0, keepdims=True)
    small[1:2, :] += bias_grad + score_sum * score
    small[2:3, :] += score_sum * bias
    shifted = []
    for r in range(columns):
        item = pltpu.roll(grad_scores, 128 - r, 1) if r else grad_scores
        shifted.append(jnp.where(lane < taps, item, 0.0).astype(bf16))
    shifted = jnp.concatenate(shifted, axis=0)
    by_score[...] += mm(hot[...].reshape(columns * rows, vocab), shifted, rows_rows)

    @at_step(steps - 1)
    def _():
        emb = embedding[...].astype(f32)
        conv = conv_weight[...].astype(f32)
        grad_embedding = jnp.zeros((vocab, width), f32)
        grad_score = small[2:3, :]
        bytes_score = mm(by_score[...].astype(bf16), embedding[...], rows_rows)
        conv_rows = []
        for tap in range(taps):
            at = taps - 1 - tap
            here = by_byte[tap * vocab : (tap + 1) * vocab, :] + by_score[:, at : at + 1] * score
            grad_embedding = grad_embedding + conv[tap : tap + 1] * here
            conv_rows.append(jnp.sum(emb * here, axis=0, keepdims=True))
            grad_score = grad_score + conv[tap : tap + 1] * bytes_score[at : at + 1, :]
        rest = packed.shape[0] - vocab
        tail = conv_rows + [small[1:2, :], grad_score]
        tail += [grad_gain_first[0:1, :], grad_gain_second[0:1, :]]
        copies = jnp.concatenate([rel_grad[...]] * (width // 128), axis=1)
        own = iota(copies.shape, 1) // 128 == lax.axis_index("tensor")
        tail.append(jnp.where(own, copies, 0.0))
        used = sum(item.shape[0] for item in tail)
        tail = jnp.concatenate(tail + [jnp.zeros((rest - used, width), f32)], axis=0)
        packed[0:vocab, :] = grad_embedding.astype(bf16)
        packed[vocab:, :] = tail.astype(bf16)
        section = lax.axis_index("section")
        half = keep.shape[0]
        for side, out in enumerate((keep, send)):
            out[...] = packed[pl.ds(pl.multiple_of((section ^ side) * half, half), half), :]


def deal_kernel(keep, other, *refs):
    pieces, whole_part = (refs[:-1], refs[-1])
    whole_part[...] = keep[...].astype(f32) + other[...].astype(f32)
    deal(whole_part, pieces)


def copied_out(value):
    return [value] + [exchange(value, "tensor", k) for k in range(1, lax.axis_size("tensor"))]


def spread_out(pieces):
    return [pieces[0]] + [exchange(pieces[k], "tensor", k) for k in range(1, len(pieces))]


def seq_masks():
    return [1 << bit for bit in range(lax.axis_size("seq").bit_length() - 1)]


def merged(items):
    return sum(item.astype(f32) for item in items).astype(bf16)


def half_of(item, bit):
    half = item.shape[0] // 2
    return jnp.where(bit, item[half:], item[:half])


def even(rows):
    return rows % 32 == 0


def sum_over(items, axis, mask, halved):
    if not even(items[0].shape[0]):
        part = merged(items)
        return [part, exchange(part, axis, mask)]
    bit = (lax.axis_index(axis) & mask) != 0
    sent = merged([half_of(item, jnp.logical_not(bit)) for item in items])
    halved.append(mask)
    return [half_of(item, bit) for item in items] + [exchange(sent, axis, mask)]


class Staged:
    def __init__(self, keep, send):
        self.items = [keep, exchange(send, "section", 1)]
        self.masks = seq_masks()
        self.halved = []
        self.sent = None

    def add(self):
        mask = self.masks[0]
        rows = self.items[0].shape[0]
        if even(rows):
            bit = (lax.axis_index("seq") & mask) != 0
            self.sent = merged([half_of(item, jnp.logical_not(bit)) for item in self.items])
            self.items = [half_of(item, bit) for item in self.items]
            self.halved.append(mask)
        else:
            self.sent = merged(self.items)
            self.items = [self.sent]

    def swap(self):
        self.items = self.items + [exchange(self.sent, "seq", self.masks.pop(0))]

    def before(self, value):
        self.sent, value = lax.optimization_barrier((self.sent, value))
        return value

    def received_before(self, value):
        self.items[-1], value = lax.optimization_barrier((self.items[-1], value))
        return value

    def finish(self):
        while self.masks:
            self.add()
            self.swap()
        return merged(self.items)


def gather_sum(total, halved):
    pieces = {0: total}
    for mask in reversed(halved):
        for at, item in list(pieces.items()):
            pieces[at ^ mask] = exchange(item, "seq", mask)
    names = list(pieces)
    pieces = [pieces[name] for name in names]
    return (pieces + [exchange(item, "section", 1) for item in pieces], names)


def place_of(halved, at, rows, index):
    first = 0
    size = rows
    for mask in halved:
        size = size // 2
        first = first + jnp.where(((index ^ at) & mask) != 0, size, 0)
    return first


def unstack(pieces, halved, names, chunks, stack):
    count = len(names)
    section, seq = (lax.axis_index("section"), lax.axis_index("seq"))
    rows = pieces[0].shape[0] // chunks
    half = rows * count
    for i, item in enumerate(pieces):
        side, at = divmod(i, count)
        place = place_of(halved, names[at], half, seq) + (section ^ side) * half
        for chunk in range(chunks):
            first = pl.multiple_of(place + 2 * half * chunk, 8)
            stack[pl.ds(first, rows), :] = item[chunk * rows : (chunk + 1) * rows, :].astype(f32)


def weights_kernel(halved, names, *refs):
    count = 2 * len(names)
    pieces, outs, stack = (refs[:count], refs[count:-1], refs[-1])
    unstack(pieces, halved, names, 1, stack)
    rows = outs[0].shape[0]
    for i, out in enumerate(outs):
        out[...] = stack[i * rows : (i + 1) * rows, :]


def feed_weights_kernel(halved, names, chunks, *refs):
    count = 2 * len(names)
    pieces, outs, stack = (refs[:count], refs[count:-1], refs[-1])
    unstack(pieces, halved, names, chunks, stack)
    first = 0
    for out in outs:
        rows, columns = out.shape
        for at in range(0, columns, 256):
            out[:, at : at + 256] = stack[first : first + rows, :]
            first += rows


def packed_kernel(ways, heads, *refs):
    pieces = refs[: 2 * ways]
    embedding, conv, bias, score, first, second, rel, stack = refs[2 * ways :]
    rows = pieces[0].shape[0]
    vocab, width = embedding.shape
    section, tensor = (lax.axis_index("section"), lax.axis_index("tensor"))
    for i, item in enumerate(pieces):
        side, k = divmod(i, ways)
        at = ((section ^ side) * ways + (tensor ^ k)) * rows
        stack[pl.ds(pl.multiple_of(at, rows), rows), :] = item[...].astype(f32)
    embedding[...] = stack[0:vocab, :]
    conv[...] = stack[vocab : vocab + taps, :]
    for i, out in enumerate((bias, score, first, second)):
        out[...] = stack[vocab + taps + i : vocab + taps + i + 1, :].reshape(width)
    at = vocab + taps + 4
    own = stack[at : at + heads, pl.ds(pl.multiple_of(tensor * 128, 128), 128)]
    rel[...] = own[:, : rel.shape[1]]


def encoded_kernel(ways, *refs):
    pieces, middle, out = (refs[:ways], refs[ways], refs[ways + 1])
    piece = out.shape[0]
    at = pl.multiple_of(lax.axis_index("tensor") * piece, piece)
    total = sum(item[...].astype(f32) for item in pieces)
    out[...] = (middle[pl.ds(at, piece), :] + total).astype(bf16)


def assemble_kernel(ways, *refs):
    collect(refs[:ways], refs[ways])


def exchange(value, axis, mask):
    size = lax.axis_size(axis)
    return lax.ppermute(value, axis, [(i, i ^ mask) for i in range(size)])


def shards(
    byte_ids,
    byte_lengths,
    embedding,
    conv_weight,
    conv_bias,
    score_weight,
    norm_first,
    query_weight,
    key_weight,
    value_weight,
    out_weight,
    rel_bias,
    norm_second,
    gate_weight,
    up_weight,
    down_weight,
    out_grad,
):
    group = byte_ids.shape[1]
    ways = lax.axis_size("tensor")
    total_bytes = group * lax.axis_size("seq")
    count = group // 2
    seq_tokens = total_bytes // 2
    heads = rel_bias.shape[1]
    width = query_weight.shape[1]
    vocab, model = embedding.shape
    units = gate_weight.shape[1]
    piece = count // ways
    query_weight, key_weight, value_weight, rel_bias = (
        item.T for item in (query_weight, key_weight, value_weight, rel_bias)
    )
    steps = -(-total_bytes // (period * chunk_rows))
    rows = steps * chunk_rows
    token_rows = rows * pairs
    chunk_tokens = chunk_rows * pairs

    near = seq_tokens <= 1024
    held = pltpu.VMEM if near else like
    far = pltpu.HBM if near else like
    place = functools.partial(call, near=near)
    table, score_table, bias_score = place(
        prepare_kernel,
        [held((taps * vocab, model), bf16), held((vocab, 128), bf16), held((8, 128), f32)],
        embedding,
        conv_weight,
        score_weight,
        conv_bias,
        specs=[distant] * 4,
        cost=2,
    )

    all_ids = [byte_ids] + [
        exchange(byte_ids, "seq", k) for k in range(1, lax.axis_size("seq"))
    ]
    all_ids[0], score_table = lax.optimization_barrier((all_ids[0], score_table))
    out_weights = copied_out(out_weight)
    pool, spread, total = (jnp.asarray(item, bf16) for item in pool_tables())
    def chunked(item, dims):
        if steps == 1:
            return distant
        at = next(i for i, (a, b) in enumerate(zip(item.shape, dims)) if a != b)
        return pl.BlockSpec(dims, lambda i: tuple(i if d == at else 0 for d in range(len(dims))))

    def chunks(item):
        dims = tuple(
            chunk_rows if d == rows else chunk_tokens if d == token_rows else d
            for d in item.shape
        )
        return chunked(item, dims)

    grid = None if steps == 1 else (steps,)
    gbst_out = [
        held((token_rows, model), bf16),
        far((token_rows, model), bf16),
        far((pairs, rows, taps * vocab), bf16),
        far((rows, 128), f32),
        far((4, rows, 128), f32),
        far((rows, 128), f32),
    ]
    near_tokens, tokens, mixing, coefficients, size_weights, ids = place(
        functools.partial(gbst_kernel, total_bytes, steps, len(all_ids)),
        gbst_out,
        byte_lengths,
        *all_ids,
        table,
        score_table,
        pool,
        spread,
        total,
        conv_bias,
        bias_score,
        specs=[scalars, distant]
        + [local] * (len(all_ids) - 1)
        + [local] * 2
        + [distant] * 4
        + [local],
        out_specs=[chunks(item) for item in gbst_out],
        scratch=[
            pltpu.VMEM((columns, chunk_rows, vocab), bf16),
            pltpu.VMEM((model // 128, chunk_tokens, 128), f32),
            pltpu.VMEM((8 * -(-(total_bytes // 128 + 4) // 8), 128), f32),
            pltpu.VMEM((chunk_rows, 128), bf16),
        ],
        grid=grid,
        cost=6,
    )

    normed, queries, keys, values, probs, attended, own_tokens = place(
        functools.partial(attend_kernel, heads),
        [
            far((seq_tokens, model), bf16),
            far((count, width), bf16),
            far((seq_tokens, width), bf16),
            far((seq_tokens, width), bf16),
            far((heads, count, seq_tokens), bf16),
            held((count, width), bf16),
            held((count, model), bf16),
        ],
        byte_lengths,
        near_tokens,
        norm_first,
        query_weight,
        key_weight,
        value_weight,
        rel_bias,
        specs=[scalars, local] + [whole] * 5,
        cost=4,
    )
    all_attended = copied_out(attended)

    middle, normed_second, inner, grad_gate, grad_up, *normed_parts = place(
        functools.partial(feed_kernel, ways),
        [
            held((count, model), f32),
            held((count, model), bf16),
            held((count, units), bf16),
            held((count, units), bf16),
            held((count, units), bf16),
        ]
        + [held((piece, model), bf16)] * ways,
        *all_attended,
        *out_weights,
        own_tokens,
        norm_second,
        gate_weight,
        up_weight,
        down_weight,
        out_grad,
        specs=[local] * ways + [distant] * ways + [local] + [whole] * 5,
        cost=3,
        scratch=[pltpu.VMEM((count, model), f32)],
    )
    normed_parts = spread_out(normed_parts)
    feed_rows = 3 * model * units // 256
    half = feed_rows // (2 * feed_chunks)
    feed_parts = place(
        functools.partial(feed_grad_kernel, ways, feed_chunks),
        [held((half, 256), bf16)] * (2 * feed_chunks) + [held((piece, model), bf16)] * ways,
        inner,
        normed_second,
        grad_gate,
        grad_up,
        out_grad,
        down_weight,
        specs=[local] * 4 + [whole] * 2,
        cost=1.6,
        scratch=[pltpu.VMEM((count, model), f32), pltpu.VMEM((feed_rows, 256), bf16)],
    )
    feed_parts, encoded = (feed_parts[: 2 * feed_chunks], list(feed_parts[2 * feed_chunks :]))
    normed_parts[0], encoded[0] = lax.optimization_barrier((normed_parts[0], encoded[0]))
    feed_sums = [Staged(*feed_parts[2 * i : 2 * i + 2]) for i in range(feed_chunks)]

    feed_sums[0].add()
    normed_parts[0] = feed_sums[0].before(normed_parts[0])
    feed_sums[0].swap()
    grad_branch, grad_middle, grad_gain_second = place(
        functools.partial(middle_kernel, ways),
        [held((piece, model), bf16), far((piece, model), f32), far((1, model), f32)],
        *normed_parts,
        middle,
        out_grad,
        norm_second,
        specs=[local] * (ways + 1) + [whole] * 2,
    )
    branches = copied_out(grad_branch)
    stack_rows = 4 * width
    weight_keep, weight_send, grad_rel, grad_queries, grad_keys, grad_values = place(
        functools.partial(attend_back_kernel, heads, ways),
        [held((stack_rows // 2, model), bf16)] * 2
        + [far((8, 128), f32)]
        + [far((token_rows, width), bf16)] * 3,
        *branches,
        attended,
        probs,
        queries,
        keys,
        values,
        normed,
        out_weight,
        specs=[local] * ways + [whole] * 7,
        cost=5.4,
        scratch=[pltpu.VMEM((count, model), bf16), pltpu.VMEM((stack_rows, model), bf16)],
    )
    grad_tokens_out = [held((model // 128, token_rows, 128), f32), held((8, model), f32)]
    per_tile = pl.BlockSpec((model // 128, chunk_tokens, 128), lambda i: (0, i, 0))
    grad_tokens, grad_gain_first = place(
        functools.partial(normed_back_kernel, steps, seq_tokens, ways),
        grad_tokens_out,
        grad_queries,
        grad_keys,
        grad_values,
        tokens,
        query_weight,
        key_weight,
        value_weight,
        norm_first,
        grad_middle,
        specs=[chunks(item) for item in (grad_queries, grad_keys, grad_values, tokens)]
        + [distant] * 5,
        out_specs=[whole if steps == 1 else per_tile, whole],
        scratch=[pltpu.VMEM((chunk_tokens, model), f32)],
        grid=grid,
        limit=20,
        cost=4,
    )
    grad_tokens = feed_sums[0].received_before(grad_tokens)
    feed_sums[0].add()
    feed_sums[0].swap()
    packed_rows = 32 * ways * -(-(vocab + taps + 12) // (32 * ways))
    quarter = packed_rows // (2 * ways)
    keep, send = place(
        functools.partial(gbst_back_kernel, total_bytes, steps),
        [held((packed_rows // 2, model), bf16)] * 2,
        grad_tokens,
        grad_gain_first,
        grad_gain_second,
        grad_rel,
        mixing,
        coefficients,
        size_weights,
        ids,
        pool,
        spread,
        total,
        embedding,
        conv_weight,
        conv_bias,
        score_weight,
        specs=[local if steps == 1 else per_tile, local if steps == 1 else whole]
        + [distant] * 2
        + [chunks(item) for item in (mixing, coefficients, size_weights, ids)]
        + [distant] * 7,
        scratch=[
            pltpu.VMEM((columns, chunk_rows, vocab), bf16),
            pltpu.VMEM((taps * vocab, model), f32),
            pltpu.VMEM((vocab, 128), f32),
            pltpu.VMEM((8, model), f32),
            pltpu.VMEM((packed_rows, model), bf16),
            pltpu.VMEM((taps * vocab, model), bf16),
            pltpu.VMEM((chunk_tokens, model), bf16),
            pltpu.VMEM((chunk_tokens, taps * vocab), f32),
            pltpu.VMEM((chunk_rows, 128), f32),
        ],
        grid=grid,
        limit=30,
        cost=12,
    )
    keep, weight_send, *encoded = lax.optimization_barrier((keep, weight_send, *encoded))
    keep = feed_sums[0].received_before(keep)
    weight_sum = Staged(weight_keep, weight_send)
    encoded = spread_out(encoded)
    (own_encoded,) = place(
        functools.partial(encoded_kernel, ways),
        [held((piece, model), bf16)],
        *encoded,
        middle,
        specs=[local] * (ways + 1),
    )
    parts = place(
        deal_kernel,
        [held((quarter, model), bf16)] * ways,
        keep,
        exchange(send, "section", 1),
        specs=[local] * 2,
        scratch=[pltpu.VMEM((packed_rows // 2, model), f32)],
    )
    items = spread_out(parts)
    for mask in seq_masks():
        part = merged(items)
        items = [part, exchange(part, "seq", mask)]
    part = merged(items)
    gathered = copied_out(part)
    gathered = gathered + [exchange(item, "section", 1) for item in gathered]
    grads = place(
        functools.partial(packed_kernel, ways, heads),
        [like((vocab, model), f32), like((taps, model), f32)]
        + [like((model,), f32)] * 4
        + [like((heads, rel_bias.shape[1]), f32)],
        *gathered,
        specs=[local] * len(gathered),
        scratch=[pltpu.VMEM((packed_rows, model), f32)],
    )
    grad_embedding, grad_conv, grad_bias, grad_score, grad_first, grad_second, grad_rel = grads

    (output,) = place(
        functools.partial(assemble_kernel, ways),
        [like((count, model), bf16)],
        *copied_out(own_encoded),
        specs=[local] * ways,
    )

    feed_total = feed_sums[0].finish()
    pieces, names = gather_sum(feed_total, feed_sums[0].halved)
    feed_grads = place(
        functools.partial(feed_weights_kernel, feed_sums[0].halved, names, feed_chunks),
        [like((model, units), f32), like((model, units), f32), like((units, model), f32)],
        *pieces,
        specs=[local] * len(pieces),
        scratch=[pltpu.VMEM((feed_rows, 256), f32)],
    )
    pieces, names = gather_sum(weight_sum.finish(), weight_sum.halved)
    weight_grads = place(
        functools.partial(weights_kernel, weight_sum.halved, names),
        [like((width, model), f32)] * 4,
        *pieces,
        specs=[local] * len(pieces),
        scratch=[pltpu.VMEM((stack_rows, model), f32)],
    )
    return (
        output[None],
        grad_embedding,
        grad_conv,
        grad_bias,
        grad_score,
        grad_first,
        *(item.T for item in weight_grads[:3]),
        weight_grads[3],
        grad_rel.T,
        grad_second,
        *feed_grads,
    )


def solution(mesh):
    return jax.shard_map(
        shards,
        mesh=mesh,
        in_specs=(
            P(None, "seq"),
            P(),
            P(),
            P(),
            P(),
            P(),
            P(),
            P(None, "tensor"),
            P(None, "tensor"),
            P(None, "tensor"),
            P("tensor", None),
            P(None, "tensor"),
            P(),
            P(None, "tensor"),
            P(None, "tensor"),
            P("tensor", None),
            P(None, "seq", None),
        ),
        out_specs=(
            P("section", "seq", None),
            P(),
            P(),
            P(),
            P(),
            P(),
            P(None, "tensor"),
            P(None, "tensor"),
            P(None, "tensor"),
            P("tensor", None),
            P(None, "tensor"),
            P(),
            P(None, "tensor"),
            P(None, "tensor"),
            P("tensor", None),
        ),
        check_vma=False,
    )
```

time: 373 us -> 164 us (0.44)
  waiting for transfers between devices: 221 us -> 51.4 us
  starting transfers between devices: 16.4 us -> 53.7 us
  blocking collectives: 28.1 us -> 0 us
  local copies, waits for them, and re-layouts: 24.6 us -> 1.62 us
  between operations: 13.9 us -> 1.08 us
  Pallas kernels: 58.8 us -> 51.8 us
  other arithmetic: 9.41 us -> 4 us
    psum x3 -> x0, waiting for transfers between devices: 202 us -> none  [the longest x1 110 us: shards(): packed = lax.psum(packed, ('section', 'tensor', 'seq')).astype(f32)]
    ppermute x12 -> x54, starting transfers between devices: 16.2 us -> 53.7 us  [exchange(): return lax.ppermute(value, axis, [(i, i ^ mask) for i in range(size)])]
    ppermute x12 -> x54, waiting for transfers between devices: 18.3 us -> 51.4 us  [exchange(): return lax.ppermute(value, axis, [(i, i ^ mask) for i in range(size)])]
    psum x1 -> x0, blocking collectives: 15.6 us -> none  [shards(): lax.psum((grad_query_weight, grad_key_weight, grad_value_weight, grad_out...]
    unnamed x60 -> x44, local copies, waits for them, and re-layouts: 14.7 us -> 1.62 us
    all_gather x1 -> x0, blocking collectives: 12.5 us -> none  [shards(): all_ids = lax.all_gather(own_ids, 'seq', axis=0, tiled=True)]
    pallas_call x8 -> x15, Pallas kernels: 58.8 us -> 51.8 us  [call(): pl.pallas_call(kernel, out_shape=out, in_specs=specs, out_specs=jax.tree....]
    broadcast_in_dim x4 -> x0, local copies, waits for them, and re-layouts: 4.37 us -> none  [shards(): item[None, :]]
  transfers between devices with their start and end apart: 15 -> 54, of which waited for: 10 -> 20; matrix products, arithmetic and copies ran while one was open for 6% -> 2% of each run, Pallas kernels for 13% -> 27%
where the time goes in v2:
time: 164 us
  starting transfers between devices  53.7 us (33%)
  Pallas kernels  51.8 us (32%)
  waiting for transfers between devices  51.4 us (31%)
  other arithmetic  4 us (2%)
    ppermute x54, starting transfers between devices, exchange(): return lax.ppermute(value, axis, [(i, i ^ mask) for i in range(size)])  53.7 us
    pallas_call x15, Pallas kernels, call(): pl.pallas_call(kernel, out_shape=out, in_specs=specs, out_specs=jax.tree....  51.8 us
    ppermute x54, waiting for transfers between devices, exchange(): return lax.ppermute(value, axis, [(i, i ^ mask) for i in range(size)])  51.4 us
  transfers between devices with their start and end apart: 54, of which 20 were waited for; matrix products, arithmetic and copies ran while one was open for 2% of the time, Pallas kernels for 27%

profile of v2, /device:TPU:0, one launch (start us, length us, event | category | flops | bytes accessed | tf_op | source)
XLA Modules:
  0.0 163.6 jit_solution(5822806861049133232)
XLA Ops:
  0.7 4.0 %collective-permute-start.8 = (bf16[192,768]{1,0:T(8,128)(2,1)}, bf16[192,768]{1,0:T(8,128)(2,1)S(1)}, u32[]{:S(2)}, u32[]{:S(2)}) collective-permute-start(bf16[192,768]{1,0:T(8,128)(2,1)} %refs_10_.3), channel_id=1, source_target_pairs={{0,12},{4,8},{8,4},{12,0},{1,13},{5,9},{9,5},{13,1},{2,14},{6,10},... | collective-permute-start | bytes 884744 | tf_op jit(solution)/shard_map/ppermute | solution.py:844
  7.3 2.5 %collective-permute-start.2 = (s32[2,512]{1,0:T(2,128)}, s32[2,512]{1,0:T(2,128)S(1)}, u32[]{:S(2)}, u32[]{:S(2)}) collective-permute-start(s32[2,512]{1,0:T(2,128)} %refs_0_), channel_id=1, source_target_pairs={{0,3},{1,2},{2,1},{3,0},{4,7},{5,6},{6,5},{7,4},{8,11},{9,10},{10,... | collective-permute-start | bytes 12296 | tf_op jit(solution)/shard_map/ppermute | solution.py:844
  9.8 2.4 %collective-permute-start.1 = (s32[2,512]{1,0:T(2,128)}, s32[2,512]{1,0:T(2,128)S(1)}, u32[]{:S(2)}, u32[]{:S(2)}) collective-permute-start(s32[2,512]{1,0:T(2,128)} %refs_0_), channel_id=1, source_target_pairs={{0,2},{1,3},{2,0},{3,1},{4,6},{5,7},{6,4},{7,5},{8,10},{9,11},{10,... | collective-permute-start | bytes 12296 | tf_op jit(solution)/shard_map/ppermute | solution.py:844
  15.1 8.2 %shard_map.308 = (bf16[1056,768]{1,0:T(8,128)(2,1)S(1)}, bf16[1056,768]{1,0:T(8,128)(2,1)}, bf16[6,176,1280]{2,1,0:T(8,128)(2,1)}, f32[176,128]{1,0:T(8,128)}, f...) custom-call(s32[2]{0:T(128)S(1)} %copy-done.15, s32[2,512]{1,0:T(2,128)} %refs_0_, s32[2,512]{1,0:T(2,128)S(1)} %collective-permute-done.refs_1_, ...), custom_call_target="tpu_custom_call" | custom-call | flops 6000000 | bytes 18000 | tf_op jit(solution)/shard_map/pallas_call | solution.py:86
  23.4 5.3 %shard_map.309 = (bf16[1024,768]{1,0:T(8,128)(2,1)}, bf16[256,192]{1,0:T(8,128)(2,1)}, bf16[1024,192]{1,0:T(8,128)(2,1)}, bf16[1024,192]{1,0:T(8,128)(2,1)}, bf1...) custom-call(s32[2]{0:T(128)S(1)} %copy-done.15, ...), custom_call_target="tpu_custom_call" | custom-call | flops 4000000 | bytes 12000 | tf_op jit(solution)/shard_map/pallas_call | solution.py:86
  28.7 2.4 %collective-permute-start.5 = (bf16[256,192]{1,0:T(8,128)(2,1)S(1)}, bf16[256,192]{1,0:T(8,128)(2,1)S(1)}, u32[]{:S(2)}, u32[]{:S(2)}) collective-permute-start(bf16[256,192]{1,0:T(8,128)(2,1)S(1)} %get-tuple-element.99.refs_0_.refs_4_), channel_id=1, source_target_pairs={{0,12},{4,8},{8,4},{12,0},{1,13},{5,9},{9,5},{13,1},{2,14},{6,10},... | collective-permute-start | bytes 294920 | tf_op jit(solution)/shard_map/ppermute | solution.py:844
  31.7 3.0 %collective-permute-done.5.refs_3_ = bf16[256,192]{1,0:T(8,128)(2,1)S(1)} collective-permute-done((bf16[256,192]{1,0:T(8,128)(2,1)S(1)}, bf16[256,192]{1,0:T(8,128)(2,1)S(1)}, u32[]{:S(2)}, u32[]{:S(2)}) %collective-permute-start.5) | collective-permute-done | bytes 98336 | tf_op jit(solution)/shard_map/ppermute | solution.py:844
  36.2 3.5 %collective-permute-done.3.refs_1_ = bf16[256,192]{1,0:T(8,128)(2,1)S(1)} collective-permute-done((bf16[256,192]{1,0:T(8,128)(2,1)S(1)}, bf16[256,192]{1,0:T(8,128)(2,1)S(1)}, u32[]{:S(2)}, u32[]{:S(2)}) %collective-permute-start.3) | collective-permute-done | bytes 98336 | tf_op jit(solution)/shard_map/ppermute | solution.py:844
  40.6 3.6 %shard_map.310 = (f32[256,768]{1,0:T(8,128)S(1)}, bf16[256,768]{1,0:T(8,128)(2,1)S(1)}, bf16[256,512]{1,0:T(8,128)(2,1)S(1)}, bf16[256,512]{1,0:T(8,128)(2,1)S(1...) custom-call(bf16[256,192]{1,0:T(8,128)(2,1)S(1)} %get-tuple-element., ...), custom_call_target="tpu_custom_call" | custom-call | flops 3000000 | bytes 9000 | tf_op jit(solution)/shard_map/pallas_call | solution.py:86
  44.2 2.7 %shard_map.311 = (bf16[2304,256]{1,0:T(8,128)(2,1)S(1)}, bf16[2304,256]{1,0:T(8,128)(2,1)}, bf16[64,768]{1,0:T(8,128)(2,1)S(1)}, bf16[64,768]{1,0:T(8,128)(2,1)S...) custom-call(bf16[256,512]{1,0:T(8,128)(2,1)S(1)} %get-tuple-element.101.inner, ...), custom_call_target="tpu_custom_call" | custom-call | flops 1600000 | bytes 4800 | tf_op jit(solution)/shard_map/pallas_call | solution.py:86
  48.5 2.4 %collective-permute-start.12 = (bf16[64,768]{1,0:T(8,128)(2,1)}, bf16[64,768]{1,0:T(8,128)(2,1)S(1)}, u32[]{:S(2)}, u32[]{:S(2)}) collective-permute-start(bf16[64,768]{1,0:T(8,128)(2,1)} %copy-done.17), channel_id=1, source_target_pairs={{0,8},{4,12},{8,0},{12,4},{1,9},{5,13},{9,1},{13,5},{2,10},{6,14},... | collective-permute-start | bytes 294920 | tf_op jit(solution)/shard_map/ppermute | solution.py:844
  65.0 6.0 %shard_map.313 = (bf16[384,768]{1,0:T(8,128)(2,1)S(1)}, bf16[384,768]{1,0:T(8,128)(2,1)S(1)}, f32[8,128]{1,0:T(8,128)}, bf16[1056,192]{1,0:T(8,128)(2,1)}, bf16[...) custom-call(bf16[64,768]{1,0:T(8,128)(2,1)S(1)} %get-tuple-element.116.refs_0_, ...), custom_call_target="tpu_custom_call" | custom-call | flops 5400000 | bytes 16200 | tf_op jit(solution)/shard_map/pallas_call | solution.py:86
  71.0 5.5 %shard_map.314 = (f32[6,1056,128]{2,1,0:T(8,128)S(1)}, f32[8,768]{1,0:T(8,128)S(1)}) custom-call(bf16[1056,192]{1,0:T(8,128)(2,1)} %get-tuple-element.122.grad_queries, bf16[1056,192]{1,0:T(8,128)(2,1)} %get-tuple-element.123.grad_keys, bf16[1056,192]{1,0:T(8,128)(2,1)} %get-tuple-element.124.grad_values, bf16[1056,768]{1,0:T(8,128)(2,1)} %get-tuple-element.125.tokens, ...), custom_call_target="tpu_custom_call" | custom-call | flops 4000000 | bytes 12000 | tf_op jit(solution)/shard_map/pallas_call | solution.py:86
  76.8 2.6 %collective-permute-start.23 = (bf16[576,256]{1,0:T(8,128)(2,1)S(1)}, bf16[576,256]{1,0:T(8,128)(2,1)S(1)}, u32[]{:S(2)}, u32[]{:S(2)}) collective-permute-start(bf16[576,256]{1,0:T(8,128)(2,1)S(1)} %add_convert_fusion.3), channel_id=1, source_target_pairs={{0,2},{1,3},{2,0},{3,1},{4,6},{5,7},{6,4},{7,5},{8,10},{9,11},{10,... | collective-permute-start | bytes 884744 | tf_op jit(solution)/shard_map/ppermute | solution.py:844
  79.4 11.5 %shard_map.315 = (bf16[192,768]{1,0:T(8,128)(2,1)S(1)}, bf16[192,768]{1,0:T(8,128)(2,1)S(1)}) custom-call(f32[6,1056,128]{2,1,0:T(8,128)S(1)} %get-tuple-element.128.grad_tokens, f32[8,768]{1,0:T(8,128)S(1)} %get-tuple-element.129.grad_gain_first, f32[1,768]{1,0:T(1,128)} %get-tuple-element.130.grad_gain_second, f32[8,128]{1,0:T(8,128)} %get-tuple-element.131.rel_grad, ...), custom_call_target="tpu_custom_call" | custom-call | flops 12000000 | bytes 36000 | tf_op jit(solution)/shard_map/pallas_call | solution.py:86
  105.5 2.4 %collective-permute-done.28 = bf16[48,768]{1,0:T(8,128)(2,1)S(1)} collective-permute-done((bf16[48,768]{1,0:T(8,128)(2,1)S(1)}, bf16[48,768]{1,0:T(8,128)(2,1)S(1)}, u32[]{:S(2)}, u32[]{:S(2)}) %collective-permute-start.28) | collective-permute-done | bytes 73760 | tf_op jit(solution)/shard_map/ppermute | solution.py:844
  110.5 2.9 %collective-permute-done.29 = bf16[48,768]{1,0:T(8,128)(2,1)S(1)} collective-permute-done((bf16[48,768]{1,0:T(8,128)(2,1)S(1)}, bf16[48,768]{1,0:T(8,128)(2,1)S(1)}, u32[]{:S(2)}, u32[]{:S(2)}) %collective-permute-start.29) | collective-permute-done | bytes 73760 | tf_op jit(solution)/shard_map/ppermute | solution.py:844
  119.4 2.9 %collective-permute-done.32.refs_3_ = bf16[48,768]{1,0:T(8,128)(2,1)S(1)} collective-permute-done((bf16[48,768]{1,0:T(8,128)(2,1)S(1)}, bf16[48,768]{1,0:T(8,128)(2,1)S(1)}, u32[]{:S(2)}, u32[]{:S(2)}) %collective-permute-start.32) | collective-permute-done | bytes 73760 | tf_op jit(solution)/shard_map/ppermute | solution.py:844
  125.3 3.5 %collective-permute-done.30.refs_1_ = bf16[48,768]{1,0:T(8,128)(2,1)S(1)} collective-permute-done((bf16[48,768]{1,0:T(8,128)(2,1)S(1)}, bf16[48,768]{1,0:T(8,128)(2,1)S(1)}, u32[]{:S(2)}, u32[]{:S(2)}) %collective-permute-start.30) | collective-permute-done | bytes 73760 | tf_op jit(solution)/shard_map/ppermute | solution.py:844
  129.4 7.1 %collective-permute-done.47.refs_1_ = bf16[576,256]{1,0:T(8,128)(2,1)S(1)} collective-permute-done((bf16[576,256]{1,0:T(8,128)(2,1)S(1)}, bf16[576,256]{1,0:T(8,128)(2,1)S(1)}, u32[]{:S(2)}, u32[]{:S(2)}) %collective-permute-start.47) | collective-permute-done | bytes 294944 | tf_op jit(solution)/shard_map/ppermute | solution.py:844
  139.3 8.8 %collective-permute-done.49.refs_3_ = bf16[576,256]{1,0:T(8,128)(2,1)S(1)} collective-permute-done((bf16[576,256]{1,0:T(8,128)(2,1)S(1)}, bf16[576,256]{1,0:T(8,128)(2,1)S(1)}, u32[]{:S(2)}, u32[]{:S(2)}) %collective-permute-start.49) | collective-permute-done | bytes 294944 | tf_op jit(solution)/shard_map/ppermute | solution.py:844
  150.7 4.1 %collective-permute-done.41.refs_2_ = bf16[96,768]{1,0:T(8,128)(2,1)S(1)} collective-permute-done((bf16[96,768]{1,0:T(8,128)(2,1)S(1)}, bf16[96,768]{1,0:T(8,128)(2,1)S(1)}, u32[]{:S(2)}, u32[]{:S(2)}) %collective-permute-start.41) | collective-permute-done | bytes 147488 | tf_op jit(solution)/shard_map/ppermute | solution.py:844
  154.8 2.8 %collective-permute-done.42.refs_3_ = bf16[96,768]{1,0:T(8,128)(2,1)S(1)} collective-permute-done((bf16[96,768]{1,0:T(8,128)(2,1)S(1)}, bf16[96,768]{1,0:T(8,128)(2,1)S(1)}, u32[]{:S(2)}, u32[]{:S(2)}) %collective-permute-start.42) | collective-permute-done | bytes 147488 | tf_op jit(solution)/shard_map/ppermute | solution.py:844
  159.4 2.6 %shard_map.321 = (f32[768,512]{1,0:T(8,128)}, f32[768,512]{1,0:T(8,128)}, f32[512,768]{1,0:T(8,128)}) custom-call(bf16[576,256]{1,0:T(8,128)(2,1)S(1)} %add_convert_fusion.1.refs_0_, bf16[576,256]{1,0:T(8,128)(2,1)S(1)} %collective-permute-done.47.refs_1_, bf16[576,256]{1,0:T(8,128)(2,1)S(1)} %collective-permute-done.48.refs_2_, ...), custom_call_target="tpu_custom_call" | custom-call | flops 1000000 | bytes 3000 | tf_op jit(solution)/shard_map/pallas_call | solution.py:86
  (156 shorter events, 59.9 us)
Async XLA Ops:
  0.7 39.0 %collective-permute-start.8 = (bf16[192,768]{1,0:T(8,128)(2,1)}, bf16[192,768]{1,0:T(8,128)(2,1)S(1)}, u32[]{:S(2)}, u32[]{:S(2)}) collective-permute-start(bf16[192,768]{1,0:T(8,128)(2,1)} %refs_10_.3), channel_id=1, source_target_pairs={{0,12},{4,8},{8,4},{12,0},{1,13},{5,9},{9,5},{13,1},{2,14},{6,10},... | collective-permute-start | bytes 884744 | tf_op jit(solution)/shard_map/ppermute | solution.py:844
  4.7 35.0 %collective-permute-start.7 = (bf16[192,768]{1,0:T(8,128)(2,1)}, bf16[192,768]{1,0:T(8,128)(2,1)S(1)}, u32[]{:S(2)}, u32[]{:S(2)}) collective-permute-start(bf16[192,768]{1,0:T(8,128)(2,1)} %refs_10_.3), channel_id=1, source_target_pairs={{0,8},{4,12},{8,0},{12,4},{1,9},{5,13},{9,1},{13,5},{2,10},{6,14},... | collective-permute-start | bytes 884744 | tf_op jit(solution)/shard_map/ppermute | solution.py:844
  5.2 34.5 %collective-permute-start.6 = (bf16[192,768]{1,0:T(8,128)(2,1)}, bf16[192,768]{1,0:T(8,128)(2,1)S(1)}, u32[]{:S(2)}, u32[]{:S(2)}) collective-permute-start(bf16[192,768]{1,0:T(8,128)(2,1)} %refs_10_.3), channel_id=1, source_target_pairs={{0,4},{4,0},{8,12},{12,8},{1,5},{5,1},{9,13},{13,9},{2,6},{6,2},{1... | collective-permute-start | bytes 884744 | tf_op jit(solution)/shard_map/ppermute | solution.py:844
  52.6 24.0 %collective-permute-start.10 = (bf16[1152,256]{1,0:T(8,128)(2,1)S(1)}, bf16[1152,256]{1,0:T(8,128)(2,1)S(1)}, u32[]{:S(2)}, u32[]{:S(2)}) collective-permute-start(bf16[1152,256]{1,0:T(8,128)(2,1)S(1)} %add_convert_fusion), channel_id=1, source_target_pairs={{0,1},{1,0},{2,3},{3,2},{4,5},{5,4},{6,7},{7,6},{8,9},{9,8},{10,11... | collective-permute-start | bytes 1769480 | tf_op jit(solution)/shard_map/ppermute | solution.py:844
  76.8 17.8 %collective-permute-start.23 = (bf16[576,256]{1,0:T(8,128)(2,1)S(1)}, bf16[576,256]{1,0:T(8,128)(2,1)S(1)}, u32[]{:S(2)}, u32[]{:S(2)}) collective-permute-start(bf16[576,256]{1,0:T(8,128)(2,1)S(1)} %add_convert_fusion.3), channel_id=1, source_target_pairs={{0,2},{1,3},{2,0},{3,1},{4,6},{5,7},{6,4},{7,5},{8,10},{9,11},{10,... | collective-permute-start | bytes 884744 | tf_op jit(solution)/shard_map/ppermute | solution.py:844
  98.6 9.7 %collective-permute-start.37 = (bf16[384,768]{1,0:T(8,128)(2,1)S(1)}, bf16[384,768]{1,0:T(8,128)(2,1)S(1)}, u32[]{:S(2)}, u32[]{:S(2)}) collective-permute-start(bf16[384,768]{1,0:T(8,128)(2,1)S(1)} %get-tuple-element.160), channel_id=1, source_target_pairs={{0,16},{16,0},{1,17},{17,1},{2,18},{18,2},{3,19},{19,3},{4,20},{20... | collective-permute-start | bytes 1769480 | tf_op jit(solution)/shard_map/ppermute | solution.py:844
  99.9 13.6 %collective-permute-start.22 = (bf16[64,768]{1,0:T(8,128)(2,1)S(1)}, bf16[64,768]{1,0:T(8,128)(2,1)S(1)}, u32[]{:S(2)}, u32[]{:S(2)}) collective-permute-start(bf16[64,768]{1,0:T(8,128)(2,1)S(1)} %shard_map.316.refs_0_), channel_id=1, source_target_pairs={{0,12},{4,8},{8,4},{12,0},{1,13},{5,9},{9,5},{13,1},{2,14},{6,10},... | collective-permute-start | bytes 294920 | tf_op jit(solution)/shard_map/ppermute | solution.py:844
  101.3 12.8 %collective-permute-start.21 = (bf16[64,768]{1,0:T(8,128)(2,1)S(1)}, bf16[64,768]{1,0:T(8,128)(2,1)S(1)}, u32[]{:S(2)}, u32[]{:S(2)}) collective-permute-start(bf16[64,768]{1,0:T(8,128)(2,1)S(1)} %shard_map.316.refs_0_), channel_id=1, source_target_pairs={{0,8},{4,12},{8,0},{12,4},{1,9},{5,13},{9,1},{13,5},{2,10},{6,14},... | collective-permute-start | bytes 294920 | tf_op jit(solution)/shard_map/ppermute | solution.py:844
  102.3 13.9 %collective-permute-start.20 = (bf16[64,768]{1,0:T(8,128)(2,1)S(1)}, bf16[64,768]{1,0:T(8,128)(2,1)S(1)}, u32[]{:S(2)}, u32[]{:S(2)}) collective-permute-start(bf16[64,768]{1,0:T(8,128)(2,1)S(1)} %shard_map.316.refs_0_), channel_id=1, source_target_pairs={{0,4},{4,0},{8,12},{12,8},{1,5},{5,1},{9,13},{13,9},{2,6},{6,2},{1... | collective-permute-start | bytes 294920 | tf_op jit(solution)/shard_map/ppermute | solution.py:844
  108.5 9.9 %collective-permute-start.38 = (bf16[192,768]{1,0:T(8,128)(2,1)S(1)}, bf16[192,768]{1,0:T(8,128)(2,1)S(1)}, u32[]{:S(2)}, u32[]{:S(2)}) collective-permute-start(bf16[192,768]{1,0:T(8,128)(2,1)S(1)} %add_convert_fusion.2), channel_id=1, source_target_pairs={{0,1},{1,0},{2,3},{3,2},{4,5},{5,4},{6,7},{7,6},{8,9},{9,8},{10,11... | collective-permute-start | bytes 884744 | tf_op jit(solution)/shard_map/ppermute | solution.py:844
  113.5 15.4 %collective-permute-start.50 = (bf16[576,256]{1,0:T(8,128)(2,1)S(1)}, bf16[576,256]{1,0:T(8,128)(2,1)S(1)}, u32[]{:S(2)}, u32[]{:S(2)}) collective-permute-start(bf16[576,256]{1,0:T(8,128)(2,1)S(1)} %add_convert_fusion.1.refs_0_), channel_id=1, source_target_pairs={{0,16},{16,0},{1,17},{17,1},{2,18},{18,2},{3,19},{19,3},{4,20},{20... | collective-permute-start | bytes 884744 | tf_op jit(solution)/shard_map/ppermute | solution.py:844
  114.1 22.4 %collective-permute-start.48 = (bf16[576,256]{1,0:T(8,128)(2,1)S(1)}, bf16[576,256]{1,0:T(8,128)(2,1)S(1)}, u32[]{:S(2)}, u32[]{:S(2)}) collective-permute-start(bf16[576,256]{1,0:T(8,128)(2,1)S(1)} %add_convert_fusion.1.refs_0_), channel_id=1, source_target_pairs={{0,1},{1,0},{2,3},{3,2},{4,5},{5,4},{6,7},{7,6},{8,9},{9,8},{10,11... | collective-permute-start | bytes 884744 | tf_op jit(solution)/shard_map/ppermute | solution.py:844
  116.2 20.3 %collective-permute-start.47 = (bf16[576,256]{1,0:T(8,128)(2,1)S(1)}, bf16[576,256]{1,0:T(8,128)(2,1)S(1)}, u32[]{:S(2)}, u32[]{:S(2)}) collective-permute-start(bf16[576,256]{1,0:T(8,128)(2,1)S(1)} %add_convert_fusion.1.refs_0_), channel_id=1, source_target_pairs={{0,2},{1,3},{2,0},{3,1},{4,6},{5,7},{6,4},{7,5},{8,10},{9,11},{10,... | collective-permute-start | bytes 884744 | tf_op jit(solution)/shard_map/ppermute | solution.py:844
  122.3 16.2 %collective-permute-start.39 = (bf16[96,768]{1,0:T(8,128)(2,1)S(1)}, bf16[96,768]{1,0:T(8,128)(2,1)S(1)}, u32[]{:S(2)}, u32[]{:S(2)}) collective-permute-start(bf16[96,768]{1,0:T(8,128)(2,1)S(1)} %add_convert_fusion.5), channel_id=1, source_target_pairs={{0,2},{1,3},{2,0},{3,1},{4,6},{5,7},{6,4},{7,5},{8,10},{9,11},{10,... | collective-permute-start | bytes 442376 | tf_op jit(solution)/shard_map/ppermute | solution.py:844
  128.9 9.8 %collective-permute-start.36 = (bf16[48,768]{1,0:T(8,128)(2,1)S(1)}, bf16[48,768]{1,0:T(8,128)(2,1)S(1)}, u32[]{:S(2)}, u32[]{:S(2)}) collective-permute-start(bf16[48,768]{1,0:T(8,128)(2,1)S(1)} %collective-permute-done.32.refs_3_), channel_id=1, source_target_pairs={{0,16},{16,0},{1,17},{17,1},{2,18},{18,2},{3,19},{19,3},{4,20},{20... | collective-permute-start | bytes 221192 | tf_op jit(solution)/shard_map/ppermute | solution.py:844
  128.9 9.9 %collective-permute-start.35 = (bf16[48,768]{1,0:T(8,128)(2,1)S(1)}, bf16[48,768]{1,0:T(8,128)(2,1)S(1)}, u32[]{:S(2)}, u32[]{:S(2)}) collective-permute-start(bf16[48,768]{1,0:T(8,128)(2,1)S(1)} %collective-permute-done.31.refs_2_), channel_id=1, source_target_pairs={{0,16},{16,0},{1,17},{17,1},{2,18},{18,2},{3,19},{19,3},{4,20},{20... | collective-permute-start | bytes 221192 | tf_op jit(solution)/shard_map/ppermute | solution.py:844
  136.5 13.7 %collective-permute-start.51 = (bf16[576,256]{1,0:T(8,128)(2,1)S(1)}, bf16[576,256]{1,0:T(8,128)(2,1)S(1)}, u32[]{:S(2)}, u32[]{:S(2)}) collective-permute-start(bf16[576,256]{1,0:T(8,128)(2,1)S(1)} %collective-permute-done.47.refs_1_), channel_id=1, source_target_pairs={{0,16},{16,0},{1,17},{17,1},{2,18},{18,2},{3,19},{19,3},{4,20},{20... | collective-permute-start | bytes 884744 | tf_op jit(solution)/shard_map/ppermute | solution.py:844
  136.5 11.6 %collective-permute-start.49 = (bf16[576,256]{1,0:T(8,128)(2,1)S(1)}, bf16[576,256]{1,0:T(8,128)(2,1)S(1)}, u32[]{:S(2)}, u32[]{:S(2)}) collective-permute-start(bf16[576,256]{1,0:T(8,128)(2,1)S(1)} %collective-permute-done.47.refs_1_), channel_id=1, source_target_pairs={{0,1},{1,0},{2,3},{3,2},{4,5},{5,4},{6,7},{7,6},{8,9},{9,8},{10,11... | collective-permute-start | bytes 884744 | tf_op jit(solution)/shard_map/ppermute | solution.py:844
  138.5 11.7 %collective-permute-start.52 = (bf16[576,256]{1,0:T(8,128)(2,1)S(1)}, bf16[576,256]{1,0:T(8,128)(2,1)S(1)}, u32[]{:S(2)}, u32[]{:S(2)}) collective-permute-start(bf16[576,256]{1,0:T(8,128)(2,1)S(1)} %collective-permute-done.48.refs_2_), channel_id=1, source_target_pairs={{0,16},{16,0},{1,17},{17,1},{2,18},{18,2},{3,19},{19,3},{4,20},{20... | collective-permute-start | bytes 884744 | tf_op jit(solution)/shard_map/ppermute | solution.py:844
  138.7 10.4 %collective-permute-start.40 = (bf16[96,768]{1,0:T(8,128)(2,1)S(1)}, bf16[96,768]{1,0:T(8,128)(2,1)S(1)}, u32[]{:S(2)}, u32[]{:S(2)}) collective-permute-start(bf16[96,768]{1,0:T(8,128)(2,1)S(1)} %add_convert_fusion.4.refs_0_), channel_id=1, source_target_pairs={{0,2},{1,3},{2,0},{3,1},{4,6},{5,7},{6,4},{7,5},{8,10},{9,11},{10,... | collective-permute-start | bytes 442376 | tf_op jit(solution)/shard_map/ppermute | solution.py:844
  138.8 9.4 %collective-permute-start.34 = (bf16[48,768]{1,0:T(8,128)(2,1)S(1)}, bf16[48,768]{1,0:T(8,128)(2,1)S(1)}, u32[]{:S(2)}, u32[]{:S(2)}) collective-permute-start(bf16[48,768]{1,0:T(8,128)(2,1)S(1)} %collective-permute-done.30.refs_1_), channel_id=1, source_target_pairs={{0,16},{16,0},{1,17},{17,1},{2,18},{18,2},{3,19},{19,3},{4,20},{20... | collective-permute-start | bytes 221192 | tf_op jit(solution)/shard_map/ppermute | solution.py:844
  148.1 11.2 %collective-permute-start.53 = (bf16[576,256]{1,0:T(8,128)(2,1)S(1)}, bf16[576,256]{1,0:T(8,128)(2,1)S(1)}, u32[]{:S(2)}, u32[]{:S(2)}) collective-permute-start(bf16[576,256]{1,0:T(8,128)(2,1)S(1)} %collective-permute-done.49.refs_3_), channel_id=1, source_target_pairs={{0,16},{16,0},{1,17},{17,1},{2,18},{18,2},{3,19},{19,3},{4,20},{20... | collective-permute-start | bytes 884744 | tf_op jit(solution)/shard_map/ppermute | solution.py:844
  150.2 11.8 %collective-permute-start.43 = (bf16[96,768]{1,0:T(8,128)(2,1)S(1)}, bf16[96,768]{1,0:T(8,128)(2,1)S(1)}, u32[]{:S(2)}, u32[]{:S(2)}) collective-permute-start(bf16[96,768]{1,0:T(8,128)(2,1)S(1)} %add_convert_fusion.4.refs_0_), channel_id=1, source_target_pairs={{0,16},{16,0},{1,17},{17,1},{2,18},{18,2},{3,19},{19,3},{4,20},{20... | collective-permute-start | bytes 442376 | tf_op jit(solution)/shard_map/ppermute | solution.py:844
  150.2 11.8 %collective-permute-start.44 = (bf16[96,768]{1,0:T(8,128)(2,1)S(1)}, bf16[96,768]{1,0:T(8,128)(2,1)S(1)}, u32[]{:S(2)}, u32[]{:S(2)}) collective-permute-start(bf16[96,768]{1,0:T(8,128)(2,1)S(1)} %collective-permute-done.40.refs_1_), channel_id=1, source_target_pairs={{0,16},{16,0},{1,17},{17,1},{2,18},{18,2},{3,19},{19,3},{4,20},{20... | collective-permute-start | bytes 442376 | tf_op jit(solution)/shard_map/ppermute | solution.py:844
  (52 other events, 429.5 us)

commit v3 on v2

--- a/solution.py
+++ b/solution.py
@@ -90,7 +90,7 @@
         out_specs=jax.tree.map(lambda _: whole, out) if out_specs is None else out_specs,
         scratch_shapes=list(scratch),
         cost_estimate=pl.CostEstimate(
-            flops=int(cost * 1e6), bytes_accessed=int(cost * 3e3), transcendentals=0
+            flops=int(cost * 1e9), bytes_accessed=int(cost * 3e6), transcendentals=0
         ),
         compiler_params=pltpu.CompilerParams(
             vmem_limit_bytes=(limit if near else 56) * 2**20
@@ -172,11 +172,11 @@
     return (lane < period * pairs) & (place < total_bytes)
 
 
-def laid_out(pieces, lengths, line, first, rows):
+def laid_out(found_ids, lengths, line, first, rows):
     section, seq = (lax.axis_index("section"), lax.axis_index("seq"))
-    count = pieces[0].shape[1] // 128
+    count = found_ids[0].shape[1] // 128
     line[...] = jnp.full(line.shape, -1.0, f32)
-    for k, item in enumerate(pieces):
+    for k, item in enumerate(found_ids):
         for at in range(count):
             both = item[:, at * 128 : (at + 1) * 128]
             row = jnp.where(section == 1, both[1:2], both[0:1])
@@ -209,16 +209,37 @@
         hot[r] = found
 
 
-def gbst_kernel(total_bytes, steps, count, lengths, *refs):
-    pieces = refs[:count]
-    table, score_table, pool, spread, total, conv_bias, bias_score = refs[count : count + 7]
-    tokens, kept, mixing, coefficients, size_weights, ids = refs[count + 7 : count + 13]
-    hot, natural, line, narrow = refs[count + 13 :]
+def fill_mixing(hot, narrow, mixing, vocab):
+    rows = narrow.shape[0]
+
+    def mix(step, carry):
+        own = pl.ds(pl.multiple_of(step * 16, 16), 16)
+        weight = narrow[own, :]
+        for j in range(pairs):
+            acc = [None] * taps
+            for r in reached(j):
+                at = period * j + r
+                column = jnp.broadcast_to(weight[:, at : at + 1], (16, vocab))
+                for tap in range(taps):
+                    term = hot[r + tap, own, :] * column
+                    acc[tap] = term if acc[tap] is None else acc[tap] + term
+            for tap in range(taps):
+                mixing[j, own, tap * vocab : (tap + 1) * vocab] = acc[tap]
+        return carry
+
+    lax.fori_loop(0, rows // 16, mix, 0, unroll=True)
+
+
+def gbst_kernel(total_bytes, steps, parts, lengths, *refs):
+    found_ids = refs[:parts]
+    table, score_table, pool, spread, total, conv_bias, bias_score = refs[parts : parts + 7]
+    tokens, kept, coefficients, size_weights, ids = refs[parts + 7 : parts + 12]
+    mixing, hot, natural, line, narrow = refs[parts + 12 :]
     rows = ids.shape[0]
     vocab = score_table.shape[0]
     width = table.shape[1]
     first = pl.program_id(0) * rows if steps > 1 else 0
-    ids[...] = laid_out(pieces, lengths, line, first, rows)
+    ids[...] = laid_out(found_ids, lengths, line, first, rows)
     fill_hot(ids, hot, vocab)
     parts = mm(hot[...].reshape(columns * rows, vocab), score_table[...])
     scores = parts[:rows]
@@ -243,22 +264,7 @@
     narrow[...] = spread_sum.astype(bf16)
     row_total = split_mm(spread_sum, total)
 
-    def mix(step, carry):
-        own = pl.ds(pl.multiple_of(step * 16, 16), 16)
-        weight = narrow[own, :]
-        for j in range(pairs):
-            acc = [None] * taps
-            for r in reached(j):
-                at = period * j + r
-                column = jnp.broadcast_to(weight[:, at : at + 1], (16, vocab))
-                for tap in range(taps):
-                    term = hot[r + tap, own, :] * column
-                    acc[tap] = term if acc[tap] is None else acc[tap] + term
-            for tap in range(taps):
-                mixing[j, own, tap * vocab : (tap + 1) * vocab] = acc[tap]
-        return carry
-
-    lax.fori_loop(0, rows // 16, mix, 0, unroll=True)
+    fill_mixing(hot, narrow, mixing, vocab)
     bias = as_row(conv_bias)
     by_phase = mm(mixing[...].reshape(pairs * rows, taps * vocab), table[...])
     for j in range(pairs):
@@ -374,9 +380,9 @@
         target[pl.ds(at, piece), :] = item[...].astype(target.dtype)
 
 
-def feed_grad_kernel(ways, chunks, inner, normed, grad_gate, grad_up, out_grad, down_weight, *refs):
-    sums, pieces = (refs[: 2 * chunks], refs[2 * chunks : 2 * chunks + ways])
-    whole_part, stack = refs[2 * chunks + ways :]
+def feed_grad_kernel(chunks, inner, normed, grad_gate, grad_up, out_grad, down_weight, *refs):
+    sums, encoded = (refs[: 2 * chunks], refs[2 * chunks])
+    stack = refs[2 * chunks + 1]
     first = 0
     for left, right in (
         (normed, grad_gate[...]),
@@ -394,8 +400,7 @@
         for side, out in enumerate(sums[2 * chunk : 2 * chunk + 2]):
             at = (2 * chunk + (section ^ side)) * half
             out[...] = stack[pl.ds(pl.multiple_of(at, half), half), :]
-    whole_part[...] = mm(inner[...], down_weight[...])
-    deal(whole_part, pieces)
+    encoded[...] = mm(inner[...], down_weight[...]).astype(bf16)
 
 
 def middle_kernel(ways, *refs):
@@ -538,6 +543,17 @@
                 grad_tokens[at, place, :] += rows[:, at * 128 : (at + 1) * 128]
 
 
+def middle_back_kernel(heads, ways, seq_tokens, *refs):
+    first, second = (refs[: ways + 7], refs[ways + 7 : ways + 13])
+    keep, send, rel_grad, grad_tokens, grad_gain = refs[ways + 13 : ways + 18]
+    branch, stack, grad_queries, grad_keys, grad_values, whole_part = refs[ways + 18 :]
+    grads = (grad_queries, grad_keys, grad_values)
+    attend_back_kernel(heads, ways, *first, keep, send, rel_grad, *grads, branch, stack)
+    normed_back_kernel(
+        1, seq_tokens, ways, *grads, *second, grad_tokens, grad_gain, whole_part
+    )
+
+
 def gbst_back_kernel(
     total_bytes,
     steps,
@@ -545,7 +561,6 @@
     grad_gain_first,
     grad_gain_second,
     rel_grad,
-    mixing,
     coefficients,
     size_weights,
     ids,
@@ -567,6 +582,8 @@
     phased,
     against,
     found,
+    mixing,
+    weights,
 ):
     rows = ids.shape[0]
     vocab, width = embedding.shape
@@ -599,6 +616,8 @@
         on_bias.append(jnp.sum(grad_rows * bias, axis=1, keepdims=True))
     against[...] = mm(phased[...], table[...], cols_cols)
     fill_hot(ids, hot, vocab)
+    weights[...] = coefficients[...].astype(bf16)
+    fill_mixing(hot, weights, mixing, vocab)
     product = mm(mixing[...].reshape(pairs * rows, taps * vocab), phased[...], rows_rows)
     if steps > 1:
         by_byte[...] = product + jnp.where(step == 0, 0.0, by_byte[...])
@@ -737,8 +756,12 @@
             self.sent = merged(self.items)
             self.items = [self.sent]
 
-    def swap(self):
-        self.items = self.items + [exchange(self.sent, "seq", self.masks.pop(0))]
+    def swap(self, extra=None):
+        rows = self.sent.shape[0]
+        sent = self.sent if extra is None else jnp.concatenate([self.sent, extra], axis=0)
+        sent = exchange(sent, "seq", self.masks.pop(0))
+        self.items = self.items + [sent[:rows]]
+        return sent[rows:]
 
     def before(self, value):
         self.sent, value = lax.optimization_barrier((self.sent, value))
@@ -755,14 +778,71 @@
         return merged(self.items)
 
 
-def gather_sum(total, halved):
-    pieces = {0: total}
-    for mask in reversed(halved):
-        for at, item in list(pieces.items()):
-            pieces[at ^ mask] = exchange(item, "seq", mask)
-    names = list(pieces)
-    pieces = [pieces[name] for name in names]
-    return (pieces + [exchange(item, "section", 1) for item in pieces], names)
+class Encoded:
+    def __init__(self, rows):
+        self.masks = [1 << bit for bit in range(lax.axis_size("tensor").bit_length() - 1)]
+        self.items = [rows]
+        self.left = list(self.masks)
+
+    def swap(self):
+        mask = self.left.pop(0)
+        bit = (lax.axis_index("tensor") & mask) != 0
+        blocks = 2 * len(self.left) if self.left else 1
+        split = [
+            item.reshape(blocks, 2, item.shape[0] // (2 * blocks), item.shape[1])
+            for item in self.items
+        ]
+        shape = (self.items[0].shape[0] // 2, self.items[0].shape[1])
+        keep = [jnp.where(bit, item[:, 1], item[:, 0]).reshape(shape) for item in split]
+        sent = [jnp.where(bit, item[:, 0], item[:, 1]).reshape(shape) for item in split]
+        self.items = keep + [exchange(merged(sent), "tensor", mask)]
+
+    def gather(self):
+        mask = self.masks.pop(0)
+        self.pieces = [*self.pieces, exchange(jnp.concatenate(self.pieces), "tensor", mask)]
+
+
+class Gather:
+    def __init__(self, total, halved):
+        self.pieces = {0: total}
+        self.ahead = {}
+        self.halved = halved
+        self.masks = list(reversed(halved))
+        self.arrays, self.holds = ([], [])
+        self.done = []
+
+    def swap(self, extra=None):
+        mask = self.masks.pop(0)
+        arrived = None
+        for at in list(self.pieces):
+            if at ^ mask in self.ahead:
+                self.pieces[at ^ mask] = self.ahead[at ^ mask]
+                continue
+            sent = self.pieces[at]
+            if extra is not None and arrived is None:
+                sent = jnp.concatenate([sent, extra], axis=0)
+            sent = exchange(sent, "seq", mask)
+            if extra is not None and arrived is None:
+                rows = self.pieces[at].shape[0]
+                arrived, sent = (sent[rows:], sent[:rows])
+            self.pieces[at ^ mask] = sent
+        return arrived
+
+    def early(self):
+        for mask in self.masks:
+            self.ahead[mask] = exchange(self.pieces[0], "seq", mask)
+
+    def finish(self):
+        while self.masks:
+            self.swap()
+
+    def across(self):
+        names = [at for at in self.pieces if at not in self.done]
+        self.done += names
+        array = jnp.concatenate([self.pieces[at] for at in names], axis=0)
+        self.arrays += [array, exchange(array, "section", 1)]
+        self.holds += [(0, names), (1, names)]
+        return self.arrays[-1]
 
 
 def place_of(halved, at, rows, index):
@@ -774,32 +854,30 @@
     return first
 
 
-def unstack(pieces, halved, names, chunks, stack):
-    count = len(names)
+def unstack(arrays, halved, holds, stack):
     section, seq = (lax.axis_index("section"), lax.axis_index("seq"))
-    rows = pieces[0].shape[0] // chunks
-    half = rows * count
-    for i, item in enumerate(pieces):
-        side, at = divmod(i, count)
-        place = place_of(halved, names[at], half, seq) + (section ^ side) * half
-        for chunk in range(chunks):
-            first = pl.multiple_of(place + 2 * half * chunk, 8)
-            stack[pl.ds(first, rows), :] = item[chunk * rows : (chunk + 1) * rows, :].astype(f32)
-
-
-def weights_kernel(halved, names, *refs):
-    count = 2 * len(names)
-    pieces, outs, stack = (refs[:count], refs[count:-1], refs[-1])
-    unstack(pieces, halved, names, 1, stack)
+    half = stack.shape[0] // 2
+    for array, (side, names) in zip(arrays, holds):
+        rows = array.shape[0] // len(names)
+        for i, name in enumerate(names):
+            first = place_of(halved, name, half, seq) + (section ^ side) * half
+            part = array[i * rows : (i + 1) * rows, :].astype(f32)
+            stack[pl.ds(pl.multiple_of(first, 8), rows), :] = part
+
+
+def weights_kernel(halved, holds, *refs):
+    count = len(holds)
+    outs, stack = (refs[count:-1], refs[-1])
+    unstack(refs[:count], halved, holds, stack)
     rows = outs[0].shape[0]
     for i, out in enumerate(outs):
         out[...] = stack[i * rows : (i + 1) * rows, :]
 
 
-def feed_weights_kernel(halved, names, chunks, *refs):
-    count = 2 * len(names)
-    pieces, outs, stack = (refs[:count], refs[count:-1], refs[-1])
-    unstack(pieces, halved, names, chunks, stack)
+def feed_weights_kernel(halved, holds, *refs):
+    count = len(holds)
+    outs, stack = (refs[count:-1], refs[-1])
+    unstack(refs[:count], halved, holds, stack)
     first = 0
     for out in outs:
         rows, columns = out.shape
@@ -809,15 +887,16 @@
 
 
 def packed_kernel(ways, heads, *refs):
-    pieces = refs[: 2 * ways]
-    embedding, conv, bias, score, first, second, rel, stack = refs[2 * ways :]
+    pieces, others = (refs[:ways], refs[ways])
+    embedding, conv, bias, score, first, second, rel, stack = refs[ways + 1 :]
     rows = pieces[0].shape[0]
     vocab, width = embedding.shape
     section, tensor = (lax.axis_index("section"), lax.axis_index("tensor"))
-    for i, item in enumerate(pieces):
-        side, k = divmod(i, ways)
-        at = ((section ^ side) * ways + (tensor ^ k)) * rows
-        stack[pl.ds(pl.multiple_of(at, rows), rows), :] = item[...].astype(f32)
+    for k, item in enumerate(pieces):
+        other = others[k * rows : (k + 1) * rows, :]
+        for side, rows_k in enumerate((item[...], other)):
+            at = ((section ^ side) * ways + (tensor ^ k)) * rows
+            stack[pl.ds(pl.multiple_of(at, rows), rows), :] = rows_k.astype(f32)
     embedding[...] = stack[0:vocab, :]
     conv[...] = stack[vocab : vocab + taps, :]
     for i, out in enumerate((bias, score, first, second)):
@@ -827,16 +906,23 @@
     rel[...] = own[:, : rel.shape[1]]
 
 
-def encoded_kernel(ways, *refs):
-    pieces, middle, out = (refs[:ways], refs[ways], refs[ways + 1])
+def encoded_kernel(*refs):
+    pieces, middle, out = (refs[:-2], refs[-2], refs[-1])
     piece = out.shape[0]
     at = pl.multiple_of(lax.axis_index("tensor") * piece, piece)
     total = sum(item[...].astype(f32) for item in pieces)
     out[...] = (middle[pl.ds(at, piece), :] + total).astype(bf16)
 
 
-def assemble_kernel(ways, *refs):
-    collect(refs[:ways], refs[ways])
+def assemble_kernel(*refs):
+    pieces, out = (refs[:-1], refs[-1])
+    rows = pieces[0].shape[0]
+    at = 0
+    for item in pieces:
+        for part in range(item.shape[0] // rows):
+            first = pl.multiple_of((lax.axis_index("tensor") ^ at) * rows, rows)
+            out[pl.ds(first, rows), :] = item[part * rows : (part + 1) * rows, :]
+            at += 1
 
 
 def exchange(value, axis, mask):
@@ -899,8 +985,11 @@
     all_ids = [byte_ids] + [
         exchange(byte_ids, "seq", k) for k in range(1, lax.axis_size("seq"))
     ]
-    all_ids[0], score_table = lax.optimization_barrier((all_ids[0], score_table))
+    all_ids[-1], score_table, out_weight = lax.optimization_barrier(
+        (all_ids[-1], score_table, out_weight)
+    )
     out_weights = copied_out(out_weight)
+
     pool, spread, total = (jnp.asarray(item, bf16) for item in pool_tables())
     def chunked(item, dims):
         if steps == 1:
@@ -919,12 +1008,11 @@
     gbst_out = [
         held((token_rows, model), bf16),
         far((token_rows, model), bf16),
-        far((pairs, rows, taps * vocab), bf16),
         far((rows, 128), f32),
         far((4, rows, 128), f32),
         far((rows, 128), f32),
     ]
-    near_tokens, tokens, mixing, coefficients, size_weights, ids = place(
+    near_tokens, tokens, coefficients, size_weights, ids = place(
         functools.partial(gbst_kernel, total_bytes, steps, len(all_ids)),
         gbst_out,
         byte_lengths,
@@ -937,12 +1025,12 @@
         conv_bias,
         bias_score,
         specs=[scalars, distant]
-        + [local] * (len(all_ids) - 1)
-        + [local] * 2
+        + [local] * (len(all_ids) + 1)
         + [distant] * 4
         + [local],
         out_specs=[chunks(item) for item in gbst_out],
         scratch=[
+            pltpu.VMEM((pairs, chunk_rows, taps * vocab), bf16),
             pltpu.VMEM((columns, chunk_rows, vocab), bf16),
             pltpu.VMEM((model // 128, chunk_tokens, 128), f32),
             pltpu.VMEM((8 * -(-(total_bytes // 128 + 4) // 8), 128), f32),
@@ -973,6 +1061,7 @@
         specs=[scalars, local] + [whole] * 5,
         cost=4,
     )
+    attended, *out_weights = lax.optimization_barrier((attended, *out_weights))
     all_attended = copied_out(attended)
 
     middle, normed_second, inner, grad_gate, grad_up, *normed_parts = place(
@@ -1001,8 +1090,8 @@
     feed_rows = 3 * model * units // 256
     half = feed_rows // (2 * feed_chunks)
     feed_parts = place(
-        functools.partial(feed_grad_kernel, ways, feed_chunks),
-        [held((half, 256), bf16)] * (2 * feed_chunks) + [held((piece, model), bf16)] * ways,
+        functools.partial(feed_grad_kernel, feed_chunks),
+        [held((half, 256), bf16)] * (2 * feed_chunks) + [far((count, model), bf16)],
         inner,
         normed_second,
         grad_gate,
@@ -1010,16 +1099,16 @@
         out_grad,
         down_weight,
         specs=[local] * 4 + [whole] * 2,
-        cost=1.6,
-        scratch=[pltpu.VMEM((count, model), f32), pltpu.VMEM((feed_rows, 256), bf16)],
-    )
-    feed_parts, encoded = (feed_parts[: 2 * feed_chunks], list(feed_parts[2 * feed_chunks :]))
-    normed_parts[0], encoded[0] = lax.optimization_barrier((normed_parts[0], encoded[0]))
+        cost=2,
+        scratch=[pltpu.VMEM((feed_rows, 256), bf16)],
+    )
+    feed_parts, encoded = (feed_parts[: 2 * feed_chunks], feed_parts[2 * feed_chunks])
     feed_sums = [Staged(*feed_parts[2 * i : 2 * i + 2]) for i in range(feed_chunks)]
 
-    feed_sums[0].add()
-    normed_parts[0] = feed_sums[0].before(normed_parts[0])
-    feed_sums[0].swap()
+    feed = feed_sums[0]
+    feed.add()
+    normed_parts[0] = feed.before(normed_parts[0])
+    feed.swap()
     grad_branch, grad_middle, grad_gain_second = place(
         functools.partial(middle_kernel, ways),
         [held((piece, model), bf16), far((piece, model), f32), far((1, model), f32)],
@@ -1030,49 +1119,63 @@
         specs=[local] * (ways + 1) + [whole] * 2,
     )
     branches = copied_out(grad_branch)
+    branches[0] = feed.received_before(branches[0])
+    feed.add()
+    branches[0] = feed.before(branches[0])
+    feed.swap()
     stack_rows = 4 * width
-    weight_keep, weight_send, grad_rel, grad_queries, grad_keys, grad_values = place(
-        functools.partial(attend_back_kernel, heads, ways),
-        [held((stack_rows // 2, model), bf16)] * 2
-        + [far((8, 128), f32)]
-        + [far((token_rows, width), bf16)] * 3,
-        *branches,
-        attended,
-        probs,
-        queries,
-        keys,
-        values,
-        normed,
-        out_weight,
-        specs=[local] * ways + [whole] * 7,
-        cost=5.4,
-        scratch=[pltpu.VMEM((count, model), bf16), pltpu.VMEM((stack_rows, model), bf16)],
-    )
+    first = (*branches, attended, probs, queries, keys, values, normed, out_weight)
+    second = (tokens, query_weight, key_weight, value_weight, norm_first, grad_middle)
+    weights_out = [held((stack_rows // 2, model), bf16)] * 2 + [far((8, 128), f32)]
+    grads_out = [far((token_rows, width), bf16)] * 3
     grad_tokens_out = [held((model // 128, token_rows, 128), f32), held((8, model), f32)]
     per_tile = pl.BlockSpec((model // 128, chunk_tokens, 128), lambda i: (0, i, 0))
-    grad_tokens, grad_gain_first = place(
-        functools.partial(normed_back_kernel, steps, seq_tokens, ways),
-        grad_tokens_out,
-        grad_queries,
-        grad_keys,
-        grad_values,
-        tokens,
-        query_weight,
-        key_weight,
-        value_weight,
-        norm_first,
-        grad_middle,
-        specs=[chunks(item) for item in (grad_queries, grad_keys, grad_values, tokens)]
-        + [distant] * 5,
-        out_specs=[whole if steps == 1 else per_tile, whole],
-        scratch=[pltpu.VMEM((chunk_tokens, model), f32)],
-        grid=grid,
-        limit=20,
-        cost=4,
-    )
-    grad_tokens = feed_sums[0].received_before(grad_tokens)
-    feed_sums[0].add()
-    feed_sums[0].swap()
+    scratch = [pltpu.VMEM((count, model), bf16), pltpu.VMEM((stack_rows, model), bf16)]
+    whole_part = pltpu.VMEM((chunk_tokens, model), f32)
+    first_specs = [local] * ways + [distant] * 7
+    if steps == 1:
+        weight_keep, weight_send, grad_rel, grad_tokens, grad_gain_first = place(
+            functools.partial(middle_back_kernel, heads, ways, seq_tokens),
+            weights_out + grad_tokens_out,
+            *first,
+            *second,
+            specs=first_specs + [distant] * 6,
+            scratch=scratch + [pltpu.VMEM((token_rows, width), bf16)] * 3 + [whole_part],
+            limit=30,
+            cost=10,
+        )
+    else:
+        weight_keep, weight_send, grad_rel, *grads = place(
+            functools.partial(attend_back_kernel, heads, ways),
+            weights_out + grads_out,
+            *first,
+            specs=first_specs,
+            scratch=scratch,
+        )
+        grad_tokens, grad_gain_first = place(
+            functools.partial(normed_back_kernel, steps, seq_tokens, ways),
+            grad_tokens_out,
+            *grads,
+            *second,
+            specs=[chunks(item) for item in (*grads, tokens)] + [distant] * 5,
+            out_specs=[per_tile, whole],
+            scratch=[whole_part],
+            grid=grid,
+        )
+    grad_tokens, weight_send, feed.items, encoded = lax.optimization_barrier(
+        (grad_tokens, weight_send, feed.items, encoded)
+    )
+    branch = Encoded(encoded)
+    feed_gather = Gather(feed.finish(), feed.halved)
+    feed_gather.pieces[0], grad_tokens = lax.optimization_barrier(
+        (feed_gather.pieces[0], grad_tokens)
+    )
+    feed_gather.swap()
+    weight_sum = Staged(weight_keep, weight_send)
+    weight_sum.add()
+    grad_tokens = weight_sum.before(grad_tokens)
+    weight_sum.swap()
+    branch.swap()
     packed_rows = 32 * ways * -(-(vocab + taps + 12) // (32 * ways))
     quarter = packed_rows // (2 * ways)
     keep, send = place(
@@ -1082,7 +1185,6 @@
         grad_gain_first,
         grad_gain_second,
         grad_rel,
-        mixing,
         coefficients,
         size_weights,
         ids,
@@ -1095,7 +1197,7 @@
         score_weight,
         specs=[local if steps == 1 else per_tile, local if steps == 1 else whole]
         + [distant] * 2
-        + [chunks(item) for item in (mixing, coefficients, size_weights, ids)]
+        + [chunks(item) for item in (coefficients, size_weights, ids)]
         + [distant] * 7,
         scratch=[
             pltpu.VMEM((columns, chunk_rows, vocab), bf16),
@@ -1107,37 +1209,66 @@
             pltpu.VMEM((chunk_tokens, model), bf16),
             pltpu.VMEM((chunk_tokens, taps * vocab), f32),
             pltpu.VMEM((chunk_rows, 128), f32),
+            pltpu.VMEM((pairs, chunk_rows, taps * vocab), bf16),
+            pltpu.VMEM((chunk_rows, 128), bf16),
         ],
         grid=grid,
         limit=30,
         cost=12,
     )
-    keep, weight_send, *encoded = lax.optimization_barrier((keep, weight_send, *encoded))
-    keep = feed_sums[0].received_before(keep)
-    weight_sum = Staged(weight_keep, weight_send)
-    encoded = spread_out(encoded)
-    (own_encoded,) = place(
-        functools.partial(encoded_kernel, ways),
-        [held((piece, model), bf16)],
-        *encoded,
-        middle,
-        specs=[local] * (ways + 1),
-    )
+    together = lax.optimization_barrier
+    keep, send, feed_gather.pieces, weight_sum.items, branch.items = together(
+        (keep, send, feed_gather.pieces, weight_sum.items, branch.items)
+    )
+    other = exchange(send, "section", 1)
+    branch.swap()
+    feed_gather.early()
     parts = place(
         deal_kernel,
         [held((quarter, model), bf16)] * ways,
         keep,
-        exchange(send, "section", 1),
+        other,
         specs=[local] * 2,
         scratch=[pltpu.VMEM((packed_rows // 2, model), f32)],
     )
-    items = spread_out(parts)
-    for mask in seq_masks():
+    part = merged(spread_out(parts))
+    weight_sum.add()
+    part, branch.items, weight_sum.sent, weight_sum.items = together(
+        (part, branch.items, weight_sum.sent, weight_sum.items)
+    )
+    masks = seq_masks()
+    items = [part, exchange(part, "seq", masks[0])]
+    weight_sum.swap()
+    (own_encoded,) = place(
+        encoded_kernel,
+        [held((piece, model), bf16)],
+        *branch.items,
+        middle,
+        specs=[local] * (len(branch.items) + 1),
+    )
+    branch.pieces = [own_encoded]
+    branch.gather()
+    items, branch.pieces, feed_gather.pieces, feed_gather.ahead = together(
+        (items, branch.pieces, feed_gather.pieces, feed_gather.ahead)
+    )
+    for mask in masks[1:]:
         part = merged(items)
         items = [part, exchange(part, "seq", mask)]
+    feed_gather.finish()
+    while branch.masks:
+        branch.gather()
+    items, weight_sum.items, feed_gather.pieces, branch.pieces = together(
+        (items, weight_sum.items, feed_gather.pieces, branch.pieces)
+    )
+    weight_gather = Gather(weight_sum.finish(), weight_sum.halved)
+    weight_gather.swap()
+    weight_gather.early()
     part = merged(items)
     gathered = copied_out(part)
-    gathered = gathered + [exchange(item, "section", 1) for item in gathered]
+    feed_gather.across()
+    gathered = [*gathered, exchange(jnp.concatenate(gathered, axis=0), "section", 1)]
+    weight_gather.finish()
+    weight_gather.across()
     grads = place(
         functools.partial(packed_kernel, ways, heads),
         [like((vocab, model), f32), like((taps, model), f32)]
@@ -1147,32 +1278,31 @@
         specs=[local] * len(gathered),
         scratch=[pltpu.VMEM((packed_rows, model), f32)],
     )
+
+    (output,) = place(
+        assemble_kernel,
+        [like((count, model), bf16)],
+        *branch.pieces,
+        specs=[local] * len(branch.pieces),
+    )
+    feed_grads = place(
+        functools.partial(feed_weights_kernel, feed_gather.halved, feed_gather.holds),
+        [like((model, units), f32), like((model, units), f32), like((units, model), f32)],
+        *feed_gather.arrays,
+        specs=[local] * len(feed_gather.arrays),
+        scratch=[pltpu.VMEM((feed_rows, 256), f32)],
+    )
+    weight_gather.arrays, grads, output, feed_grads = together(
+        (weight_gather.arrays, grads, output, feed_grads)
+    )
+    weight_grads = place(
+        functools.partial(weights_kernel, weight_gather.halved, weight_gather.holds),
+        [like((width, model), f32)] * 4,
+        *weight_gather.arrays,
+        specs=[local] * len(weight_gather.arrays),
+        scratch=[pltpu.VMEM((stack_rows, model), f32)],
+    )
     grad_embedding, grad_conv, grad_bias, grad_score, grad_first, grad_second, grad_rel = grads
-
-    (output,) = place(
-        functools.partial(assemble_kernel, ways),
-        [like((count, model), bf16)],
-        *copied_out(own_encoded),
-        specs=[local] * ways,
-    )
-
-    feed_total = feed_sums[0].finish()
-    pieces, names = gather_sum(feed_total, feed_sums[0].halved)
-    feed_grads = place(
-        functools.partial(feed_weights_kernel, feed_sums[0].halved, names, feed_chunks),
-        [like((model, units), f32), like((model, units), f32), like((units, model), f32)],
-        *pieces,
-        specs=[local] * len(pieces),
-        scratch=[pltpu.VMEM((feed_rows, 256), f32)],
-    )
-    pieces, names = gather_sum(weight_sum.finish(), weight_sum.halved)
-    weight_grads = place(
-        functools.partial(weights_kernel, weight_sum.halved, names),
-        [like((width, model), f32)] * 4,
-        *pieces,
-        specs=[local] * len(pieces),
-        scratch=[pltpu.VMEM((stack_rows, model), f32)],
-    )
     return (
         output[None],
         grad_embedding,

time: 164 us -> 150 us (0.915)
  starting transfers between devices: 53.7 us -> 35.7 us
  waiting for transfers between devices: 51.4 us -> 55 us
    ppermute x54 -> x43, starting transfers between devices: 53.7 us -> 35.7 us  [exchange(): return lax.ppermute(value, axis, [(i, i ^ mask) for i in range(size)])]
    ppermute x54 -> x43, waiting for transfers between devices: 51.4 us -> 55 us  [exchange(): return lax.ppermute(value, axis, [(i, i ^ mask) for i in range(size)])]
    pallas_call x15 -> x14, Pallas kernels: 51.8 us -> 52 us  [call(): pl.pallas_call(kernel, out_shape=out, in_specs=specs, out_specs=jax.tree....]
  transfers between devices with their start and end apart: 54 -> 43, of which waited for: 20 -> 25; matrix products, arithmetic and copies ran while one was open for 2% -> 3% of each run, Pallas kernels for 27% -> 30%
where the time goes in v3:
time: 150 us; the launch traced here: 149 us
  waiting for transfers between devices  55 us (37%)
  Pallas kernels  52 us (35%)
  starting transfers between devices  35.7 us (24%)
  other arithmetic  4.21 us (3%)
    ppermute x43, waiting for transfers between devices, exchange(): return lax.ppermute(value, axis, [(i, i ^ mask) for i in range(size)])  55 us
    pallas_call x14, Pallas kernels, call(): pl.pallas_call(kernel, out_shape=out, in_specs=specs, out_specs=jax.tree....  52 us
    ppermute x43, starting transfers between devices, exchange(): return lax.ppermute(value, axis, [(i, i ^ mask) for i in range(size)])  35.7 us
  transfers between devices with their start and end apart: 43, of which 25 were waited for; matrix products, arithmetic and copies ran while one was open for 3% of the time, Pallas kernels for 30%

profile of v3, /device:TPU:0, one launch (start us, length us, event | category | flops | bytes accessed | tf_op | source)
XLA Modules:
  0.0 149.5 jit_solution(17624970472636166378)
XLA Ops:
  0.7 4.1 %collective-permute-start.1 = (s32[2,512]{1,0:T(2,128)}, s32[2,512]{1,0:T(2,128)S(1)}, u32[]{:S(2)}, u32[]{:S(2)}) collective-permute-start(s32[2,512]{1,0:T(2,128)} %refs_0_.1), channel_id=1, source_target_pairs={{0,2},{1,3},{2,0},{3,1},{4,6},{5,7},{6,4},{7,5},{8,10},{9,11},{10,... | collective-permute-start | bytes 12296 | tf_op jit(solution)/shard_map/ppermute | solution.py:930
  6.3 2.0 %shard_map.307 = (bf16[1280,768]{1,0:T(8,128)(2,1)S(1)}, bf16[256,128]{1,0:T(8,128)(2,1)S(1)}, f32[8,128]{1,0:T(8,128)S(1)}) custom-call(bf16[256,768]{1,0:T(8,128)(2,1)} %embedding.3, bf16[5,768]{1,0:T(8,128)(2,1)} %conv_weight.3, bf16[768]{0:T(1024)(128)(2,1)} %score_weight.3, bf16[768]{0:T(1024)(128)(2,1)} %conv_bias.3), custom_call_target="tpu_custom_call" | custom-call | flops 2000000000 | bytes 6000000 | tf_op jit(solution)/shard_map/pallas_call | solution.py:86
  8.3 3.6 %collective-permute-done.2.refs_3_ = s32[2,512]{1,0:T(2,128)S(1)} collective-permute-done((s32[2,512]{1,0:T(2,128)}, s32[2,512]{1,0:T(2,128)S(1)}, u32[]{:S(2)}, u32[]{:S(2)}) %collective-permute-start.2) | collective-permute-done | bytes 4128 | tf_op jit(solution)/shard_map/ppermute | solution.py:930
  12.0 2.4 %collective-permute-start.5 = (bf16[192,768]{1,0:T(8,128)(2,1)S(1)}, bf16[192,768]{1,0:T(8,128)(2,1)S(1)}, u32[]{:S(2)}, u32[]{:S(2)}) collective-permute-start(bf16[192,768]{1,0:T(8,128)(2,1)S(1)} %copy-done.15), channel_id=1, source_target_pairs={{0,12},{4,8},{8,4},{12,0},{1,13},{5,9},{9,5},{13,1},{2,14},{6,10},... | collective-permute-start | bytes 884744 | tf_op jit(solution)/shard_map/ppermute | solution.py:930
  15.5 8.2 %shard_map.308 = (bf16[1056,768]{1,0:T(8,128)(2,1)S(1)}, bf16[1056,768]{1,0:T(8,128)(2,1)}, f32[176,128]{1,0:T(8,128)}, f32[4,176,128]{2,1,0:T(8,128)}, f32[176,128]{1,0:T(8,128)}) custom-call(s32[2]{0:T(128)S(1)} %copy-done.11, s32[2,512]{1,0:T(2,128)} %refs_0_.1, s32[2,512]{1,0:T(2,128)S(1)} %collective-permute-done.refs_1_, ...), custom_call_target="tpu_custom_call" | custom-call | flops 6000000000 | bytes 18000000 | tf_op jit(solution)/shard_map/pallas_call | solution.py:86
  23.9 5.3 %shard_map.309 = (bf16[1024,768]{1,0:T(8,128)(2,1)}, bf16[256,192]{1,0:T(8,128)(2,1)}, bf16[1024,192]{1,0:T(8,128)(2,1)}, bf16[1024,192]{1,0:T(8,128)(2,1)}, bf1...) custom-call(s32[2]{0:T(128)S(1)} %copy-done.11, ...), custom_call_target="tpu_custom_call" | custom-call | flops 4000000000 | bytes 12000000 | tf_op jit(solution)/shard_map/pallas_call | solution.py:86
  29.3 2.5 %collective-permute-start.8 = (bf16[256,192]{1,0:T(8,128)(2,1)S(1)}, bf16[256,192]{1,0:T(8,128)(2,1)S(1)}, u32[]{:S(2)}, u32[]{:S(2)}) collective-permute-start(bf16[256,192]{1,0:T(8,128)(2,1)S(1)} %get-tuple-element.153.refs_0_.refs_4_), channel_id=1, source_target_pairs={{0,12},{4,8},{8,4},{12,0},{1,13},{5,9},{9,5},{13,1},{2,14},{6,10},... | collective-permute-start | bytes 294920 | tf_op jit(solution)/shard_map/ppermute | solution.py:930
  32.8 2.5 %collective-permute-done.8.refs_3_ = bf16[256,192]{1,0:T(8,128)(2,1)S(1)} collective-permute-done((bf16[256,192]{1,0:T(8,128)(2,1)S(1)}, bf16[256,192]{1,0:T(8,128)(2,1)S(1)}, u32[]{:S(2)}, u32[]{:S(2)}) %collective-permute-start.8) | collective-permute-done | bytes 98336 | tf_op jit(solution)/shard_map/ppermute | solution.py:930
  37.3 3.6 %shard_map.310 = (f32[256,768]{1,0:T(8,128)S(1)}, bf16[256,768]{1,0:T(8,128)(2,1)S(1)}, bf16[256,512]{1,0:T(8,128)(2,1)S(1)}, bf16[256,512]{1,0:T(8,128)(2,1)S(1...) custom-call(bf16[256,192]{1,0:T(8,128)(2,1)S(1)} %get-tuple-element., ...), custom_call_target="tpu_custom_call" | custom-call | flops 3000000000 | bytes 9000000 | tf_op jit(solution)/shard_map/pallas_call | solution.py:86
  41.8 2.5 %shard_map.311 = (bf16[2304,256]{1,0:T(8,128)(2,1)S(1)}, bf16[2304,256]{1,0:T(8,128)(2,1)S(1)}, bf16[256,768]{1,0:T(8,128)(2,1)}) custom-call(bf16[256,512]{1,0:T(8,128)(2,1)S(1)} %get-tuple-element.159.inner, bf16[256,768]{1,0:T(8,128)(2,1)S(1)} %get-tuple-element.160.normed, bf16[256,512]{1,0:T(8,128)(2,1)S(1)} %get-tuple-element.161.grad_gate, ...), custom_call_target="tpu_custom_call" | custom-call | flops 2000000000 | bytes 6000000 | tf_op jit(solution)/shard_map/pallas_call | solution.py:86
  50.9 1.6 %collective-permute-done.13.refs_3_ = bf16[64,768]{1,0:T(8,128)(2,1)S(1)} collective-permute-done((bf16[64,768]{1,0:T(8,128)(2,1)S(1)}, bf16[64,768]{1,0:T(8,128)(2,1)S(1)}, u32[]{:S(2)}, u32[]{:S(2)}) %collective-permute-start.13) | collective-permute-done | bytes 98336 | tf_op jit(solution)/shard_map/ppermute | solution.py:930
  53.4 1.8 %collective-permute-start.16 = (bf16[64,768]{1,0:T(8,128)(2,1)S(1)}, bf16[64,768]{1,0:T(8,128)(2,1)S(1)}, u32[]{:S(2)}, u32[]{:S(2)}) collective-permute-start(bf16[64,768]{1,0:T(8,128)(2,1)S(1)} %get-tuple-element.175.refs_0_), channel_id=1, source_target_pairs={{0,12},{4,8},{8,4},{12,0},{1,13},{5,9},{9,5},{13,1},{2,14},{6,10},... | collective-permute-start | bytes 294920 | tf_op jit(solution)/shard_map/ppermute | solution.py:930
  58.2 6.3 %collective-permute-done.10 = bf16[1152,256]{1,0:T(8,128)(2,1)S(1)} collective-permute-done((bf16[1152,256]{1,0:T(8,128)(2,1)S(1)}, bf16[1152,256]{1,0:T(8,128)(2,1)S(1)}, u32[]{:S(2)}, u32[]{:S(2)}) %collective-permute-start.10) | collective-permute-done | bytes 589856 | tf_op jit(solution)/shard_map/ppermute | solution.py:930
  64.8 12.2 %shard_map.313 = (bf16[384,768]{1,0:T(8,128)(2,1)S(1)}, bf16[384,768]{1,0:T(8,128)(2,1)S(1)}, f32[8,128]{1,0:T(8,128)}, f32[6,1056,128]{2,1,0:T(8,128)S(1)}, f32[8,768]{1,0:T(8,128)S(1)}) custom-call(bf16[64,768]{1,0:T(8,128)(2,1)S(1)} %get-tuple-element.175.refs_0_, bf16[64,768]{1,0:T(8,128)(2,1)S(1)} %collective-permute-done.14.refs_1_, ...), custom_call_target="tpu_custom_call" | custom-call | flops 10000000000 | bytes 30000000 | tf_op jit(solution)/shard_map/pallas_call | solution.py:86
  77.0 2.6 %collective-permute-done.17 = bf16[576,256]{1,0:T(8,128)(2,1)S(1)} collective-permute-done((bf16[576,256]{1,0:T(8,128)(2,1)S(1)}, bf16[576,256]{1,0:T(8,128)(2,1)S(1)}, u32[]{:S(2)}, u32[]{:S(2)}) %collective-permute-start.17) | collective-permute-done | bytes 294944 | tf_op jit(solution)/shard_map/ppermute | solution.py:930
  82.1 11.1 %shard_map.314 = (bf16[192,768]{1,0:T(8,128)(2,1)S(1)}, bf16[192,768]{1,0:T(8,128)(2,1)S(1)}) custom-call(f32[6,1056,128]{2,1,0:T(8,128)S(1)} %get-tuple-element.195.grad_tokens, f32[8,768]{1,0:T(8,128)S(1)} %get-tuple-element.196.grad_gain_first, f32[1,768]{1,0:T(1,128)} %get-tuple-element.197.grad_gain_second, f32[8,128]{1,0:T(8,128)} %get-tuple-element.198.rel_grad, ...), custom_call_target="tpu_custom_call" | custom-call | flops 12000000000 | bytes 36000000 | tf_op jit(solution)/shard_map/pallas_call | solution.py:86
  94.5 2.8 %collective-permute-done.20 = bf16[192,768]{1,0:T(8,128)(2,1)S(1)} collective-permute-done((bf16[192,768]{1,0:T(8,128)(2,1)S(1)}, bf16[192,768]{1,0:T(8,128)(2,1)S(1)}, u32[]{:S(2)}, u32[]{:S(2)}) %collective-permute-start.20) | collective-permute-done | bytes 294944 | tf_op jit(solution)/shard_map/ppermute | solution.py:930
  110.8 3.4 %collective-permute-done.29 = bf16[576,256]{1,0:T(8,128)(2,1)S(1)} collective-permute-done((bf16[576,256]{1,0:T(8,128)(2,1)S(1)}, bf16[576,256]{1,0:T(8,128)(2,1)S(1)}, u32[]{:S(2)}, u32[]{:S(2)}) %collective-permute-start.29) | collective-permute-done | bytes 294944 | tf_op jit(solution)/shard_map/ppermute | solution.py:930
  118.5 4.2 %collective-permute-done.30 = bf16[48,768]{1,0:T(8,128)(2,1)S(1)} collective-permute-done((bf16[48,768]{1,0:T(8,128)(2,1)S(1)}, bf16[48,768]{1,0:T(8,128)(2,1)S(1)}, u32[]{:S(2)}, u32[]{:S(2)}) %collective-permute-start.30) | collective-permute-done | bytes 73760 | tf_op jit(solution)/shard_map/ppermute | solution.py:930
  122.6 2.9 %collective-permute-done.32 = bf16[576,256]{1,0:T(8,128)(2,1)S(1)} collective-permute-done((bf16[576,256]{1,0:T(8,128)(2,1)S(1)}, bf16[576,256]{1,0:T(8,128)(2,1)S(1)}, u32[]{:S(2)}, u32[]{:S(2)}) %collective-permute-start.32) | collective-permute-done | bytes 294944 | tf_op jit(solution)/shard_map/ppermute | solution.py:930
  126.5 8.8 %collective-permute-done.34 = bf16[96,768]{1,0:T(8,128)(2,1)S(1)} collective-permute-done((bf16[96,768]{1,0:T(8,128)(2,1)S(1)}, bf16[96,768]{1,0:T(8,128)(2,1)S(1)}, u32[]{:S(2)}, u32[]{:S(2)}) %collective-permute-start.34) | collective-permute-done | bytes 147488 | tf_op jit(solution)/shard_map/ppermute | solution.py:930
  135.4 2.4 %collective-permute-start.40 = (bf16[48,768]{1,0:T(8,128)(2,1)S(1)}, bf16[48,768]{1,0:T(8,128)(2,1)S(1)}, u32[]{:S(2)}, u32[]{:S(2)}) collective-permute-start(bf16[48,768]{1,0:T(8,128)(2,1)S(1)} %add_convert_fusion.7.refs_0_), channel_id=1, source_target_pairs={{0,12},{4,8},{8,4},{12,0},{1,13},{5,9},{9,5},{13,1},{2,14},{6,10},... | collective-permute-start | bytes 221192 | tf_op jit(solution)/shard_map/ppermute | solution.py:930
  138.9 2.2 %collective-permute-done.36 = bf16[96,768]{1,0:T(8,128)(2,1)S(1)} collective-permute-done((bf16[96,768]{1,0:T(8,128)(2,1)S(1)}, bf16[96,768]{1,0:T(8,128)(2,1)S(1)}, u32[]{:S(2)}, u32[]{:S(2)}) %collective-permute-start.36) | collective-permute-done | bytes 147488 | tf_op jit(solution)/shard_map/ppermute | solution.py:930
  145.2 2.6 %shard_map.319 = (f32[768,512]{1,0:T(8,128)}, f32[768,512]{1,0:T(8,128)}, f32[512,768]{1,0:T(8,128)}) custom-call(bf16[2304,256]{1,0:T(8,128)(2,1)S(1)} %constant_dynamic-update-slice_fusion.refs_0_, bf16[2304,256]{1,0:T(8,128)(2,1)S(1)} %collective-permute-done.42.refs_1_), custom_call_target="tpu_custom_call" | custom-call | flops 1000000000 | bytes 3000000 | tf_op jit(solution)/shard_map/pallas_call | solution.py:86
  (143 shorter events, 46.7 us)
Async XLA Ops:
  0.7 14.8 %collective-permute-start.1 = (s32[2,512]{1,0:T(2,128)}, s32[2,512]{1,0:T(2,128)S(1)}, u32[]{:S(2)}, u32[]{:S(2)}) collective-permute-start(s32[2,512]{1,0:T(2,128)} %refs_0_.1), channel_id=1, source_target_pairs={{0,2},{1,3},{2,0},{3,1},{4,6},{5,7},{6,4},{7,5},{8,10},{9,11},{10,... | collective-permute-start | bytes 12296 | tf_op jit(solution)/shard_map/ppermute | solution.py:930
  4.8 10.7 %collective-permute-start = (s32[2,512]{1,0:T(2,128)}, s32[2,512]{1,0:T(2,128)S(1)}, u32[]{:S(2)}, u32[]{:S(2)}) collective-permute-start(s32[2,512]{1,0:T(2,128)} %refs_0_.1), channel_id=1, source_target_pairs={{0,1},{1,0},{2,3},{3,2},{4,5},{5,4},{6,7},{7,6},{8,9},{9,8},{10,11... | collective-permute-start | bytes 12296 | tf_op jit(solution)/shard_map/ppermute | solution.py:930
  12.0 17.3 %collective-permute-start.5 = (bf16[192,768]{1,0:T(8,128)(2,1)S(1)}, bf16[192,768]{1,0:T(8,128)(2,1)S(1)}, u32[]{:S(2)}, u32[]{:S(2)}) collective-permute-start(bf16[192,768]{1,0:T(8,128)(2,1)S(1)} %copy-done.15), channel_id=1, source_target_pairs={{0,12},{4,8},{8,4},{12,0},{1,13},{5,9},{9,5},{13,1},{2,14},{6,10},... | collective-permute-start | bytes 884744 | tf_op jit(solution)/shard_map/ppermute | solution.py:930
  14.4 14.8 %collective-permute-start.4 = (bf16[192,768]{1,0:T(8,128)(2,1)S(1)}, bf16[192,768]{1,0:T(8,128)(2,1)S(1)}, u32[]{:S(2)}, u32[]{:S(2)}) collective-permute-start(bf16[192,768]{1,0:T(8,128)(2,1)S(1)} %copy-done.15), channel_id=1, source_target_pairs={{0,8},{4,12},{8,0},{12,4},{1,9},{5,13},{9,1},{13,5},{2,10},{6,14},... | collective-permute-start | bytes 884744 | tf_op jit(solution)/shard_map/ppermute | solution.py:930
  14.9 14.3 %collective-permute-start.3 = (bf16[192,768]{1,0:T(8,128)(2,1)S(1)}, bf16[192,768]{1,0:T(8,128)(2,1)S(1)}, u32[]{:S(2)}, u32[]{:S(2)}) collective-permute-start(bf16[192,768]{1,0:T(8,128)(2,1)S(1)} %copy-done.15), channel_id=1, source_target_pairs={{0,4},{4,0},{8,12},{12,8},{1,5},{5,1},{9,13},{13,9},{2,6},{6,2},{1... | collective-permute-start | bytes 884744 | tf_op jit(solution)/shard_map/ppermute | solution.py:930
  46.3 6.2 %collective-permute-start.13 = (bf16[64,768]{1,0:T(8,128)(2,1)S(1)}, bf16[64,768]{1,0:T(8,128)(2,1)S(1)}, u32[]{:S(2)}, u32[]{:S(2)}) collective-permute-start(bf16[64,768]{1,0:T(8,128)(2,1)S(1)} %get-tuple-element.170), channel_id=1, source_target_pairs={{0,12},{4,8},{8,4},{12,0},{1,13},{5,9},{9,5},{13,1},{2,14},{6,10},... | collective-permute-start | bytes 294920 | tf_op jit(solution)/shard_map/ppermute | solution.py:930
  49.5 15.0 %collective-permute-start.10 = (bf16[1152,256]{1,0:T(8,128)(2,1)S(1)}, bf16[1152,256]{1,0:T(8,128)(2,1)S(1)}, u32[]{:S(2)}, u32[]{:S(2)}) collective-permute-start(bf16[1152,256]{1,0:T(8,128)(2,1)S(1)} %add_convert_fusion), channel_id=1, source_target_pairs={{0,1},{1,0},{2,3},{3,2},{4,5},{5,4},{6,7},{7,6},{8,9},{9,8},{10,11... | collective-permute-start | bytes 1769480 | tf_op jit(solution)/shard_map/ppermute | solution.py:930
  53.4 11.4 %collective-permute-start.16 = (bf16[64,768]{1,0:T(8,128)(2,1)S(1)}, bf16[64,768]{1,0:T(8,128)(2,1)S(1)}, u32[]{:S(2)}, u32[]{:S(2)}) collective-permute-start(bf16[64,768]{1,0:T(8,128)(2,1)S(1)} %get-tuple-element.175.refs_0_), channel_id=1, source_target_pairs={{0,12},{4,8},{8,4},{12,0},{1,13},{5,9},{9,5},{13,1},{2,14},{6,10},... | collective-permute-start | bytes 294920 | tf_op jit(solution)/shard_map/ppermute | solution.py:930
  55.1 9.6 %collective-permute-start.15 = (bf16[64,768]{1,0:T(8,128)(2,1)S(1)}, bf16[64,768]{1,0:T(8,128)(2,1)S(1)}, u32[]{:S(2)}, u32[]{:S(2)}) collective-permute-start(bf16[64,768]{1,0:T(8,128)(2,1)S(1)} %get-tuple-element.175.refs_0_), channel_id=1, source_target_pairs={{0,8},{4,12},{8,0},{12,4},{1,9},{5,13},{9,1},{13,5},{2,10},{6,14},... | collective-permute-start | bytes 294920 | tf_op jit(solution)/shard_map/ppermute | solution.py:930
  55.7 9.1 %collective-permute-start.14 = (bf16[64,768]{1,0:T(8,128)(2,1)S(1)}, bf16[64,768]{1,0:T(8,128)(2,1)S(1)}, u32[]{:S(2)}, u32[]{:S(2)}) collective-permute-start(bf16[64,768]{1,0:T(8,128)(2,1)S(1)} %get-tuple-element.175.refs_0_), channel_id=1, source_target_pairs={{0,4},{4,0},{8,12},{12,8},{1,5},{5,1},{9,13},{13,9},{2,6},{6,2},{1... | collective-permute-start | bytes 294920 | tf_op jit(solution)/shard_map/ppermute | solution.py:930
  64.7 15.0 %collective-permute-start.17 = (bf16[576,256]{1,0:T(8,128)(2,1)S(1)}, bf16[576,256]{1,0:T(8,128)(2,1)S(1)}, u32[]{:S(2)}, u32[]{:S(2)}) collective-permute-start(bf16[576,256]{1,0:T(8,128)(2,1)S(1)} %add_convert_fusion.3), channel_id=1, source_target_pairs={{0,2},{1,3},{2,0},{3,1},{4,6},{5,7},{6,4},{7,5},{8,10},{9,11},{10,... | collective-permute-start | bytes 884744 | tf_op jit(solution)/shard_map/ppermute | solution.py:930
  79.9 14.6 %collective-permute-start.19 = (bf16[576,256]{1,0:T(8,128)(2,1)S(1)}, bf16[576,256]{1,0:T(8,128)(2,1)S(1)}, u32[]{:S(2)}, u32[]{:S(2)}) collective-permute-start(bf16[576,256]{1,0:T(8,128)(2,1)S(1)} %add_convert_fusion.1), channel_id=1, source_target_pairs={{0,2},{1,3},{2,0},{3,1},{4,6},{5,7},{6,4},{7,5},{8,10},{9,11},{10,... | collective-permute-start | bytes 884744 | tf_op jit(solution)/shard_map/ppermute | solution.py:930
  80.7 12.6 %collective-permute-start.21 = (bf16[128,768]{1,0:T(8,128)(2,1)S(1)}, bf16[128,768]{1,0:T(8,128)(2,1)S(1)}, u32[]{:S(2)}, u32[]{:S(2)}) collective-permute-start(bf16[128,768]{1,0:T(8,128)(2,1)S(1)} %bitcast.32), channel_id=1, source_target_pairs={{0,4},{4,0},{8,12},{12,8},{1,5},{5,1},{9,13},{13,9},{2,6},{6,2},{1... | collective-permute-start | bytes 589832 | tf_op jit(solution)/shard_map/ppermute | solution.py:930
  81.8 15.4 %collective-permute-start.20 = (bf16[192,768]{1,0:T(8,128)(2,1)S(1)}, bf16[192,768]{1,0:T(8,128)(2,1)S(1)}, u32[]{:S(2)}, u32[]{:S(2)}) collective-permute-start(bf16[192,768]{1,0:T(8,128)(2,1)S(1)} %add_convert_fusion.2), channel_id=1, source_target_pairs={{0,1},{1,0},{2,3},{3,2},{4,5},{5,4},{6,7},{7,6},{8,9},{9,8},{10,11... | collective-permute-start | bytes 884744 | tf_op jit(solution)/shard_map/ppermute | solution.py:930
  104.2 10.0 %collective-permute-start.29 = (bf16[576,256]{1,0:T(8,128)(2,1)S(1)}, bf16[576,256]{1,0:T(8,128)(2,1)S(1)}, u32[]{:S(2)}, u32[]{:S(2)}) collective-permute-start(bf16[576,256]{1,0:T(8,128)(2,1)S(1)} %add_convert_fusion.1), channel_id=1, source_target_pairs={{0,1},{1,0},{2,3},{3,2},{4,5},{5,4},{6,7},{7,6},{8,9},{9,8},{10,11... | collective-permute-start | bytes 884744 | tf_op jit(solution)/shard_map/ppermute | solution.py:930
  108.4 6.5 %collective-permute-start.28 = (bf16[64,768]{1,0:T(8,128)(2,1)S(1)}, bf16[64,768]{1,0:T(8,128)(2,1)S(1)}, u32[]{:S(2)}, u32[]{:S(2)}) collective-permute-start(bf16[64,768]{1,0:T(8,128)(2,1)S(1)} %shard_map.316.refs_0_), channel_id=1, source_target_pairs={{0,4},{4,0},{8,12},{12,8},{1,5},{5,1},{9,13},{13,9},{2,6},{6,2},{1... | collective-permute-start | bytes 294920 | tf_op jit(solution)/shard_map/ppermute | solution.py:930
  109.5 9.0 %collective-permute-start.31 = (bf16[96,768]{1,0:T(8,128)(2,1)S(1)}, bf16[96,768]{1,0:T(8,128)(2,1)S(1)}, u32[]{:S(2)}, u32[]{:S(2)}) collective-permute-start(bf16[96,768]{1,0:T(8,128)(2,1)S(1)} %add_convert_fusion.5), channel_id=1, source_target_pairs={{0,2},{1,3},{2,0},{3,1},{4,6},{5,7},{6,4},{7,5},{8,10},{9,11},{10,... | collective-permute-start | bytes 442376 | tf_op jit(solution)/shard_map/ppermute | solution.py:930
  114.9 7.7 %collective-permute-start.33 = (bf16[128,768]{1,0:T(8,128)(2,1)S(1)}, bf16[128,768]{1,0:T(8,128)(2,1)S(1)}, u32[]{:S(2)}, u32[]{:S(2)}) collective-permute-start(bf16[128,768]{1,0:T(8,128)(2,1)S(1)} %pad_maximum_fusion.2), channel_id=1, source_target_pairs={{0,8},{4,12},{8,0},{12,4},{1,9},{5,13},{9,1},{13,5},{2,10},{6,14},... | collective-permute-start | bytes 589832 | tf_op jit(solution)/shard_map/ppermute | solution.py:930
  115.7 9.7 %collective-permute-start.32 = (bf16[576,256]{1,0:T(8,128)(2,1)S(1)}, bf16[576,256]{1,0:T(8,128)(2,1)S(1)}, u32[]{:S(2)}, u32[]{:S(2)}) collective-permute-start(bf16[576,256]{1,0:T(8,128)(2,1)S(1)} %collective-permute-done.19), channel_id=1, source_target_pairs={{0,1},{1,0},{2,3},{3,2},{4,5},{5,4},{6,7},{7,6},{8,9},{9,8},{10,11... | collective-permute-start | bytes 884744 | tf_op jit(solution)/shard_map/ppermute | solution.py:930
  116.1 6.5 %collective-permute-start.30 = (bf16[48,768]{1,0:T(8,128)(2,1)S(1)}, bf16[48,768]{1,0:T(8,128)(2,1)S(1)}, u32[]{:S(2)}, u32[]{:S(2)}) collective-permute-start(bf16[48,768]{1,0:T(8,128)(2,1)S(1)} %add_convert_fusion.8), channel_id=1, source_target_pairs={{0,2},{1,3},{2,0},{3,1},{4,6},{5,7},{6,4},{7,5},{8,10},{9,11},{10,... | collective-permute-start | bytes 221192 | tf_op jit(solution)/shard_map/ppermute | solution.py:930
  125.6 19.6 %collective-permute-start.42 = (bf16[2304,256]{1,0:T(8,128)(2,1)S(1)}, bf16[2304,256]{1,0:T(8,128)(2,1)S(1)}, u32[]{:S(2)}, u32[]{:S(2)}) collective-permute-start(bf16[2304,256]{1,0:T(8,128)(2,1)S(1)} %constant_dynamic-update-slice_fusion.refs_0_), channel_id=1, source_target_pairs={{0,16},{16,0},{1,17},{17,1},{2,18},{18,2},{3,19},{19,3},{4,20},{20... | collective-permute-start | bytes 3538952 | tf_op jit(solution)/shard_map/ppermute | solution.py:930
  125.8 9.6 %collective-permute-start.34 = (bf16[96,768]{1,0:T(8,128)(2,1)S(1)}, bf16[96,768]{1,0:T(8,128)(2,1)S(1)}, u32[]{:S(2)}, u32[]{:S(2)}) collective-permute-start(bf16[96,768]{1,0:T(8,128)(2,1)S(1)} %add_convert_fusion.4), channel_id=1, source_target_pairs={{0,2},{1,3},{2,0},{3,1},{4,6},{5,7},{6,4},{7,5},{8,10},{9,11},{10,... | collective-permute-start | bytes 442376 | tf_op jit(solution)/shard_map/ppermute | solution.py:930
  126.3 11.8 %collective-permute-start.35 = (bf16[96,768]{1,0:T(8,128)(2,1)S(1)}, bf16[96,768]{1,0:T(8,128)(2,1)S(1)}, u32[]{:S(2)}, u32[]{:S(2)}) collective-permute-start(bf16[96,768]{1,0:T(8,128)(2,1)S(1)} %add_convert_fusion.4), channel_id=1, source_target_pairs={{0,1},{1,0},{2,3},{3,2},{4,5},{5,4},{6,7},{7,6},{8,9},{9,8},{10,11... | collective-permute-start | bytes 442376 | tf_op jit(solution)/shard_map/ppermute | solution.py:930
  141.1 6.7 %collective-permute-start.37 = (bf16[384,768]{1,0:T(8,128)(2,1)S(1)}, bf16[384,768]{1,0:T(8,128)(2,1)S(1)}, u32[]{:S(2)}, u32[]{:S(2)}) collective-permute-start(bf16[384,768]{1,0:T(8,128)(2,1)S(1)} %pad_maximum_fusion.refs_0_), channel_id=1, source_target_pairs={{0,16},{16,0},{1,17},{17,1},{2,18},{18,2},{3,19},{19,3},{4,20},{20... | collective-permute-start | bytes 1769480 | tf_op jit(solution)/shard_map/ppermute | solution.py:930
  (38 other events, 266.4 us)

commit v4 on v3

--- a/solution.py
+++ b/solution.py
@@ -985,9 +985,7 @@
     all_ids = [byte_ids] + [
         exchange(byte_ids, "seq", k) for k in range(1, lax.axis_size("seq"))
     ]
-    all_ids[-1], score_table, out_weight = lax.optimization_barrier(
-        (all_ids[-1], score_table, out_weight)
-    )
+    score_table, out_weight = lax.optimization_barrier((score_table, out_weight))
     out_weights = copied_out(out_weight)
 
     pool, spread, total = (jnp.asarray(item, bf16) for item in pool_tables())
@@ -1082,7 +1080,7 @@
         up_weight,
         down_weight,
         out_grad,
-        specs=[local] * ways + [distant] * ways + [local] + [whole] * 5,
+        specs=[local] * ways + [distant] * ways + [local, distant] + [whole] * 4,
         cost=3,
         scratch=[pltpu.VMEM((count, model), f32)],
     )
@@ -1116,7 +1114,7 @@
         middle,
         out_grad,
         norm_second,
-        specs=[local] * (ways + 1) + [whole] * 2,
+        specs=[local] * (ways + 1) + [whole, distant],
     )
     branches = copied_out(grad_branch)
     branches[0] = feed.received_before(branches[0])
@@ -1266,8 +1264,25 @@
     part = merged(items)
     gathered = copied_out(part)
     feed_gather.across()
+    weight_gather.pieces = together((weight_gather.pieces, gathered))[0]
     gathered = [*gathered, exchange(jnp.concatenate(gathered, axis=0), "section", 1)]
+    (output,) = place(
+        assemble_kernel,
+        [like((count, model), bf16)],
+        *branch.pieces,
+        specs=[local] * len(branch.pieces),
+    )
+    feed_grads = place(
+        functools.partial(feed_weights_kernel, feed_gather.halved, feed_gather.holds),
+        [like((model, units), f32), like((model, units), f32), like((units, model), f32)],
+        *feed_gather.arrays,
+        specs=[local] * len(feed_gather.arrays),
+        scratch=[pltpu.VMEM((feed_rows, 256), f32)],
+    )
     weight_gather.finish()
+    weight_gather.pieces, feed_grads, output = together(
+        (weight_gather.pieces, feed_grads, output)
+    )
     weight_gather.across()
     grads = place(
         functools.partial(packed_kernel, ways, heads),
@@ -1279,19 +1294,6 @@
         scratch=[pltpu.VMEM((packed_rows, model), f32)],
     )
 
-    (output,) = place(
-        assemble_kernel,
-        [like((count, model), bf16)],
-        *branch.pieces,
-        specs=[local] * len(branch.pieces),
-    )
-    feed_grads = place(
-        functools.partial(feed_weights_kernel, feed_gather.halved, feed_gather.holds),
-        [like((model, units), f32), like((model, units), f32), like((units, model), f32)],
-        *feed_gather.arrays,
-        specs=[local] * len(feed_gather.arrays),
-        scratch=[pltpu.VMEM((feed_rows, 256), f32)],
-    )
     weight_gather.arrays, grads, output, feed_grads = together(
         (weight_gather.arrays, grads, output, feed_grads)
     )

time: 150 us -> 144 us (0.960)
  waiting for transfers between devices: 55 us -> 33.8 us
  starting transfers between devices: 35.7 us -> 50.8 us
    ppermute x43, waiting for transfers between devices: 55 us -> 33.8 us  [exchange(): return lax.ppermute(value, axis, [(i, i ^ mask) for i in range(size)])]
    ppermute x43, starting transfers between devices: 35.7 us -> 50.8 us  [exchange(): return lax.ppermute(value, axis, [(i, i ^ mask) for i in range(size)])]
  transfers between devices with their start and end apart: 43 -> 43, of which waited for: 25 -> 20; matrix products, arithmetic and copies ran while one was open for 3% -> 3% of each run, Pallas kernels for 30% -> 31%
where the time goes in v4:
time: 144 us; the launch traced here: 143 us
  Pallas kernels  52.6 us (37%)
  starting transfers between devices  50.8 us (35%)
  waiting for transfers between devices  33.8 us (23%)
  other arithmetic  4.17 us (3%)
    pallas_call x14, Pallas kernels, call(): pl.pallas_call(kernel, out_shape=out, in_specs=specs, out_specs=jax.tree....  52.6 us
    ppermute x43, starting transfers between devices, exchange(): return lax.ppermute(value, axis, [(i, i ^ mask) for i in range(size)])  50.8 us
    ppermute x43, waiting for transfers between devices, exchange(): return lax.ppermute(value, axis, [(i, i ^ mask) for i in range(size)])  33.8 us
  transfers between devices with their start and end apart: 43, of which 20 were waited for; matrix products, arithmetic and copies ran while one was open for 3% of the time, Pallas kernels for 31%

profile of v4, /device:TPU:0, one launch (start us, length us, event | category | flops | bytes accessed | tf_op | source)
XLA Modules:
  0.0 143.3 jit_solution(12639909902947320151)
XLA Ops:
  0.7 4.1 %collective-permute-start.1 = (s32[2,512]{1,0:T(2,128)}, s32[2,512]{1,0:T(2,128)S(1)}, u32[]{:S(2)}, u32[]{:S(2)}) collective-permute-start(s32[2,512]{1,0:T(2,128)} %refs_0_.1), channel_id=1, source_target_pairs={{0,2},{1,3},{2,0},{3,1},{4,6},{5,7},{6,4},{7,5},{8,10},{9,11},{10,... | collective-permute-start | bytes 12296 | tf_op jit(solution)/shard_map/ppermute | solution.py:930
  6.3 2.0 %shard_map.307 = (bf16[1280,768]{1,0:T(8,128)(2,1)S(1)}, bf16[256,128]{1,0:T(8,128)(2,1)S(1)}, f32[8,128]{1,0:T(8,128)S(1)}) custom-call(bf16[256,768]{1,0:T(8,128)(2,1)} %embedding.3, bf16[5,768]{1,0:T(8,128)(2,1)} %conv_weight.3, bf16[768]{0:T(1024)(128)(2,1)} %score_weight.3, bf16[768]{0:T(1024)(128)(2,1)} %conv_bias.3), custom_call_target="tpu_custom_call" | custom-call | flops 2000000000 | bytes 6000000 | tf_op jit(solution)/shard_map/pallas_call | solution.py:86
  8.4 2.7 %collective-permute-start.5 = (bf16[192,768]{1,0:T(8,128)(2,1)S(1)}, bf16[192,768]{1,0:T(8,128)(2,1)S(1)}, u32[]{:S(2)}, u32[]{:S(2)}) collective-permute-start(bf16[192,768]{1,0:T(8,128)(2,1)S(1)} %copy-done.14), channel_id=1, source_target_pairs={{0,12},{4,8},{8,4},{12,0},{1,13},{5,9},{9,5},{13,1},{2,14},{6,10},... | collective-permute-start | bytes 884744 | tf_op jit(solution)/shard_map/ppermute | solution.py:930
  12.0 8.3 %shard_map.308 = (bf16[1056,768]{1,0:T(8,128)(2,1)S(1)}, bf16[1056,768]{1,0:T(8,128)(2,1)}, f32[176,128]{1,0:T(8,128)}, f32[4,176,128]{2,1,0:T(8,128)}, f32[176,128]{1,0:T(8,128)}) custom-call(s32[2]{0:T(128)S(1)} %copy-done.10, s32[2,512]{1,0:T(2,128)} %refs_0_.1, s32[2,512]{1,0:T(2,128)S(1)} %collective-permute-done.refs_1_, ...), custom_call_target="tpu_custom_call" | custom-call | flops 6000000000 | bytes 18000000 | tf_op jit(solution)/shard_map/pallas_call | solution.py:86
  20.4 5.3 %shard_map.309 = (bf16[1024,768]{1,0:T(8,128)(2,1)}, bf16[256,192]{1,0:T(8,128)(2,1)}, bf16[1024,192]{1,0:T(8,128)(2,1)}, bf16[1024,192]{1,0:T(8,128)(2,1)}, bf1...) custom-call(s32[2]{0:T(128)S(1)} %copy-done.10, ...), custom_call_target="tpu_custom_call" | custom-call | flops 4000000000 | bytes 12000000 | tf_op jit(solution)/shard_map/pallas_call | solution.py:86
  25.8 2.7 %collective-permute-start.8 = (bf16[256,192]{1,0:T(8,128)(2,1)S(1)}, bf16[256,192]{1,0:T(8,128)(2,1)S(1)}, u32[]{:S(2)}, u32[]{:S(2)}) collective-permute-start(bf16[256,192]{1,0:T(8,128)(2,1)S(1)} %get-tuple-element.161.refs_0_.refs_4_), channel_id=1, source_target_pairs={{0,12},{4,8},{8,4},{12,0},{1,13},{5,9},{9,5},{13,1},{2,14},{6,10},... | collective-permute-start | bytes 294920 | tf_op jit(solution)/shard_map/ppermute | solution.py:930
  29.3 3.8 %collective-permute-done.8.refs_3_ = bf16[256,192]{1,0:T(8,128)(2,1)S(1)} collective-permute-done((bf16[256,192]{1,0:T(8,128)(2,1)S(1)}, bf16[256,192]{1,0:T(8,128)(2,1)S(1)}, u32[]{:S(2)}, u32[]{:S(2)}) %collective-permute-start.8) | collective-permute-done | bytes 98336 | tf_op jit(solution)/shard_map/ppermute | solution.py:930
  34.0 3.5 %shard_map.310 = (f32[256,768]{1,0:T(8,128)S(1)}, bf16[256,768]{1,0:T(8,128)(2,1)S(1)}, bf16[256,512]{1,0:T(8,128)(2,1)S(1)}, bf16[256,512]{1,0:T(8,128)(2,1)S(1...) custom-call(bf16[256,192]{1,0:T(8,128)(2,1)S(1)} %get-tuple-element., ...), custom_call_target="tpu_custom_call" | custom-call | flops 3000000000 | bytes 9000000 | tf_op jit(solution)/shard_map/pallas_call | solution.py:86
  37.6 2.5 %shard_map.311 = (bf16[2304,256]{1,0:T(8,128)(2,1)S(1)}, bf16[2304,256]{1,0:T(8,128)(2,1)S(1)}, bf16[256,768]{1,0:T(8,128)(2,1)}) custom-call(bf16[256,512]{1,0:T(8,128)(2,1)S(1)} %get-tuple-element.167.inner, bf16[256,768]{1,0:T(8,128)(2,1)S(1)} %get-tuple-element.168.normed, bf16[256,512]{1,0:T(8,128)(2,1)S(1)} %get-tuple-element.169.grad_gate, ...), custom_call_target="tpu_custom_call" | custom-call | flops 2000000000 | bytes 6000000 | tf_op jit(solution)/shard_map/pallas_call | solution.py:86
  46.2 2.1 %collective-permute-done.13.refs_3_ = bf16[64,768]{1,0:T(8,128)(2,1)S(1)} collective-permute-done((bf16[64,768]{1,0:T(8,128)(2,1)S(1)}, bf16[64,768]{1,0:T(8,128)(2,1)S(1)}, u32[]{:S(2)}, u32[]{:S(2)}) %collective-permute-start.13) | collective-permute-done | bytes 98336 | tf_op jit(solution)/shard_map/ppermute | solution.py:930
  54.6 5.6 %collective-permute-done.10 = bf16[1152,256]{1,0:T(8,128)(2,1)S(1)} collective-permute-done((bf16[1152,256]{1,0:T(8,128)(2,1)S(1)}, bf16[1152,256]{1,0:T(8,128)(2,1)S(1)}, u32[]{:S(2)}, u32[]{:S(2)}) %collective-permute-start.10) | collective-permute-done | bytes 589856 | tf_op jit(solution)/shard_map/ppermute | solution.py:930
  60.5 2.5 %collective-permute-start.17 = (bf16[576,256]{1,0:T(8,128)(2,1)S(1)}, bf16[576,256]{1,0:T(8,128)(2,1)S(1)}, u32[]{:S(2)}, u32[]{:S(2)}) collective-permute-start(bf16[576,256]{1,0:T(8,128)(2,1)S(1)} %add_convert_fusion.3), channel_id=1, source_target_pairs={{0,2},{1,3},{2,0},{3,1},{4,6},{5,7},{6,4},{7,5},{8,10},{9,11},{10,... | collective-permute-start | bytes 884744 | tf_op jit(solution)/shard_map/ppermute | solution.py:930
  63.0 12.2 %shard_map.313 = (bf16[384,768]{1,0:T(8,128)(2,1)S(1)}, bf16[384,768]{1,0:T(8,128)(2,1)S(1)}, f32[8,128]{1,0:T(8,128)}, f32[6,1056,128]{2,1,0:T(8,128)S(1)}, f32[8,768]{1,0:T(8,128)S(1)}) custom-call(bf16[64,768]{1,0:T(8,128)(2,1)S(1)} %get-tuple-element.183.refs_0_, bf16[64,768]{1,0:T(8,128)(2,1)S(1)} %collective-permute-done.14.refs_1_, ...), custom_call_target="tpu_custom_call" | custom-call | flops 10000000000 | bytes 30000000 | tf_op jit(solution)/shard_map/pallas_call | solution.py:86
  77.8 3.4 %collective-permute-start.20 = (bf16[192,768]{1,0:T(8,128)(2,1)S(1)}, bf16[192,768]{1,0:T(8,128)(2,1)S(1)}, u32[]{:S(2)}, u32[]{:S(2)}) collective-permute-start(bf16[192,768]{1,0:T(8,128)(2,1)S(1)} %add_convert_fusion.2), channel_id=1, source_target_pairs={{0,1},{1,0},{2,3},{3,2},{4,5},{5,4},{6,7},{7,6},{8,9},{9,8},{10,11... | collective-permute-start | bytes 884744 | tf_op jit(solution)/shard_map/ppermute | solution.py:930
  81.2 11.1 %shard_map.314 = (bf16[192,768]{1,0:T(8,128)(2,1)S(1)}, bf16[192,768]{1,0:T(8,128)(2,1)S(1)}) custom-call(f32[6,1056,128]{2,1,0:T(8,128)S(1)} %get-tuple-element.203.grad_tokens, f32[8,768]{1,0:T(8,128)S(1)} %get-tuple-element.204.grad_gain_first, f32[1,768]{1,0:T(1,128)} %get-tuple-element.205.grad_gain_second, f32[8,128]{1,0:T(8,128)} %get-tuple-element.206.rel_grad, ...), custom_call_target="tpu_custom_call" | custom-call | flops 12000000000 | bytes 36000000 | tf_op jit(solution)/shard_map/pallas_call | solution.py:86
  105.7 3.7 %collective-permute-start.31 = (bf16[96,768]{1,0:T(8,128)(2,1)S(1)}, bf16[96,768]{1,0:T(8,128)(2,1)S(1)}, u32[]{:S(2)}, u32[]{:S(2)}) collective-permute-start(bf16[96,768]{1,0:T(8,128)(2,1)S(1)} %add_convert_fusion.5), channel_id=1, source_target_pairs={{0,2},{1,3},{2,0},{3,1},{4,6},{5,7},{6,4},{7,5},{8,10},{9,11},{10,... | collective-permute-start | bytes 442376 | tf_op jit(solution)/shard_map/ppermute | solution.py:930
  109.4 2.5 %collective-permute-done.27 = bf16[48,768]{1,0:T(8,128)(2,1)S(1)} collective-permute-done((bf16[48,768]{1,0:T(8,128)(2,1)S(1)}, bf16[48,768]{1,0:T(8,128)(2,1)S(1)}, u32[]{:S(2)}, u32[]{:S(2)}) %collective-permute-start.27) | collective-permute-done | bytes 73760 | tf_op jit(solution)/shard_map/ppermute | solution.py:930
  112.1 3.7 %collective-permute-start.30 = (bf16[48,768]{1,0:T(8,128)(2,1)S(1)}, bf16[48,768]{1,0:T(8,128)(2,1)S(1)}, u32[]{:S(2)}, u32[]{:S(2)}) collective-permute-start(bf16[48,768]{1,0:T(8,128)(2,1)S(1)} %add_convert_fusion.8), channel_id=1, source_target_pairs={{0,2},{1,3},{2,0},{3,1},{4,6},{5,7},{6,4},{7,5},{8,10},{9,11},{10,... | collective-permute-start | bytes 221192 | tf_op jit(solution)/shard_map/ppermute | solution.py:930
  116.0 3.6 %collective-permute-done.30 = bf16[48,768]{1,0:T(8,128)(2,1)S(1)} collective-permute-done((bf16[48,768]{1,0:T(8,128)(2,1)S(1)}, bf16[48,768]{1,0:T(8,128)(2,1)S(1)}, u32[]{:S(2)}, u32[]{:S(2)}) %collective-permute-start.30) | collective-permute-done | bytes 73760 | tf_op jit(solution)/shard_map/ppermute | solution.py:930
  121.4 2.0 %collective-permute-start.34 = (bf16[96,768]{1,0:T(8,128)(2,1)S(1)}, bf16[96,768]{1,0:T(8,128)(2,1)S(1)}, u32[]{:S(2)}, u32[]{:S(2)}) collective-permute-start(bf16[96,768]{1,0:T(8,128)(2,1)S(1)} %add_convert_fusion.4), channel_id=1, source_target_pairs={{0,2},{1,3},{2,0},{3,1},{4,6},{5,7},{6,4},{7,5},{8,10},{9,11},{10,... | collective-permute-start | bytes 442376 | tf_op jit(solution)/shard_map/ppermute | solution.py:930
  123.4 2.1 %collective-permute-start.37 = (bf16[48,768]{1,0:T(8,128)(2,1)S(1)}, bf16[48,768]{1,0:T(8,128)(2,1)S(1)}, u32[]{:S(2)}, u32[]{:S(2)}) collective-permute-start(bf16[48,768]{1,0:T(8,128)(2,1)S(1)} %add_convert_fusion.7.refs_0_), channel_id=1, source_target_pairs={{0,12},{4,8},{8,4},{12,0},{1,13},{5,9},{9,5},{13,1},{2,14},{6,10},... | collective-permute-start | bytes 221192 | tf_op jit(solution)/shard_map/ppermute | solution.py:930
  126.9 1.9 %collective-permute-done.37.refs_3_ = bf16[48,768]{1,0:T(8,128)(2,1)S(1)} collective-permute-done((bf16[48,768]{1,0:T(8,128)(2,1)S(1)}, bf16[48,768]{1,0:T(8,128)(2,1)S(1)}, u32[]{:S(2)}, u32[]{:S(2)}) %collective-permute-start.37) | collective-permute-done | bytes 73760 | tf_op jit(solution)/shard_map/ppermute | solution.py:930
  128.8 2.4 %collective-permute-start.38 = (bf16[96,768]{1,0:T(8,128)(2,1)S(1)}, bf16[96,768]{1,0:T(8,128)(2,1)S(1)}, u32[]{:S(2)}, u32[]{:S(2)}) collective-permute-start(bf16[96,768]{1,0:T(8,128)(2,1)S(1)} %add_convert_fusion.4), channel_id=1, source_target_pairs={{0,1},{1,0},{2,3},{3,2},{4,5},{5,4},{6,7},{7,6},{8,9},{9,8},{10,11... | collective-permute-start | bytes 442376 | tf_op jit(solution)/shard_map/ppermute | solution.py:930
  133.7 2.6 %shard_map.317 = (f32[768,512]{1,0:T(8,128)}, f32[768,512]{1,0:T(8,128)}, f32[512,768]{1,0:T(8,128)}) custom-call(bf16[2304,256]{1,0:T(8,128)(2,1)S(1)} %constant_dynamic-update-slice_fusion.refs_0_, bf16[2304,256]{1,0:T(8,128)(2,1)S(1)} %collective-permute-done.40.refs_1_), custom_call_target="tpu_custom_call" | custom-call | flops 1000000000 | bytes 3000000 | tf_op jit(solution)/shard_map/pallas_call | solution.py:86
  (144 shorter events, 45.8 us)
Async XLA Ops:
  0.7 10.9 %collective-permute-start.1 = (s32[2,512]{1,0:T(2,128)}, s32[2,512]{1,0:T(2,128)S(1)}, u32[]{:S(2)}, u32[]{:S(2)}) collective-permute-start(s32[2,512]{1,0:T(2,128)} %refs_0_.1), channel_id=1, source_target_pairs={{0,2},{1,3},{2,0},{3,1},{4,6},{5,7},{6,4},{7,5},{8,10},{9,11},{10,... | collective-permute-start | bytes 12296 | tf_op jit(solution)/shard_map/ppermute | solution.py:930
  4.8 7.2 %collective-permute-start = (s32[2,512]{1,0:T(2,128)}, s32[2,512]{1,0:T(2,128)S(1)}, u32[]{:S(2)}, u32[]{:S(2)}) collective-permute-start(s32[2,512]{1,0:T(2,128)} %refs_0_.1), channel_id=1, source_target_pairs={{0,1},{1,0},{2,3},{3,2},{4,5},{5,4},{6,7},{7,6},{8,9},{9,8},{10,11... | collective-permute-start | bytes 12296 | tf_op jit(solution)/shard_map/ppermute | solution.py:930
  8.4 17.3 %collective-permute-start.5 = (bf16[192,768]{1,0:T(8,128)(2,1)S(1)}, bf16[192,768]{1,0:T(8,128)(2,1)S(1)}, u32[]{:S(2)}, u32[]{:S(2)}) collective-permute-start(bf16[192,768]{1,0:T(8,128)(2,1)S(1)} %copy-done.14), channel_id=1, source_target_pairs={{0,12},{4,8},{8,4},{12,0},{1,13},{5,9},{9,5},{13,1},{2,14},{6,10},... | collective-permute-start | bytes 884744 | tf_op jit(solution)/shard_map/ppermute | solution.py:930
  11.1 14.6 %collective-permute-start.4 = (bf16[192,768]{1,0:T(8,128)(2,1)S(1)}, bf16[192,768]{1,0:T(8,128)(2,1)S(1)}, u32[]{:S(2)}, u32[]{:S(2)}) collective-permute-start(bf16[192,768]{1,0:T(8,128)(2,1)S(1)} %copy-done.14), channel_id=1, source_target_pairs={{0,8},{4,12},{8,0},{12,4},{1,9},{5,13},{9,1},{13,5},{2,10},{6,14},... | collective-permute-start | bytes 884744 | tf_op jit(solution)/shard_map/ppermute | solution.py:930
  11.6 14.1 %collective-permute-start.3 = (bf16[192,768]{1,0:T(8,128)(2,1)S(1)}, bf16[192,768]{1,0:T(8,128)(2,1)S(1)}, u32[]{:S(2)}, u32[]{:S(2)}) collective-permute-start(bf16[192,768]{1,0:T(8,128)(2,1)S(1)} %copy-done.14), channel_id=1, source_target_pairs={{0,4},{4,0},{8,12},{12,8},{1,5},{5,1},{9,13},{13,9},{2,6},{6,2},{1... | collective-permute-start | bytes 884744 | tf_op jit(solution)/shard_map/ppermute | solution.py:930
  25.8 7.3 %collective-permute-start.8 = (bf16[256,192]{1,0:T(8,128)(2,1)S(1)}, bf16[256,192]{1,0:T(8,128)(2,1)S(1)}, u32[]{:S(2)}, u32[]{:S(2)}) collective-permute-start(bf16[256,192]{1,0:T(8,128)(2,1)S(1)} %get-tuple-element.161.refs_0_.refs_4_), channel_id=1, source_target_pairs={{0,12},{4,8},{8,4},{12,0},{1,13},{5,9},{9,5},{13,1},{2,14},{6,10},... | collective-permute-start | bytes 294920 | tf_op jit(solution)/shard_map/ppermute | solution.py:930
  45.3 15.0 %collective-permute-start.10 = (bf16[1152,256]{1,0:T(8,128)(2,1)S(1)}, bf16[1152,256]{1,0:T(8,128)(2,1)S(1)}, u32[]{:S(2)}, u32[]{:S(2)}) collective-permute-start(bf16[1152,256]{1,0:T(8,128)(2,1)S(1)} %add_convert_fusion), channel_id=1, source_target_pairs={{0,1},{1,0},{2,3},{3,2},{4,5},{5,4},{6,7},{7,6},{8,9},{9,8},{10,11... | collective-permute-start | bytes 1769480 | tf_op jit(solution)/shard_map/ppermute | solution.py:930
  49.8 13.2 %collective-permute-start.16 = (bf16[64,768]{1,0:T(8,128)(2,1)S(1)}, bf16[64,768]{1,0:T(8,128)(2,1)S(1)}, u32[]{:S(2)}, u32[]{:S(2)}) collective-permute-start(bf16[64,768]{1,0:T(8,128)(2,1)S(1)} %get-tuple-element.183.refs_0_), channel_id=1, source_target_pairs={{0,12},{4,8},{8,4},{12,0},{1,13},{5,9},{9,5},{13,1},{2,14},{6,10},... | collective-permute-start | bytes 294920 | tf_op jit(solution)/shard_map/ppermute | solution.py:930
  51.6 11.5 %collective-permute-start.15 = (bf16[64,768]{1,0:T(8,128)(2,1)S(1)}, bf16[64,768]{1,0:T(8,128)(2,1)S(1)}, u32[]{:S(2)}, u32[]{:S(2)}) collective-permute-start(bf16[64,768]{1,0:T(8,128)(2,1)S(1)} %get-tuple-element.183.refs_0_), channel_id=1, source_target_pairs={{0,8},{4,12},{8,0},{12,4},{1,9},{5,13},{9,1},{13,5},{2,10},{6,14},... | collective-permute-start | bytes 294920 | tf_op jit(solution)/shard_map/ppermute | solution.py:930
  52.1 10.9 %collective-permute-start.14 = (bf16[64,768]{1,0:T(8,128)(2,1)S(1)}, bf16[64,768]{1,0:T(8,128)(2,1)S(1)}, u32[]{:S(2)}, u32[]{:S(2)}) collective-permute-start(bf16[64,768]{1,0:T(8,128)(2,1)S(1)} %get-tuple-element.183.refs_0_), channel_id=1, source_target_pairs={{0,4},{4,0},{8,12},{12,8},{1,5},{5,1},{9,13},{13,9},{2,6},{6,2},{1... | collective-permute-start | bytes 294920 | tf_op jit(solution)/shard_map/ppermute | solution.py:930
  60.5 15.1 %collective-permute-start.17 = (bf16[576,256]{1,0:T(8,128)(2,1)S(1)}, bf16[576,256]{1,0:T(8,128)(2,1)S(1)}, u32[]{:S(2)}, u32[]{:S(2)}) collective-permute-start(bf16[576,256]{1,0:T(8,128)(2,1)S(1)} %add_convert_fusion.3), channel_id=1, source_target_pairs={{0,2},{1,3},{2,0},{3,1},{4,6},{5,7},{6,4},{7,5},{8,10},{9,11},{10,... | collective-permute-start | bytes 884744 | tf_op jit(solution)/shard_map/ppermute | solution.py:930
  75.8 16.8 %collective-permute-start.19 = (bf16[576,256]{1,0:T(8,128)(2,1)S(1)}, bf16[576,256]{1,0:T(8,128)(2,1)S(1)}, u32[]{:S(2)}, u32[]{:S(2)}) collective-permute-start(bf16[576,256]{1,0:T(8,128)(2,1)S(1)} %add_convert_fusion.1), channel_id=1, source_target_pairs={{0,2},{1,3},{2,0},{3,1},{4,6},{5,7},{6,4},{7,5},{8,10},{9,11},{10,... | collective-permute-start | bytes 884744 | tf_op jit(solution)/shard_map/ppermute | solution.py:930
  76.6 15.7 %collective-permute-start.21 = (bf16[128,768]{1,0:T(8,128)(2,1)S(1)}, bf16[128,768]{1,0:T(8,128)(2,1)S(1)}, u32[]{:S(2)}, u32[]{:S(2)}) collective-permute-start(bf16[128,768]{1,0:T(8,128)(2,1)S(1)} %bitcast.32), channel_id=1, source_target_pairs={{0,4},{4,0},{8,12},{12,8},{1,5},{5,1},{9,13},{13,9},{2,6},{6,2},{1... | collective-permute-start | bytes 589832 | tf_op jit(solution)/shard_map/ppermute | solution.py:930
  77.8 15.8 %collective-permute-start.20 = (bf16[192,768]{1,0:T(8,128)(2,1)S(1)}, bf16[192,768]{1,0:T(8,128)(2,1)S(1)}, u32[]{:S(2)}, u32[]{:S(2)}) collective-permute-start(bf16[192,768]{1,0:T(8,128)(2,1)S(1)} %add_convert_fusion.2), channel_id=1, source_target_pairs={{0,1},{1,0},{2,3},{3,2},{4,5},{5,4},{6,7},{7,6},{8,9},{9,8},{10,11... | collective-permute-start | bytes 884744 | tf_op jit(solution)/shard_map/ppermute | solution.py:930
  100.1 9.3 %collective-permute-start.29 = (bf16[576,256]{1,0:T(8,128)(2,1)S(1)}, bf16[576,256]{1,0:T(8,128)(2,1)S(1)}, u32[]{:S(2)}, u32[]{:S(2)}) collective-permute-start(bf16[576,256]{1,0:T(8,128)(2,1)S(1)} %add_convert_fusion.1), channel_id=1, source_target_pairs={{0,1},{1,0},{2,3},{3,2},{4,5},{5,4},{6,7},{7,6},{8,9},{9,8},{10,11... | collective-permute-start | bytes 884744 | tf_op jit(solution)/shard_map/ppermute | solution.py:930
  104.7 7.2 %collective-permute-start.28 = (bf16[64,768]{1,0:T(8,128)(2,1)S(1)}, bf16[64,768]{1,0:T(8,128)(2,1)S(1)}, u32[]{:S(2)}, u32[]{:S(2)}) collective-permute-start(bf16[64,768]{1,0:T(8,128)(2,1)S(1)} %shard_map.316.refs_0_), channel_id=1, source_target_pairs={{0,4},{4,0},{8,12},{12,8},{1,5},{5,1},{9,13},{13,9},{2,6},{6,2},{1... | collective-permute-start | bytes 294920 | tf_op jit(solution)/shard_map/ppermute | solution.py:930
  105.7 10.3 %collective-permute-start.31 = (bf16[96,768]{1,0:T(8,128)(2,1)S(1)}, bf16[96,768]{1,0:T(8,128)(2,1)S(1)}, u32[]{:S(2)}, u32[]{:S(2)}) collective-permute-start(bf16[96,768]{1,0:T(8,128)(2,1)S(1)} %add_convert_fusion.5), channel_id=1, source_target_pairs={{0,2},{1,3},{2,0},{3,1},{4,6},{5,7},{6,4},{7,5},{8,10},{9,11},{10,... | collective-permute-start | bytes 442376 | tf_op jit(solution)/shard_map/ppermute | solution.py:930
  111.9 7.7 %collective-permute-start.33 = (bf16[128,768]{1,0:T(8,128)(2,1)S(1)}, bf16[128,768]{1,0:T(8,128)(2,1)S(1)}, u32[]{:S(2)}, u32[]{:S(2)}) collective-permute-start(bf16[128,768]{1,0:T(8,128)(2,1)S(1)} %pad_maximum_fusion.1), channel_id=1, source_target_pairs={{0,8},{4,12},{8,0},{12,4},{1,9},{5,13},{9,1},{13,5},{2,10},{6,14},... | collective-permute-start | bytes 589832 | tf_op jit(solution)/shard_map/ppermute | solution.py:930
  112.0 9.1 %collective-permute-start.32 = (bf16[576,256]{1,0:T(8,128)(2,1)S(1)}, bf16[576,256]{1,0:T(8,128)(2,1)S(1)}, u32[]{:S(2)}, u32[]{:S(2)}) collective-permute-start(bf16[576,256]{1,0:T(8,128)(2,1)S(1)} %collective-permute-done.19), channel_id=1, source_target_pairs={{0,1},{1,0},{2,3},{3,2},{4,5},{5,4},{6,7},{7,6},{8,9},{9,8},{10,11... | collective-permute-start | bytes 884744 | tf_op jit(solution)/shard_map/ppermute | solution.py:930
  112.1 7.5 %collective-permute-start.30 = (bf16[48,768]{1,0:T(8,128)(2,1)S(1)}, bf16[48,768]{1,0:T(8,128)(2,1)S(1)}, u32[]{:S(2)}, u32[]{:S(2)}) collective-permute-start(bf16[48,768]{1,0:T(8,128)(2,1)S(1)} %add_convert_fusion.8), channel_id=1, source_target_pairs={{0,2},{1,3},{2,0},{3,1},{4,6},{5,7},{6,4},{7,5},{8,10},{9,11},{10,... | collective-permute-start | bytes 221192 | tf_op jit(solution)/shard_map/ppermute | solution.py:930
  121.2 12.5 %collective-permute-start.40 = (bf16[2304,256]{1,0:T(8,128)(2,1)S(1)}, bf16[2304,256]{1,0:T(8,128)(2,1)S(1)}, u32[]{:S(2)}, u32[]{:S(2)}) collective-permute-start(bf16[2304,256]{1,0:T(8,128)(2,1)S(1)} %constant_dynamic-update-slice_fusion.refs_0_), channel_id=1, source_target_pairs={{0,16},{16,0},{1,17},{17,1},{2,18},{18,2},{3,19},{19,3},{4,20},{20... | collective-permute-start | bytes 3538952 | tf_op jit(solution)/shard_map/ppermute | solution.py:930
  121.4 10.4 %collective-permute-start.34 = (bf16[96,768]{1,0:T(8,128)(2,1)S(1)}, bf16[96,768]{1,0:T(8,128)(2,1)S(1)}, u32[]{:S(2)}, u32[]{:S(2)}) collective-permute-start(bf16[96,768]{1,0:T(8,128)(2,1)S(1)} %add_convert_fusion.4), channel_id=1, source_target_pairs={{0,2},{1,3},{2,0},{3,1},{4,6},{5,7},{6,4},{7,5},{8,10},{9,11},{10,... | collective-permute-start | bytes 442376 | tf_op jit(solution)/shard_map/ppermute | solution.py:930
  128.8 7.5 %collective-permute-start.38 = (bf16[96,768]{1,0:T(8,128)(2,1)S(1)}, bf16[96,768]{1,0:T(8,128)(2,1)S(1)}, u32[]{:S(2)}, u32[]{:S(2)}) collective-permute-start(bf16[96,768]{1,0:T(8,128)(2,1)S(1)} %add_convert_fusion.4), channel_id=1, source_target_pairs={{0,1},{1,0},{2,3},{3,2},{4,5},{5,4},{6,7},{7,6},{8,9},{9,8},{10,11... | collective-permute-start | bytes 442376 | tf_op jit(solution)/shard_map/ppermute | solution.py:930
  131.8 6.3 %collective-permute-start.39 = (bf16[96,768]{1,0:T(8,128)(2,1)S(1)}, bf16[96,768]{1,0:T(8,128)(2,1)S(1)}, u32[]{:S(2)}, u32[]{:S(2)}) collective-permute-start(bf16[96,768]{1,0:T(8,128)(2,1)S(1)} %collective-permute-done.34), channel_id=1, source_target_pairs={{0,1},{1,0},{2,3},{3,2},{4,5},{5,4},{6,7},{7,6},{8,9},{9,8},{10,11... | collective-permute-start | bytes 442376 | tf_op jit(solution)/shard_map/ppermute | solution.py:930
  (37 other events, 250.4 us)

commit v5 on v4

--- a/solution.py
+++ b/solution.py
@@ -1137,7 +1137,7 @@
             weights_out + grad_tokens_out,
             *first,
             *second,
-            specs=first_specs + [distant] * 6,
+            specs=first_specs + [whole] * 6,
             scratch=scratch + [pltpu.VMEM((token_rows, width), bf16)] * 3 + [whole_part],
             limit=30,
             cost=10,

time: 144 us -> 144 us (level)
  no operation moved by 1% of the time
where the time goes in v5:
time: 144 us; the launch traced here: 143 us
  Pallas kernels  51.7 us (36%)
  starting transfers between devices  50.6 us (35%)
  waiting for transfers between devices  34.4 us (24%)
  other arithmetic  4.26 us (3%)
    pallas_call x14, Pallas kernels, call(): pl.pallas_call(kernel, out_shape=out, in_specs=specs, out_specs=jax.tree....  51.7 us
    ppermute x43, starting transfers between devices, exchange(): return lax.ppermute(value, axis, [(i, i ^ mask) for i in range(size)])  50.6 us
    ppermute x43, waiting for transfers between devices, exchange(): return lax.ppermute(value, axis, [(i, i ^ mask) for i in range(size)])  34.4 us
  transfers between devices with their start and end apart: 43, of which 20 were waited for; matrix products, arithmetic and copies ran while one was open for 3% of the time, Pallas kernels for 31%

profile of v5, /device:TPU:0, one launch (start us, length us, event | category | flops | bytes accessed | tf_op | source)
XLA Modules:
  0.0 143.2 jit_solution(7988146335372182345)
XLA Ops:
  0.7 4.1 %collective-permute-start.1 = (s32[2,512]{1,0:T(2,128)}, s32[2,512]{1,0:T(2,128)S(1)}, u32[]{:S(2)}, u32[]{:S(2)}) collective-permute-start(s32[2,512]{1,0:T(2,128)} %refs_0_.1), channel_id=1, source_target_pairs={{0,2},{1,3},{2,0},{3,1},{4,6},{5,7},{6,4},{7,5},{8,10},{9,11},{10,... | collective-permute-start | bytes 12296 | tf_op jit(solution)/shard_map/ppermute | solution.py:930
  6.3 2.0 %shard_map.307 = (bf16[1280,768]{1,0:T(8,128)(2,1)S(1)}, bf16[256,128]{1,0:T(8,128)(2,1)S(1)}, f32[8,128]{1,0:T(8,128)S(1)}) custom-call(bf16[256,768]{1,0:T(8,128)(2,1)} %embedding.3, bf16[5,768]{1,0:T(8,128)(2,1)} %conv_weight.3, bf16[768]{0:T(1024)(128)(2,1)} %score_weight.3, bf16[768]{0:T(1024)(128)(2,1)} %conv_bias.3), custom_call_target="tpu_custom_call" | custom-call | flops 2000000000 | bytes 6000000 | tf_op jit(solution)/shard_map/pallas_call | solution.py:86
  8.4 2.7 %collective-permute-start.5 = (bf16[192,768]{1,0:T(8,128)(2,1)S(1)}, bf16[192,768]{1,0:T(8,128)(2,1)S(1)}, u32[]{:S(2)}, u32[]{:S(2)}) collective-permute-start(bf16[192,768]{1,0:T(8,128)(2,1)S(1)} %copy-done.22), channel_id=1, source_target_pairs={{0,12},{4,8},{8,4},{12,0},{1,13},{5,9},{9,5},{13,1},{2,14},{6,10},... | collective-permute-start | bytes 884744 | tf_op jit(solution)/shard_map/ppermute | solution.py:930
  12.0 8.2 %shard_map.308 = (bf16[1056,768]{1,0:T(8,128)(2,1)S(1)}, bf16[1056,768]{1,0:T(8,128)(2,1)}, f32[176,128]{1,0:T(8,128)}, f32[4,176,128]{2,1,0:T(8,128)}, f32[176,128]{1,0:T(8,128)}) custom-call(s32[2]{0:T(128)S(1)} %copy-done.14, s32[2,512]{1,0:T(2,128)} %refs_0_.1, s32[2,512]{1,0:T(2,128)S(1)} %collective-permute-done.refs_1_, ...), custom_call_target="tpu_custom_call" | custom-call | flops 6000000000 | bytes 18000000 | tf_op jit(solution)/shard_map/pallas_call | solution.py:86
  20.3 5.3 %shard_map.309 = (bf16[1024,768]{1,0:T(8,128)(2,1)}, bf16[256,192]{1,0:T(8,128)(2,1)}, bf16[1024,192]{1,0:T(8,128)(2,1)}, bf16[1024,192]{1,0:T(8,128)(2,1)}, bf1...) custom-call(s32[2]{0:T(128)S(1)} %copy-done.14, ...), custom_call_target="tpu_custom_call" | custom-call | flops 4000000000 | bytes 12000000 | tf_op jit(solution)/shard_map/pallas_call | solution.py:86
  25.7 2.7 %collective-permute-start.8 = (bf16[256,192]{1,0:T(8,128)(2,1)S(1)}, bf16[256,192]{1,0:T(8,128)(2,1)S(1)}, u32[]{:S(2)}, u32[]{:S(2)}) collective-permute-start(bf16[256,192]{1,0:T(8,128)(2,1)S(1)} %get-tuple-element.161.refs_0_.refs_4_), channel_id=1, source_target_pairs={{0,12},{4,8},{8,4},{12,0},{1,13},{5,9},{9,5},{13,1},{2,14},{6,10},... | collective-permute-start | bytes 294920 | tf_op jit(solution)/shard_map/ppermute | solution.py:930
  29.2 3.8 %collective-permute-done.8.refs_3_ = bf16[256,192]{1,0:T(8,128)(2,1)S(1)} collective-permute-done((bf16[256,192]{1,0:T(8,128)(2,1)S(1)}, bf16[256,192]{1,0:T(8,128)(2,1)S(1)}, u32[]{:S(2)}, u32[]{:S(2)}) %collective-permute-start.8) | collective-permute-done | bytes 98336 | tf_op jit(solution)/shard_map/ppermute | solution.py:930
  34.0 3.5 %shard_map.310 = (f32[256,768]{1,0:T(8,128)S(1)}, bf16[256,768]{1,0:T(8,128)(2,1)S(1)}, bf16[256,512]{1,0:T(8,128)(2,1)S(1)}, bf16[256,512]{1,0:T(8,128)(2,1)S(1...) custom-call(bf16[256,192]{1,0:T(8,128)(2,1)S(1)} %get-tuple-element., ...), custom_call_target="tpu_custom_call" | custom-call | flops 3000000000 | bytes 9000000 | tf_op jit(solution)/shard_map/pallas_call | solution.py:86
  37.5 2.5 %shard_map.311 = (bf16[2304,256]{1,0:T(8,128)(2,1)S(1)}, bf16[2304,256]{1,0:T(8,128)(2,1)S(1)}, bf16[256,768]{1,0:T(8,128)(2,1)}) custom-call(bf16[256,512]{1,0:T(8,128)(2,1)S(1)} %get-tuple-element.167.inner, bf16[256,768]{1,0:T(8,128)(2,1)S(1)} %get-tuple-element.168.normed, bf16[256,512]{1,0:T(8,128)(2,1)S(1)} %get-tuple-element.169.grad_gate, ...), custom_call_target="tpu_custom_call" | custom-call | flops 2000000000 | bytes 6000000 | tf_op jit(solution)/shard_map/pallas_call | solution.py:86
  55.0 5.2 %collective-permute-done.10 = bf16[1152,256]{1,0:T(8,128)(2,1)S(1)} collective-permute-done((bf16[1152,256]{1,0:T(8,128)(2,1)S(1)}, bf16[1152,256]{1,0:T(8,128)(2,1)S(1)}, u32[]{:S(2)}, u32[]{:S(2)}) %collective-permute-start.10) | collective-permute-done | bytes 589856 | tf_op jit(solution)/shard_map/ppermute | solution.py:930
  60.5 2.5 %collective-permute-start.17 = (bf16[576,256]{1,0:T(8,128)(2,1)S(1)}, bf16[576,256]{1,0:T(8,128)(2,1)S(1)}, u32[]{:S(2)}, u32[]{:S(2)}) collective-permute-start(bf16[576,256]{1,0:T(8,128)(2,1)S(1)} %add_convert_fusion.3), channel_id=1, source_target_pairs={{0,2},{1,3},{2,0},{3,1},{4,6},{5,7},{6,4},{7,5},{8,10},{9,11},{10,... | collective-permute-start | bytes 884744 | tf_op jit(solution)/shard_map/ppermute | solution.py:930
  63.1 11.3 %shard_map.313 = (bf16[384,768]{1,0:T(8,128)(2,1)S(1)}, bf16[384,768]{1,0:T(8,128)(2,1)S(1)}, f32[8,128]{1,0:T(8,128)}, f32[6,1056,128]{2,1,0:T(8,128)S(1)}, f32[8,768]{1,0:T(8,128)S(1)}) custom-call(bf16[64,768]{1,0:T(8,128)(2,1)S(1)} %get-tuple-element.183.refs_0_, bf16[64,768]{1,0:T(8,128)(2,1)S(1)} %collective-permute-done.14.refs_1_, ...), custom_call_target="tpu_custom_call" | custom-call | flops 10000000000 | bytes 30000000 | tf_op jit(solution)/shard_map/pallas_call | solution.py:86
  77.7 3.4 %collective-permute-start.20 = (bf16[192,768]{1,0:T(8,128)(2,1)S(1)}, bf16[192,768]{1,0:T(8,128)(2,1)S(1)}, u32[]{:S(2)}, u32[]{:S(2)}) collective-permute-start(bf16[192,768]{1,0:T(8,128)(2,1)S(1)} %add_convert_fusion.2), channel_id=1, source_target_pairs={{0,1},{1,0},{2,3},{3,2},{4,5},{5,4},{6,7},{7,6},{8,9},{9,8},{10,11... | collective-permute-start | bytes 884744 | tf_op jit(solution)/shard_map/ppermute | solution.py:930
  81.1 11.1 %shard_map.314 = (bf16[192,768]{1,0:T(8,128)(2,1)S(1)}, bf16[192,768]{1,0:T(8,128)(2,1)S(1)}) custom-call(f32[6,1056,128]{2,1,0:T(8,128)S(1)} %get-tuple-element.203.grad_tokens, f32[8,768]{1,0:T(8,128)S(1)} %get-tuple-element.204.grad_gain_first, f32[1,768]{1,0:T(1,128)} %get-tuple-element.205.grad_gain_second, f32[8,128]{1,0:T(8,128)} %get-tuple-element.206.rel_grad, ...), custom_call_target="tpu_custom_call" | custom-call | flops 12000000000 | bytes 36000000 | tf_op jit(solution)/shard_map/pallas_call | solution.py:86
  105.7 3.7 %collective-permute-start.31 = (bf16[96,768]{1,0:T(8,128)(2,1)S(1)}, bf16[96,768]{1,0:T(8,128)(2,1)S(1)}, u32[]{:S(2)}, u32[]{:S(2)}) collective-permute-start(bf16[96,768]{1,0:T(8,128)(2,1)S(1)} %add_convert_fusion.5), channel_id=1, source_target_pairs={{0,2},{1,3},{2,0},{3,1},{4,6},{5,7},{6,4},{7,5},{8,10},{9,11},{10,... | collective-permute-start | bytes 442376 | tf_op jit(solution)/shard_map/ppermute | solution.py:930
  109.4 2.5 %collective-permute-done.27 = bf16[48,768]{1,0:T(8,128)(2,1)S(1)} collective-permute-done((bf16[48,768]{1,0:T(8,128)(2,1)S(1)}, bf16[48,768]{1,0:T(8,128)(2,1)S(1)}, u32[]{:S(2)}, u32[]{:S(2)}) %collective-permute-start.27) | collective-permute-done | bytes 73760 | tf_op jit(solution)/shard_map/ppermute | solution.py:930
  112.0 3.7 %collective-permute-start.30 = (bf16[48,768]{1,0:T(8,128)(2,1)S(1)}, bf16[48,768]{1,0:T(8,128)(2,1)S(1)}, u32[]{:S(2)}, u32[]{:S(2)}) collective-permute-start(bf16[48,768]{1,0:T(8,128)(2,1)S(1)} %add_convert_fusion.8), channel_id=1, source_target_pairs={{0,2},{1,3},{2,0},{3,1},{4,6},{5,7},{6,4},{7,5},{8,10},{9,11},{10,... | collective-permute-start | bytes 221192 | tf_op jit(solution)/shard_map/ppermute | solution.py:930
  115.9 3.6 %collective-permute-done.30 = bf16[48,768]{1,0:T(8,128)(2,1)S(1)} collective-permute-done((bf16[48,768]{1,0:T(8,128)(2,1)S(1)}, bf16[48,768]{1,0:T(8,128)(2,1)S(1)}, u32[]{:S(2)}, u32[]{:S(2)}) %collective-permute-start.30) | collective-permute-done | bytes 73760 | tf_op jit(solution)/shard_map/ppermute | solution.py:930
  121.4 2.0 %collective-permute-start.34 = (bf16[96,768]{1,0:T(8,128)(2,1)S(1)}, bf16[96,768]{1,0:T(8,128)(2,1)S(1)}, u32[]{:S(2)}, u32[]{:S(2)}) collective-permute-start(bf16[96,768]{1,0:T(8,128)(2,1)S(1)} %add_convert_fusion.4), channel_id=1, source_target_pairs={{0,2},{1,3},{2,0},{3,1},{4,6},{5,7},{6,4},{7,5},{8,10},{9,11},{10,... | collective-permute-start | bytes 442376 | tf_op jit(solution)/shard_map/ppermute | solution.py:930
  123.3 2.0 %collective-permute-start.37 = (bf16[48,768]{1,0:T(8,128)(2,1)S(1)}, bf16[48,768]{1,0:T(8,128)(2,1)S(1)}, u32[]{:S(2)}, u32[]{:S(2)}) collective-permute-start(bf16[48,768]{1,0:T(8,128)(2,1)S(1)} %add_convert_fusion.7.refs_0_), channel_id=1, source_target_pairs={{0,12},{4,8},{8,4},{12,0},{1,13},{5,9},{9,5},{13,1},{2,14},{6,10},... | collective-permute-start | bytes 221192 | tf_op jit(solution)/shard_map/ppermute | solution.py:930
  126.9 1.9 %collective-permute-done.37.refs_3_ = bf16[48,768]{1,0:T(8,128)(2,1)S(1)} collective-permute-done((bf16[48,768]{1,0:T(8,128)(2,1)S(1)}, bf16[48,768]{1,0:T(8,128)(2,1)S(1)}, u32[]{:S(2)}, u32[]{:S(2)}) %collective-permute-start.37) | collective-permute-done | bytes 73760 | tf_op jit(solution)/shard_map/ppermute | solution.py:930
  128.8 2.4 %collective-permute-start.38 = (bf16[96,768]{1,0:T(8,128)(2,1)S(1)}, bf16[96,768]{1,0:T(8,128)(2,1)S(1)}, u32[]{:S(2)}, u32[]{:S(2)}) collective-permute-start(bf16[96,768]{1,0:T(8,128)(2,1)S(1)} %add_convert_fusion.4), channel_id=1, source_target_pairs={{0,1},{1,0},{2,3},{3,2},{4,5},{5,4},{6,7},{7,6},{8,9},{9,8},{10,11... | collective-permute-start | bytes 442376 | tf_op jit(solution)/shard_map/ppermute | solution.py:930
  133.6 2.6 %shard_map.317 = (f32[768,512]{1,0:T(8,128)}, f32[768,512]{1,0:T(8,128)}, f32[512,768]{1,0:T(8,128)}) custom-call(bf16[2304,256]{1,0:T(8,128)(2,1)S(1)} %constant_dynamic-update-slice_fusion.refs_0_, bf16[2304,256]{1,0:T(8,128)(2,1)S(1)} %collective-permute-done.40.refs_1_), custom_call_target="tpu_custom_call" | custom-call | flops 1000000000 | bytes 3000000 | tf_op jit(solution)/shard_map/pallas_call | solution.py:86
  138.8 1.8 %collective-permute-done.42.refs_4_ = bf16[192,768]{1,0:T(8,128)(2,1)S(1)} collective-permute-done((bf16[192,768]{1,0:T(8,128)(2,1)S(1)}, bf16[192,768]{1,0:T(8,128)(2,1)S(1)}, u32[]{:S(2)}, u32[]{:S(2)}) %collective-permute-start.42) | collective-permute-done | bytes 294944 | tf_op jit(solution)/shard_map/ppermute | solution.py:930
  (160 shorter events, 47.3 us)
Async XLA Ops:
  0.7 10.9 %collective-permute-start.1 = (s32[2,512]{1,0:T(2,128)}, s32[2,512]{1,0:T(2,128)S(1)}, u32[]{:S(2)}, u32[]{:S(2)}) collective-permute-start(s32[2,512]{1,0:T(2,128)} %refs_0_.1), channel_id=1, source_target_pairs={{0,2},{1,3},{2,0},{3,1},{4,6},{5,7},{6,4},{7,5},{8,10},{9,11},{10,... | collective-permute-start | bytes 12296 | tf_op jit(solution)/shard_map/ppermute | solution.py:930
  4.8 7.2 %collective-permute-start = (s32[2,512]{1,0:T(2,128)}, s32[2,512]{1,0:T(2,128)S(1)}, u32[]{:S(2)}, u32[]{:S(2)}) collective-permute-start(s32[2,512]{1,0:T(2,128)} %refs_0_.1), channel_id=1, source_target_pairs={{0,1},{1,0},{2,3},{3,2},{4,5},{5,4},{6,7},{7,6},{8,9},{9,8},{10,11... | collective-permute-start | bytes 12296 | tf_op jit(solution)/shard_map/ppermute | solution.py:930
  8.4 17.3 %collective-permute-start.5 = (bf16[192,768]{1,0:T(8,128)(2,1)S(1)}, bf16[192,768]{1,0:T(8,128)(2,1)S(1)}, u32[]{:S(2)}, u32[]{:S(2)}) collective-permute-start(bf16[192,768]{1,0:T(8,128)(2,1)S(1)} %copy-done.22), channel_id=1, source_target_pairs={{0,12},{4,8},{8,4},{12,0},{1,13},{5,9},{9,5},{13,1},{2,14},{6,10},... | collective-permute-start | bytes 884744 | tf_op jit(solution)/shard_map/ppermute | solution.py:930
  11.1 14.5 %collective-permute-start.4 = (bf16[192,768]{1,0:T(8,128)(2,1)S(1)}, bf16[192,768]{1,0:T(8,128)(2,1)S(1)}, u32[]{:S(2)}, u32[]{:S(2)}) collective-permute-start(bf16[192,768]{1,0:T(8,128)(2,1)S(1)} %copy-done.22), channel_id=1, source_target_pairs={{0,8},{4,12},{8,0},{12,4},{1,9},{5,13},{9,1},{13,5},{2,10},{6,14},... | collective-permute-start | bytes 884744 | tf_op jit(solution)/shard_map/ppermute | solution.py:930
  11.6 14.1 %collective-permute-start.3 = (bf16[192,768]{1,0:T(8,128)(2,1)S(1)}, bf16[192,768]{1,0:T(8,128)(2,1)S(1)}, u32[]{:S(2)}, u32[]{:S(2)}) collective-permute-start(bf16[192,768]{1,0:T(8,128)(2,1)S(1)} %copy-done.22), channel_id=1, source_target_pairs={{0,4},{4,0},{8,12},{12,8},{1,5},{5,1},{9,13},{13,9},{2,6},{6,2},{1... | collective-permute-start | bytes 884744 | tf_op jit(solution)/shard_map/ppermute | solution.py:930
  25.7 7.3 %collective-permute-start.8 = (bf16[256,192]{1,0:T(8,128)(2,1)S(1)}, bf16[256,192]{1,0:T(8,128)(2,1)S(1)}, u32[]{:S(2)}, u32[]{:S(2)}) collective-permute-start(bf16[256,192]{1,0:T(8,128)(2,1)S(1)} %get-tuple-element.161.refs_0_.refs_4_), channel_id=1, source_target_pairs={{0,12},{4,8},{8,4},{12,0},{1,13},{5,9},{9,5},{13,1},{2,14},{6,10},... | collective-permute-start | bytes 294920 | tf_op jit(solution)/shard_map/ppermute | solution.py:930
  42.2 6.3 %collective-permute-start.13 = (bf16[64,768]{1,0:T(8,128)(2,1)S(1)}, bf16[64,768]{1,0:T(8,128)(2,1)S(1)}, u32[]{:S(2)}, u32[]{:S(2)}) collective-permute-start(bf16[64,768]{1,0:T(8,128)(2,1)S(1)} %get-tuple-element.178), channel_id=1, source_target_pairs={{0,12},{4,8},{8,4},{12,0},{1,13},{5,9},{9,5},{13,1},{2,14},{6,10},... | collective-permute-start | bytes 294920 | tf_op jit(solution)/shard_map/ppermute | solution.py:930
  45.4 14.9 %collective-permute-start.10 = (bf16[1152,256]{1,0:T(8,128)(2,1)S(1)}, bf16[1152,256]{1,0:T(8,128)(2,1)S(1)}, u32[]{:S(2)}, u32[]{:S(2)}) collective-permute-start(bf16[1152,256]{1,0:T(8,128)(2,1)S(1)} %add_convert_fusion), channel_id=1, source_target_pairs={{0,1},{1,0},{2,3},{3,2},{4,5},{5,4},{6,7},{7,6},{8,9},{9,8},{10,11... | collective-permute-start | bytes 1769480 | tf_op jit(solution)/shard_map/ppermute | solution.py:930
  50.1 13.0 %collective-permute-start.16 = (bf16[64,768]{1,0:T(8,128)(2,1)S(1)}, bf16[64,768]{1,0:T(8,128)(2,1)S(1)}, u32[]{:S(2)}, u32[]{:S(2)}) collective-permute-start(bf16[64,768]{1,0:T(8,128)(2,1)S(1)} %get-tuple-element.183.refs_0_), channel_id=1, source_target_pairs={{0,12},{4,8},{8,4},{12,0},{1,13},{5,9},{9,5},{13,1},{2,14},{6,10},... | collective-permute-start | bytes 294920 | tf_op jit(solution)/shard_map/ppermute | solution.py:930
  51.8 11.2 %collective-permute-start.15 = (bf16[64,768]{1,0:T(8,128)(2,1)S(1)}, bf16[64,768]{1,0:T(8,128)(2,1)S(1)}, u32[]{:S(2)}, u32[]{:S(2)}) collective-permute-start(bf16[64,768]{1,0:T(8,128)(2,1)S(1)} %get-tuple-element.183.refs_0_), channel_id=1, source_target_pairs={{0,8},{4,12},{8,0},{12,4},{1,9},{5,13},{9,1},{13,5},{2,10},{6,14},... | collective-permute-start | bytes 294920 | tf_op jit(solution)/shard_map/ppermute | solution.py:930
  52.4 10.7 %collective-permute-start.14 = (bf16[64,768]{1,0:T(8,128)(2,1)S(1)}, bf16[64,768]{1,0:T(8,128)(2,1)S(1)}, u32[]{:S(2)}, u32[]{:S(2)}) collective-permute-start(bf16[64,768]{1,0:T(8,128)(2,1)S(1)} %get-tuple-element.183.refs_0_), channel_id=1, source_target_pairs={{0,4},{4,0},{8,12},{12,8},{1,5},{5,1},{9,13},{13,9},{2,6},{6,2},{1... | collective-permute-start | bytes 294920 | tf_op jit(solution)/shard_map/ppermute | solution.py:930
  60.5 15.0 %collective-permute-start.17 = (bf16[576,256]{1,0:T(8,128)(2,1)S(1)}, bf16[576,256]{1,0:T(8,128)(2,1)S(1)}, u32[]{:S(2)}, u32[]{:S(2)}) collective-permute-start(bf16[576,256]{1,0:T(8,128)(2,1)S(1)} %add_convert_fusion.3), channel_id=1, source_target_pairs={{0,2},{1,3},{2,0},{3,1},{4,6},{5,7},{6,4},{7,5},{8,10},{9,11},{10,... | collective-permute-start | bytes 884744 | tf_op jit(solution)/shard_map/ppermute | solution.py:930
  75.7 16.8 %collective-permute-start.19 = (bf16[576,256]{1,0:T(8,128)(2,1)S(1)}, bf16[576,256]{1,0:T(8,128)(2,1)S(1)}, u32[]{:S(2)}, u32[]{:S(2)}) collective-permute-start(bf16[576,256]{1,0:T(8,128)(2,1)S(1)} %add_convert_fusion.1), channel_id=1, source_target_pairs={{0,2},{1,3},{2,0},{3,1},{4,6},{5,7},{6,4},{7,5},{8,10},{9,11},{10,... | collective-permute-start | bytes 884744 | tf_op jit(solution)/shard_map/ppermute | solution.py:930
  76.6 15.7 %collective-permute-start.21 = (bf16[128,768]{1,0:T(8,128)(2,1)S(1)}, bf16[128,768]{1,0:T(8,128)(2,1)S(1)}, u32[]{:S(2)}, u32[]{:S(2)}) collective-permute-start(bf16[128,768]{1,0:T(8,128)(2,1)S(1)} %bitcast.32), channel_id=1, source_target_pairs={{0,4},{4,0},{8,12},{12,8},{1,5},{5,1},{9,13},{13,9},{2,6},{6,2},{1... | collective-permute-start | bytes 589832 | tf_op jit(solution)/shard_map/ppermute | solution.py:930
  77.7 15.9 %collective-permute-start.20 = (bf16[192,768]{1,0:T(8,128)(2,1)S(1)}, bf16[192,768]{1,0:T(8,128)(2,1)S(1)}, u32[]{:S(2)}, u32[]{:S(2)}) collective-permute-start(bf16[192,768]{1,0:T(8,128)(2,1)S(1)} %add_convert_fusion.2), channel_id=1, source_target_pairs={{0,1},{1,0},{2,3},{3,2},{4,5},{5,4},{6,7},{7,6},{8,9},{9,8},{10,11... | collective-permute-start | bytes 884744 | tf_op jit(solution)/shard_map/ppermute | solution.py:930
  100.1 9.2 %collective-permute-start.29 = (bf16[576,256]{1,0:T(8,128)(2,1)S(1)}, bf16[576,256]{1,0:T(8,128)(2,1)S(1)}, u32[]{:S(2)}, u32[]{:S(2)}) collective-permute-start(bf16[576,256]{1,0:T(8,128)(2,1)S(1)} %add_convert_fusion.1), channel_id=1, source_target_pairs={{0,1},{1,0},{2,3},{3,2},{4,5},{5,4},{6,7},{7,6},{8,9},{9,8},{10,11... | collective-permute-start | bytes 884744 | tf_op jit(solution)/shard_map/ppermute | solution.py:930
  104.7 7.1 %collective-permute-start.28 = (bf16[64,768]{1,0:T(8,128)(2,1)S(1)}, bf16[64,768]{1,0:T(8,128)(2,1)S(1)}, u32[]{:S(2)}, u32[]{:S(2)}) collective-permute-start(bf16[64,768]{1,0:T(8,128)(2,1)S(1)} %shard_map.316.refs_0_), channel_id=1, source_target_pairs={{0,4},{4,0},{8,12},{12,8},{1,5},{5,1},{9,13},{13,9},{2,6},{6,2},{1... | collective-permute-start | bytes 294920 | tf_op jit(solution)/shard_map/ppermute | solution.py:930
  105.7 10.3 %collective-permute-start.31 = (bf16[96,768]{1,0:T(8,128)(2,1)S(1)}, bf16[96,768]{1,0:T(8,128)(2,1)S(1)}, u32[]{:S(2)}, u32[]{:S(2)}) collective-permute-start(bf16[96,768]{1,0:T(8,128)(2,1)S(1)} %add_convert_fusion.5), channel_id=1, source_target_pairs={{0,2},{1,3},{2,0},{3,1},{4,6},{5,7},{6,4},{7,5},{8,10},{9,11},{10,... | collective-permute-start | bytes 442376 | tf_op jit(solution)/shard_map/ppermute | solution.py:930
  111.9 7.7 %collective-permute-start.33 = (bf16[128,768]{1,0:T(8,128)(2,1)S(1)}, bf16[128,768]{1,0:T(8,128)(2,1)S(1)}, u32[]{:S(2)}, u32[]{:S(2)}) collective-permute-start(bf16[128,768]{1,0:T(8,128)(2,1)S(1)} %pad_maximum_fusion.1), channel_id=1, source_target_pairs={{0,8},{4,12},{8,0},{12,4},{1,9},{5,13},{9,1},{13,5},{2,10},{6,14},... | collective-permute-start | bytes 589832 | tf_op jit(solution)/shard_map/ppermute | solution.py:930
  111.9 9.1 %collective-permute-start.32 = (bf16[576,256]{1,0:T(8,128)(2,1)S(1)}, bf16[576,256]{1,0:T(8,128)(2,1)S(1)}, u32[]{:S(2)}, u32[]{:S(2)}) collective-permute-start(bf16[576,256]{1,0:T(8,128)(2,1)S(1)} %collective-permute-done.19), channel_id=1, source_target_pairs={{0,1},{1,0},{2,3},{3,2},{4,5},{5,4},{6,7},{7,6},{8,9},{9,8},{10,11... | collective-permute-start | bytes 884744 | tf_op jit(solution)/shard_map/ppermute | solution.py:930
  112.0 7.5 %collective-permute-start.30 = (bf16[48,768]{1,0:T(8,128)(2,1)S(1)}, bf16[48,768]{1,0:T(8,128)(2,1)S(1)}, u32[]{:S(2)}, u32[]{:S(2)}) collective-permute-start(bf16[48,768]{1,0:T(8,128)(2,1)S(1)} %add_convert_fusion.8), channel_id=1, source_target_pairs={{0,2},{1,3},{2,0},{3,1},{4,6},{5,7},{6,4},{7,5},{8,10},{9,11},{10,... | collective-permute-start | bytes 221192 | tf_op jit(solution)/shard_map/ppermute | solution.py:930
  121.2 12.4 %collective-permute-start.40 = (bf16[2304,256]{1,0:T(8,128)(2,1)S(1)}, bf16[2304,256]{1,0:T(8,128)(2,1)S(1)}, u32[]{:S(2)}, u32[]{:S(2)}) collective-permute-start(bf16[2304,256]{1,0:T(8,128)(2,1)S(1)} %constant_dynamic-update-slice_fusion.refs_0_), channel_id=1, source_target_pairs={{0,16},{16,0},{1,17},{17,1},{2,18},{18,2},{3,19},{19,3},{4,20},{20... | collective-permute-start | bytes 3538952 | tf_op jit(solution)/shard_map/ppermute | solution.py:930
  121.4 10.4 %collective-permute-start.34 = (bf16[96,768]{1,0:T(8,128)(2,1)S(1)}, bf16[96,768]{1,0:T(8,128)(2,1)S(1)}, u32[]{:S(2)}, u32[]{:S(2)}) collective-permute-start(bf16[96,768]{1,0:T(8,128)(2,1)S(1)} %add_convert_fusion.4), channel_id=1, source_target_pairs={{0,2},{1,3},{2,0},{3,1},{4,6},{5,7},{6,4},{7,5},{8,10},{9,11},{10,... | collective-permute-start | bytes 442376 | tf_op jit(solution)/shard_map/ppermute | solution.py:930
  128.8 7.5 %collective-permute-start.38 = (bf16[96,768]{1,0:T(8,128)(2,1)S(1)}, bf16[96,768]{1,0:T(8,128)(2,1)S(1)}, u32[]{:S(2)}, u32[]{:S(2)}) collective-permute-start(bf16[96,768]{1,0:T(8,128)(2,1)S(1)} %add_convert_fusion.4), channel_id=1, source_target_pairs={{0,1},{1,0},{2,3},{3,2},{4,5},{5,4},{6,7},{7,6},{8,9},{9,8},{10,11... | collective-permute-start | bytes 442376 | tf_op jit(solution)/shard_map/ppermute | solution.py:930
  (45 other events, 297.1 us)
